TPU v7x, 256 devices: a whole 4x4x8 slice. The times are simulated.
256 devices in a mesh: grp: 4 (over y), sub: 64 (over z, x, core).
Axes of the slice: x: 4, y: 4, z: 8, core: 2. Of those that a mesh axis runs over, the one named last changes fastest.
Arguments:
- model: float32 [2048, 64, 128], P('grp', 'sub'), may hold values from -4 to 4
- block_owner_rank: int32 [4, 32768, 8], P('grp', 'sub'), may hold values from 0 to 63, all different within a row; in each aligned block of 512 rows (0 to 511, 512 to 1023, ..., all dimensions but the last counted through in order) at most 128 rows name the same one
- source_slot: int32 [4, 32768, 8], P('grp', 'sub'), may hold values from 0 to 2047
- weights: float32 [4, 32768, 8], P('grp', 'sub'), may hold values from 0.05 to 0.3
- field: float32 [4, 2, 3, 512, 64, 128], P('grp', None, None, 'sub'), may hold values from -2 to 2
- source: float32 [4, 2, 3, 512, 64, 128], P('grp', None, None, 'sub'), may hold values from -6 to 6
- freq: float32 [4], P('grp'), may hold values from 0.5 to 4
Outputs:
- residual: float32 [4, 2, 3, 512, 64, 128], P('grp', None, None, 'sub')
Inputs may be any that keep to these rules, and one draw needn't show every extreme that they name: `block_owner_rank`: each row names 8 different owners; among the rows of one subdomain's 512 columns (aligned blocks), no owner is named more than 128 times, a bound that some block reaches.
All inputs are finite; a program needn't handle non-finite values.
Results may differ from a plain program's by a relative error of at most 0.0003.
Values sent between devices are 32-bit elements; how exact they have to be, the bound alone decides.
No kernel may reach another device: no remote copies, remote signals or barrier semaphores. Data moves between devices by JAX's collectives and lax.ppermute only.
A program may use at most 192 MiB of HBM per device.

v0:
```python
import math

import jax
import jax.numpy as jnp
from jax import lax
from jax.sharding import PartitionSpec as P

highest_precision = lax.Precision.HIGHEST


def shifted(shard, axis, by):
    devices = lax.axis_size(axis)
    pairs = [(i, i + by) for i in range(devices) if 0 <= i + by < devices]
    return lax.ppermute(shard, axis, pairs)


def padded_2(shard, sides, width):
    for axis, dim in sides:
        devices, length = (lax.axis_size(axis), shard.shape[dim])
        up = [(i, (i + 1) % devices) for i in range(devices - 1)]
        down = [(j, i) for i, j in up]
        last = lax.slice_in_dim(shard, length - width, length, axis=dim)
        initial = lax.slice_in_dim(shard, 0, width, axis=dim)
        before = lax.ppermute(last, axis, up)
        after = lax.ppermute(initial, axis, down)
        shard = jnp.concatenate([before, shard, after], axis=dim)
    return shard


def ahead(values, along):
    count = values.shape[along]
    tail = jnp.zeros_like(lax.slice_in_dim(values, 0, 1, axis=along))
    return jnp.concatenate([lax.slice_in_dim(values, 1, count, axis=along), tail], along)


def behind(values, along):
    count = values.shape[along]
    head = jnp.zeros_like(lax.slice_in_dim(values, 0, 1, axis=along))
    return jnp.concatenate([head, lax.slice_in_dim(values, 0, count - 1, axis=along)], along)


def lower_mean(values, along):
    count = values.shape[along]
    moved = jnp.concatenate(
        [
            lax.slice_in_dim(values, 0, 1, axis=along),
            lax.slice_in_dim(values, 0, count - 1, axis=along),
        ],
        along,
    )
    return 0.5 * (values + moved)


def forward_diff(values, along):
    return ahead(values, along) - values


def backward_diff(values, along):
    return values - behind(values, along)


def owner_ranks(owner_marks):
    total = owner_marks.shape[0]
    width = math.gcd(total, 128)
    blocks = owner_marks.reshape(total // width, width, -1)
    inner = jnp.arange(width, dtype=jnp.int32)
    lower = (inner[:, None] >= inner[None, :]).astype(jnp.bfloat16)
    within = jnp.einsum("ij,bjo->bio", lower, blocks, preferred_element_type=jnp.float32)
    totals = within[:, -1, :]
    offsets = jnp.cumsum(totals, axis=0) - totals
    running = (within + offsets[:, None, :]).reshape(total, -1) - 1.0
    marks_float = owner_marks.astype(jnp.float32)
    return jnp.sum(marks_float * running, axis=1).astype(jnp.int32)


def build_table(owner_marks, rank_hot, slots_flat):
    high_part = (slots_flat // 256).astype(jnp.bfloat16)
    low_part = (slots_flat % 256).astype(jnp.bfloat16)
    table_high = jnp.einsum(
        "eo,er->or", owner_marks * high_part[:, None], rank_hot, preferred_element_type=jnp.float32
    )
    table_low = jnp.einsum(
        "eo,er->or", owner_marks * low_part[:, None], rank_hot, preferred_element_type=jnp.float32
    )
    return (table_high * 256.0 + table_low).astype(jnp.int32)


def per_device(model, block_owner_rank, source_slot, weights, field, source, freq):
    local_model_block = lax.all_gather(model, "grp", axis=0, tiled=True)
    owners_flat = block_owner_rank.reshape(-1)
    slots_flat = source_slot.reshape(-1)
    count_owners = lax.axis_size("sub")
    columns = weights.shape[1]
    per_column = weights.shape[2]
    slot_count = local_model_block.shape[0]
    capacity = min(max(2, 2 * columns * per_column // count_owners), columns)
    owner_marks = (
        owners_flat[:, None] == jnp.arange(count_owners, dtype=jnp.int32)[None, :]
    ).astype(jnp.bfloat16)
    slot_rank = owner_ranks(owner_marks)
    rank_hot = (slot_rank[:, None] == jnp.arange(capacity, dtype=jnp.int32)[None, :]).astype(
        jnp.bfloat16
    )
    request_table = build_table(owner_marks, rank_hot, slots_flat)
    slot_iota = jnp.arange(slot_count, dtype=jnp.int32)
    asked_slots = lax.all_to_all(request_table, "sub", split_axis=0, concat_axis=0, tiled=True)
    request_onehot = (asked_slots[:, :, None] == slot_iota[None, None, :]).astype(jnp.float32)
    reply_row_buffer = jnp.einsum(
        "glm,ma->gla", request_onehot, local_model_block[:, 0, :], precision=highest_precision
    )
    returned = lax.all_to_all(reply_row_buffer, "sub", split_axis=0, concat_axis=0, tiled=True)
    efield = field[0]
    x_cell_count = efield.shape[2]
    cells_y = efield.shape[3]
    coefs = weights[0]
    owner_cols = (
        owner_marks.astype(jnp.float32).reshape(columns, per_column, count_owners)
        * coefs[:, :, None]
    )
    rank_cols = rank_hot.astype(jnp.float32).reshape(columns, per_column, capacity)
    mixing = jnp.einsum("cko,ckr->cor", owner_cols, rank_cols, precision=highest_precision)
    log_cond = jnp.einsum("cor,orz->cz", mixing, returned, precision=highest_precision).reshape(
        x_cell_count, cells_y, -1
    )
    conduct = jnp.exp(log_cond)
    first_device = lax.axis_index("sub") == 0
    prior_plane = shifted(conduct[-1:], "sub", 1)
    prior_plane = jnp.where(first_device, conduct[:1], prior_plane)
    extended = jnp.concatenate([prior_plane, conduct], 0)
    sig_x = lower_mean(lower_mean(conduct, 1), 2)
    z_means = lower_mean(extended, 2)
    sig_y = 0.5 * (z_means[1:] + z_means[:-1])
    y_means = lower_mean(extended, 1)
    sig_z = 0.5 * (y_means[1:] + y_means[:-1])
    sigma_edges = jnp.stack([sig_x, sig_y, sig_z], 0)
    padded = padded_2(efield, (("sub", 2),), 1)
    field_x, field_y, field_z = (padded[:, 0], padded[:, 1], padded[:, 2])
    lower_x, lower_y, lower_z = (field_x[:, :-1], field_y[:, :-1], field_z[:, :-1])
    hx_part = forward_diff(lower_z, 2) - forward_diff(lower_y, 3)
    hy_part = forward_diff(lower_x, 3) - (field_z[:, 1:] - field_z[:, :-1])
    hz_part = field_y[:, 1:] - field_y[:, :-1] - forward_diff(lower_x, 2)
    rim_scale = jnp.where(first_device, 0.0, 1.0).astype(jnp.float32)
    plane_scale = jnp.concatenate(
        [rim_scale[None], jnp.ones((x_cell_count,), jnp.float32)]
    ).reshape(1, x_cell_count + 1, 1, 1)
    hx_part = hx_part * plane_scale
    hy_part = hy_part * plane_scale
    hz_part = hz_part * plane_scale
    curl_x = backward_diff(hz_part[:, 1:], 2) - backward_diff(hy_part[:, 1:], 3)
    curl_y = backward_diff(hx_part[:, 1:], 3) - (hz_part[:, 1:] - hz_part[:, :-1])
    curl_z = hy_part[:, 1:] - hy_part[:, :-1] - backward_diff(hx_part[:, 1:], 2)
    curl = jnp.stack([curl_x, curl_y, curl_z], 1)
    omega = freq[0]
    real_part = curl[0] - omega * sigma_edges * efield[1] - source[0, 0]
    imaginary_component = curl[1] + omega * sigma_edges * efield[0] - source[0, 1]
    return jnp.stack([real_part, imaginary_component], 0)[None]


def solution(mesh):
    in_specs = (
        P("grp", "sub", None),
        P("grp", "sub", None),
        P("grp", "sub", None),
        P("grp", "sub", None),
        P("grp", None, None, "sub", None, None),
        P("grp", None, None, "sub", None, None),
        P("grp"),
    )
    out_specs = P("grp", None, None, "sub", None, None)
    return jax.shard_map(
        per_device, mesh=mesh, in_specs=in_specs, out_specs=out_specs, check_vma=False
    )
```

profile of v0, /device:TPU:56, one launch (start us, length us, event | category | flops | bytes accessed | tf_op | source)
XLA Modules:
  0.0 216.4 jit_solution(14857390888116052415)
XLA Ops:
  6.5 0.7 all-gather.2.cloned.1.call-update
  7.3 0.8 copy.101
  8.1 0.1 eq.79
  8.3 0.3 convolution_bitcast_fusion
  8.6 0.1 eq.86
  8.7 0.0 copy-start.3
  8.7 0.3 slice.223
  9.1 0.4 copy.102
  9.5 0.4 copy.103
  9.9 0.0 copy-done.3
  9.9 0.1 copy.105
  10.0 0.2 reshape.328
  10.2 0.7 subtract_reduce_fusion
  10.9 0.4 multiply_reduce_fusion
  11.3 2.1 fusion.18
  13.4 2.1 fusion.20
  15.6 20.0 %all_to_all.14 = s32[64,1,128]{2,1,0:T(1,128)S(1)} all-to-all(s32[64,1,128]{2,1,0:T(1,128)S(1)} %bitcast.102), channel_id=1, replica_groups=mesh['grp'=4,'sub'=64] {'sub'}, dimensions={0} | all-to-all | bytes 65536 | tf_op jit(solution)/shard_map/all_to_all | solution.py:106
  35.6 1.5 all-gather.2.cloned.1.call-done
  37.1 32.3 %fusion = f32[64,128,128]{2,1,0:T(8,128)} fusion(s32[64,128]{1,0:T(8,128)S(1)} %bitcast.101, f32[2048,1,128]{2,0,1:T(8,128)} %all-gather.2.cloned.1.call-done), kind=kOutput, calls=%fused_computation.1 | convolution fusion | flops 25786580992 | bytes 5275648 | tf_op jit(solution)/shard_map/glm,ma->gla/dot_general | solution.py:108
  69.4 10.4 %all-to-all-start.1 = ((f32[64,128,128]{2,1,0:T(8,128)}), f32[64,128,128]{2,1,0:T(8,128)}, u32[]{:S(2)}, u32[]{:S(2)}) async-start(f32[64,128,128]{2,1,0:T(8,128)} %fusion), calls=%async_computation.1 | async-start | bytes 8388608 | tf_op jit(solution)/shard_map/all_to_all | solution.py:111
  79.9 2.1 collective-permute-start
  81.9 5.8 %collective-permute-start.1 = (f32[2,3,1,64,128]{4,3,2,1,0:T(8,128)S(1)}, f32[2,3,1,64,128]{4,3,2,1,0:T(8,128)S(1)}, u32[]{:S(2)}, u32[]{:S(2)}) collective-permute-start(f32[2,3,1,64,128]{4,3,2,1,0:T(8,128)S(1)} %get-tuple-element.11), channel_id=1, source_target_pairs={{1,0},{2,1},{3,2},{4,3},{5,4},{6,5},{7,6},{8,7},{9,8},{10,9},{11,1... | collective-permute-start | bytes 589832 | tf_op jit(solution)/shard_map/ppermute | solution.py:25
  87.8 0.2 convert_element_type.55
  87.9 0.1 copy.100
  88.1 0.0 copy-done.2
  88.1 0.1 copy.99
  88.2 17.8 %fusion.8 = f32[512,64,128]{2,1,0:T(8,128)} fusion(s32[512,8]{1,0:T(8,128)S(1)} %convert_element_type.55, f32[512,8]{1,0:T(8,128)S(1)} %copy.100, s32[512,8]{1,0:T(8,128)S(1)} %copy.99), kind=kOutput, calls=%fused_computation.12 | convolution fusion | flops 404226048 | bytes 16826368 | tf_op jit(solution)/shard_map/cko,ckr->cor/dot_general | solution.py:121
  106.7 68.0 %collective-permute-done = f32[2,3,1,64,128]{4,3,2,1,0:T(8,128)S(1)} collective-permute-done((f32[2,3,1,64,128]{4,3,2,1,0:T(8,128)S(1)}, f32[2,3,1,64,128]{4,3,2,1,0:T(8,128)S(1)}, u32[]{:S(2)}, u32[]{:S(2)}) %collective-permute-start) | collective-permute-done | bytes 196640 | tf_op jit(solution)/shard_map/ppermute | solution.py:24
  174.7 0.0 collective-permute-done.1
  174.7 0.1 pad_maximum_fusion
  174.8 0.1 slice_bitcast_fusion.2
  174.9 0.1 slice.205
  175.0 0.2 slice.209
  175.2 0.1 slice.215
  175.3 0.2 slice.216
  175.5 0.7 fusion.38
  176.4 0.6 subtract_bitcast_fusion
  176.9 0.2 pad_maximum_fusion.1
  177.1 0.0 all-to-all-done.1
  177.1 21.6 %fusion.15 = f32[512,128]{1,0:T(8,128)S(1)} fusion(f32[64,128,128]{2,1,0:T(8,128)} %all-to-all-done.1, f32[512,64,128]{2,1,0:T(8,128)} %fusion.8), kind=kOutput, calls=%fused_computation.22 | convolution fusion | flops 6442450944 | bytes 21233664 | tf_op jit(solution)/shard_map/cor,orz->cz/dot_general | solution.py:122
  198.9 1.9 collective-permute-start.2
  200.8 0.1 fusion.60
  200.9 5.3 %collective-permute-done.2 = f32[1,64,128]{2,1,0:T(8,128)S(1)} collective-permute-done((f32[1,64,128]{2,1,0:T(8,128)S(1)}, f32[1,64,128]{2,1,0:T(8,128)S(1)}, u32[]{:S(2)}, u32[]{:S(2)}) %collective-permute-start.2) | collective-permute-done | bytes 32800 | tf_op jit(solution)/shard_map/ppermute | solution.py:14
  206.3 0.0 copy-start.1
  206.3 0.2 fusion.51
  206.5 1.2 copy-done.1
  207.7 0.6 fusion.34
  208.3 1.2 maximum_bitcast_fusion
  (27 shorter events, 0.5 us)
Async XLA Ops:
  6.5 30.6 %all-gather.2.cloned.1.call-start = ((), (), s32[]{:S(2)}) async-start(), calls=%async_computation.2 | async-start | bytes 1310720 | tf_op jit(solution)/shard_map/all_gather | solution.py:89
  8.7 1.2 copy-start.3
  69.4 10.5 %copy-start = (f32[1,2,3,8,64,128]{5,4,3,2,1,0:T(8,128)S(1)}, f32[1,2,3,8,64,128]{5,4,3,2,1,0:T(8,128)}, u32[]{:S(2)}) copy-start(f32[1,2,3,8,64,128]{5,4,3,2,1,0:T(8,128)} %param.11) | copy-start | bytes 4718596
  69.4 18.6 %copy-start.4 = (f32[1,512,8]{1,2,0:T(8,128)S(1)}, f32[1,512,8]{1,2,0:T(8,128)}, u32[]{:S(2)}) copy-start(f32[1,512,8]{1,2,0:T(8,128)} %param.10) | copy-start | bytes 49156
  69.4 18.7 %copy-start.2 = (s32[1,512,8]{1,2,0:T(8,128)S(1)}, s32[1,512,8]{1,2,0:T(8,128)}, u32[]{:S(2)}) copy-start(s32[1,512,8]{1,2,0:T(8,128)} %param.8) | copy-start | bytes 49156
  69.4 107.7 %all-to-all-start.1 = ((f32[64,128,128]{2,1,0:T(8,128)}), f32[64,128,128]{2,1,0:T(8,128)}, u32[]{:S(2)}, u32[]{:S(2)}) async-start(f32[64,128,128]{2,1,0:T(8,128)} %fusion), calls=%async_computation.1 | async-start | bytes 8388608 | tf_op jit(solution)/shard_map/all_to_all | solution.py:111
  79.9 94.8 %collective-permute-start = (f32[2,3,1,64,128]{4,3,2,1,0:T(8,128)S(1)}, f32[2,3,1,64,128]{4,3,2,1,0:T(8,128)S(1)}, u32[]{:S(2)}, u32[]{:S(2)}) collective-permute-start(f32[2,3,1,64,128]{4,3,2,1,0:T(8,128)S(1)} %get-tuple-element.10), channel_id=1, source_target_pairs={{0,1},{1,2},{2,3},{3,4},{4,5},{5,6},{6,7},{7,8},{8,9},{9,10},{10,1... | collective-permute-start | bytes 589832 | tf_op jit(solution)/shard_map/ppermute | solution.py:24
  81.9 92.7 %collective-permute-start.1 = (f32[2,3,1,64,128]{4,3,2,1,0:T(8,128)S(1)}, f32[2,3,1,64,128]{4,3,2,1,0:T(8,128)S(1)}, u32[]{:S(2)}, u32[]{:S(2)}) collective-permute-start(f32[2,3,1,64,128]{4,3,2,1,0:T(8,128)S(1)} %get-tuple-element.11), channel_id=1, source_target_pairs={{1,0},{2,1},{3,2},{4,3},{5,4},{6,5},{7,6},{8,7},{9,8},{10,9},{11,1... | collective-permute-start | bytes 589832 | tf_op jit(solution)/shard_map/ppermute | solution.py:25
  198.9 7.3 %collective-permute-start.2 = (f32[1,64,128]{2,1,0:T(8,128)S(1)}, f32[1,64,128]{2,1,0:T(8,128)S(1)}, u32[]{:S(2)}, u32[]{:S(2)}) collective-permute-start(f32[1,64,128]{2,1,0:T(8,128)S(1)} %slice_bitcast_fusion.5), channel_id=1, source_target_pairs={{0,1},{1,2},{2,3},{3,4},{4,5},{5,6},{6,7},{7,8},{8,9},{9,10},{10,1... | collective-permute-start | bytes 98312 | tf_op jit(solution)/shard_map/ppermute | solution.py:14
  206.3 1.4 copy-start.1
Sparse Core Ops, SparseCore 0:
  9.2 27.8 all-gather.1
where the time goes:
time: 219 us; the launch traced here: 216 us
  matrix products  76.2 us (35%)
  waiting for transfers between devices  75.5 us (34%)
  starting transfers between devices  20.3 us (9%)
  blocking collectives  20 us (9%)
  between operations  14.4 us (7%)
  local copies, waits for them, and re-layouts  5.07 us (2%)
  other arithmetic  4.96 us (2%)
    ppermute x1, waiting for transfers between devices, padded_2(): before = lax.ppermute(last, axis, up)  68 us
    dot_general x1, matrix products, per_device(): jnp.einsum('glm,ma->gla', request_onehot, local_model_block[:, 0, :], pre...  32.3 us
    dot_general x1, matrix products, per_device(): jnp.einsum('cor,orz->cz', mixing, returned, precision=highest_precision)  21.6 us
    all_to_all x1, blocking collectives, per_device(): lax.all_to_all(request_table, 'sub', split_axis=0, concat_axis=0, tiled=T...  20 us
    dot_general x1, matrix products, per_device(): jnp.einsum('cko,ckr->cor', owner_cols, rank_cols, precision=highest_preci...  17.8 us
    all_to_all x1, starting transfers between devices, per_device(): lax.all_to_all(reply_row_buffer, 'sub', split_axis=0, concat_axis=0, tile...  10.4 us
    ppermute x1, starting transfers between devices, padded_2(): after = lax.ppermute(initial, axis, down)  5.84 us
    ppermute x1, waiting for transfers between devices, shifted(): return lax.ppermute(shard, axis, pairs)  5.27 us
  transfers between devices with their start and end apart: 5, of which 3 were waited for; matrix products, arithmetic and copies ran while one was open for 13% of the time, Pallas kernels for 0%

commit v1 on v0

v1 whole, which is shorter than its diff:
```python
import functools

import jax
import jax.numpy as jnp
from jax import lax
from jax.experimental import pallas as pl
from jax.experimental.pallas import tpu as pltpu
from jax.sharding import Mesh, PartitionSpec as P

CHUNK = 256
FIELDS = 3


def shift_of(count):
    return (count - 1).bit_length()


def lists_kernel(sizes, owner_ref, slot_ref, weight_ref, out_ref, values):
    nz, nx, nc, quarter, classes, cap = sizes
    top, columns = owner_ref.shape
    owner, slot, weight = owner_ref[...], slot_ref[...], weight_ref[...]
    bits_c, bits_x, bits_q = shift_of(nc), shift_of(nx), shift_of(quarter)
    kind = (slot >> bits_q) * nx + ((owner >> bits_c) & (nx - 1))
    row = ((owner >> (bits_c + bits_x)) * nc + (owner & (nc - 1))) * quarter + (slot & (quarter - 1))
    column = lax.broadcasted_iota(jnp.int32, (top, columns), 1)
    as_float = lambda value: value.astype(jnp.float32)
    rounded = lambda value: value.astype(jnp.bfloat16).astype(jnp.float32)
    high = rounded(weight)
    middle = rounded(weight - high)
    parts = [
        as_float(row >> 7),
        as_float(row & 127),
        as_float(column >> 8),
        as_float(column & 255),
        high,
        middle,
        weight - high - middle,
        jnp.ones((top, columns), jnp.float32),
    ]
    iota_kind = lax.broadcasted_iota(jnp.int32, (classes, columns), 0)
    marks = []
    for k in range(top):
        mark = iota_kind == kind[k : k + 1, :]
        marks.append(jnp.where(mark, 1.0, 0.0))
        stacked = [jnp.where(mark, part[k : k + 1, :], 0.0) for part in parts]
        values[k] = jnp.concatenate(stacked, 0).astype(jnp.bfloat16)
    marks = jnp.concatenate(marks, 0)
    marks_low = marks.astype(jnp.bfloat16)
    rows = top * classes
    before = lax.broadcasted_iota(jnp.int32, (columns, columns), 0) < lax.broadcasted_iota(
        jnp.int32, (columns, columns), 1
    )
    prefix = jnp.dot(
        marks_low,
        jnp.where(before, 1.0, 0.0).astype(jnp.bfloat16),
        preferred_element_type=jnp.float32,
    )
    row_i = lax.broadcasted_iota(jnp.int32, (rows, rows), 0)
    row_j = lax.broadcasted_iota(jnp.int32, (rows, rows), 1)
    earlier = (row_j < row_i) & ((row_i & (classes - 1)) == (row_j & (classes - 1)))
    above = jnp.dot(
        jnp.where(earlier, 1.0, 0.0).astype(jnp.bfloat16),
        marks_low,
        preferred_element_type=jnp.float32,
    )
    offset = jnp.sum(above, axis=1, keepdims=True)
    placed = marks * (prefix + offset)
    ranks = [
        jnp.sum(placed[k * classes : (k + 1) * classes], axis=0, keepdims=True).astype(jnp.int32)
        for k in range(top)
    ]
    totals = jnp.sum(marks, axis=1, keepdims=True)
    total = totals[:classes]
    for k in range(1, top):
        total = total + totals[k * classes : (k + 1) * classes]
    most = jnp.max(total.astype(jnp.int32))
    lane_rows = cap // 128
    spread = jnp.broadcast_to(total, (classes, 128))
    for c in range(classes):
        out_ref[c, FIELDS * lane_rows : FIELDS * lane_rows + 1, :] = spread[c : c + 1, :]
    iota_rank = lax.broadcasted_iota(jnp.int32, (CHUNK, columns), 0)

    def one_chunk(j, carry):
        found = jnp.zeros((CHUNK, len(parts) * classes), jnp.float32)
        for k in range(top):
            hot = jnp.where(iota_rank == ranks[k] - j * CHUNK, 1.0, 0.0).astype(jnp.bfloat16)
            found = found + lax.dot_general(
                hot, values[k], (((1,), (1,)), ((), ())), preferred_element_type=jnp.float32
            )
        turned = found.T
        part = lambda p: turned[p * classes : (p + 1) * classes]
        fields = [
            part(0) * 128.0 + part(1),
            part(4) + part(5) + part(6),
            part(2) * 256.0 + part(3) + part(7) - 1.0,
        ]
        for f in range(FIELDS):
            for h in range(CHUNK // 128):
                at = f * lane_rows + j * (CHUNK // 128) + h
                for c in range(classes):
                    out_ref[c, pl.ds(at, 1), :] = fields[f][c : c + 1, h * 128 : (h + 1) * 128]
        return carry

    lax.fori_loop(0, (most + CHUNK - 1) // CHUNK, one_chunk, 0)


def build_lists(sizes, owner, slot, weight):
    nz, nx, nc, quarter, classes, cap = sizes
    top, columns = owner.shape
    lane_rows = cap // 128
    return pl.pallas_call(
        functools.partial(lists_kernel, sizes),
        out_shape=jax.ShapeDtypeStruct((classes, FIELDS * lane_rows + 8, 128), jnp.float32),
        in_specs=[pl.BlockSpec(memory_space=pltpu.VMEM)] * 3,
        out_specs=pl.BlockSpec(memory_space=pltpu.VMEM),
        scratch_shapes=[pltpu.VMEM((top, 8 * classes, columns), jnp.bfloat16)],
        compiler_params=pltpu.CompilerParams(vmem_limit_bytes=24 * 1024 * 1024),
    )(owner, slot, weight)


STEP = 16


def partials_kernel(cap, where_ref, count_ref, row_ref, weight_ref, list_ref, table_ref, out_ref, picked):
    step = pl.program_id(0)
    columns = out_ref.shape[1]

    @pl.when(step == 0)
    def _():
        picked[...] = jnp.zeros_like(picked)

    count = count_ref[where_ref[step]]

    def gather(i, carry):
        base = pl.multiple_of(i * STEP, STEP)
        for u in range(STEP):
            picked[pl.ds(base + u, 1), :] = (
                table_ref[pl.ds(row_ref[0, 0, base + u], 1), :] * weight_ref[0, 0, base + u]
            )
        return carry

    lax.fori_loop(0, (count + STEP - 1) // STEP, gather, 0)
    out_ref[...] = jnp.zeros_like(out_ref)
    lane_rows = cap // 128
    iota = lax.broadcasted_iota(jnp.int32, (columns, 128), 0)

    def combine(j, carry):
        rows = picked[pl.ds(pl.multiple_of(j * CHUNK, CHUNK), CHUNK), :]
        high = rows.astype(jnp.bfloat16)
        low = (rows - high.astype(jnp.float32)).astype(jnp.bfloat16)
        both = jnp.concatenate([high, low], 1)
        hot = []
        for h in range(CHUNK // 128):
            at = 2 * lane_rows + j * (CHUNK // 128) + h
            place = list_ref[0, pl.ds(at, 1), :].astype(jnp.int32)
            hot.append(jnp.where(iota == place, 1.0, 0.0).astype(jnp.bfloat16))
        summed = jnp.dot(jnp.concatenate(hot, 1), both, preferred_element_type=jnp.float32)
        out_ref[0] += summed[:, :128] + summed[:, 128:]
        return carry

    lax.fori_loop(0, (count + CHUNK - 1) // CHUNK, combine, 0)


def partial_sums(cap, columns, order, counts, rows, weights, lists, table):
    steps = order.shape[0]
    places = rows.shape[0]
    return pl.pallas_call(
        functools.partial(partials_kernel, cap),
        grid_spec=pltpu.PrefetchScalarGridSpec(
            num_scalar_prefetch=2,
            grid=(steps,),
            in_specs=[
                pl.BlockSpec((1, 1, cap), lambda s, at, n: (at[s], 0, 0), memory_space=pltpu.SMEM),
                pl.BlockSpec((1, 1, cap), lambda s, at, n: (at[s], 0, 0), memory_space=pltpu.SMEM),
                pl.BlockSpec((1,) + lists.shape[1:], lambda s, at, n: (at[s], 0, 0)),
                pl.BlockSpec(table.shape, lambda s, at, n: (0, 0)),
            ],
            out_specs=pl.BlockSpec((1, columns, 128), lambda s, at, n: (s, 0, 0)),
            scratch_shapes=[pltpu.VMEM((cap, 128), jnp.float32)],
        ),
        out_shape=jax.ShapeDtypeStruct((steps, columns, 128), jnp.float32),
        compiler_params=pltpu.CompilerParams(vmem_limit_bytes=32 * 1024 * 1024),
    )(order, counts, rows, weights, lists, table)


def moved(value, axis, by):
    count = lax.axis_size(axis)
    return lax.ppermute(value, axis, [(i, (i + by) % count) for i in range(count)])


def ring_sum(get, axis):
    far = get(2)
    half = far.shape[0] // 2
    up = moved(far[:half], axis, 1)
    down = moved(far[half:], axis, -1)
    near_up, near_down = get(1), get(3)
    near_up = jnp.concatenate([near_up[:half] + up, near_up[half:]], 0)
    near_down = jnp.concatenate([near_down[:half], near_down[half:] + down], 0)
    return get(0) + moved(near_up, axis, 1) + moved(near_down, axis, -1)


def shifted(shard, axis, by):
    devices = lax.axis_size(axis)
    pairs = [(i, i + by) for i in range(devices) if 0 <= i + by < devices]
    return lax.ppermute(shard, axis, pairs)


def padded_2(shard, axis, dim, width):
    length = shard.shape[dim]
    last = lax.slice_in_dim(shard, length - width, length, axis=dim)
    initial = lax.slice_in_dim(shard, 0, width, axis=dim)
    before = shifted(last, axis, 1)
    after = shifted(initial, axis, -1)
    return jnp.concatenate([before, shard, after], axis=dim)


def ahead(values, along):
    count = values.shape[along]
    tail = jnp.zeros_like(lax.slice_in_dim(values, 0, 1, axis=along))
    return jnp.concatenate([lax.slice_in_dim(values, 1, count, axis=along), tail], along)


def behind(values, along):
    count = values.shape[along]
    head = jnp.zeros_like(lax.slice_in_dim(values, 0, 1, axis=along))
    return jnp.concatenate([head, lax.slice_in_dim(values, 0, count - 1, axis=along)], along)


def lower_mean(values, along):
    count = values.shape[along]
    before = jnp.concatenate(
        [
            lax.slice_in_dim(values, 0, 1, axis=along),
            lax.slice_in_dim(values, 0, count - 1, axis=along),
        ],
        along,
    )
    return 0.5 * (values + before)


def forward_diff(values, along):
    return ahead(values, along) - values


def backward_diff(values, along):
    return values - behind(values, along)


SUB = ("z", "x", "c")


def log_conductivity(model, block_owner_rank, source_slot, weights):
    ny, nz, nx, nc = (lax.axis_size(a) for a in ("y", "z", "x", "c"))
    quarter, block = model.shape[0], model.shape[2]
    columns, top = weights.shape[1:]
    table = lax.all_gather(model, ("z", "c"), axis=0, tiled=True).reshape(-1, block)
    classes = ny * nx
    cap = min(columns * top, nz * nc * 128)
    sizes = (nz, nx, nc, quarter, classes, cap)
    lists = build_lists(sizes, block_owner_rank[0].T, source_slot[0].T, weights[0].T)
    lists = lax.all_to_all(lists, ("y", "x"), split_axis=0, concat_axis=0, tiled=True)
    lane_rows = cap // 128
    rows = lists[:, :lane_rows].reshape(classes, 1, cap).astype(jnp.int32)
    factors = lists[:, lane_rows : 2 * lane_rows].reshape(classes, 1, cap)
    counts = lists[:, FIELDS * lane_rows, 0].astype(jnp.int32)
    step = jnp.arange(classes, dtype=jnp.int32)
    order = (lax.axis_index("y") + step // nx) % ny * nx + (lax.axis_index("x") + step % nx) % nx
    sums = partial_sums(cap, columns, order, counts, rows, factors, lists, table)
    sums = sums.reshape(ny, nx, columns, block)
    half = columns // 2
    first = ring_sum(lambda d: sums[d, :, :half], "y")
    second = ring_sum(lambda d: sums[:, d, half:], "x")
    first = sum((moved(first[d], "x", d) for d in (2, 1, 3)), first[0])
    second = sum((moved(second[d], "y", d) for d in (2, 1, 3)), second[0])
    return jnp.concatenate([first, second], 0)


def per_device(model, block_owner_rank, source_slot, weights, field, source, freq):
    efield = field[0]
    x_cell_count = efield.shape[2]
    cells_y = efield.shape[3]
    log_cond = log_conductivity(model, block_owner_rank, source_slot, weights)
    log_cond = log_cond.reshape(x_cell_count, cells_y, -1)
    conduct = jnp.exp(log_cond)
    first_device = lax.axis_index(SUB) == 0
    prior_plane = shifted(conduct[-1:], SUB, 1)
    prior_plane = jnp.where(first_device, conduct[:1], prior_plane)
    extended = jnp.concatenate([prior_plane, conduct], 0)
    sig_x = lower_mean(lower_mean(conduct, 1), 2)
    z_means = lower_mean(extended, 2)
    sig_y = 0.5 * (z_means[1:] + z_means[:-1])
    y_means = lower_mean(extended, 1)
    sig_z = 0.5 * (y_means[1:] + y_means[:-1])
    sigma_edges = jnp.stack([sig_x, sig_y, sig_z], 0)
    padded = padded_2(efield, SUB, 2, 1)
    field_x, field_y, field_z = (padded[:, 0], padded[:, 1], padded[:, 2])
    lower_x, lower_y, lower_z = (field_x[:, :-1], field_y[:, :-1], field_z[:, :-1])
    hx_part = forward_diff(lower_z, 2) - forward_diff(lower_y, 3)
    hy_part = forward_diff(lower_x, 3) - (field_z[:, 1:] - field_z[:, :-1])
    hz_part = field_y[:, 1:] - field_y[:, :-1] - forward_diff(lower_x, 2)
    rim_scale = jnp.where(first_device, 0.0, 1.0).astype(jnp.float32)
    plane_scale = jnp.concatenate(
        [rim_scale[None], jnp.ones((x_cell_count,), jnp.float32)]
    ).reshape(1, x_cell_count + 1, 1, 1)
    hx_part = hx_part * plane_scale
    hy_part = hy_part * plane_scale
    hz_part = hz_part * plane_scale
    curl_x = backward_diff(hz_part[:, 1:], 2) - backward_diff(hy_part[:, 1:], 3)
    curl_y = backward_diff(hx_part[:, 1:], 3) - (hz_part[:, 1:] - hz_part[:, :-1])
    curl_z = hy_part[:, 1:] - hy_part[:, :-1] - backward_diff(hx_part[:, 1:], 2)
    curl = jnp.stack([curl_x, curl_y, curl_z], 1)
    omega = freq[0]
    real_part = curl[0] - omega * sigma_edges * efield[1] - source[0, 0]
    imaginary_component = curl[1] + omega * sigma_edges * efield[0] - source[0, 1]
    return jnp.stack([real_part, imaginary_component], 0)[None]


def solution(mesh):
    fine = Mesh(mesh.devices.reshape(4, 8, 4, 2), ("y",) + SUB)
    in_specs = (
        P("y", SUB, None),
        P("y", SUB, None),
        P("y", SUB, None),
        P("y", SUB, None),
        P("y", None, None, SUB, None, None),
        P("y", None, None, SUB, None, None),
        P("y"),
    )
    out_specs = P("y", None, None, SUB, None, None)
    return jax.shard_map(
        per_device, mesh=fine, in_specs=in_specs, out_specs=out_specs, check_vma=False
    )
```

time: 219 us -> 135 us (0.62)
  matrix products: 76.2 us -> 0 us
  waiting for transfers between devices: 75.5 us -> 53.7 us
  blocking collectives: 20 us -> 0 us
  Pallas kernels: 0 us -> 17.9 us
  starting transfers between devices: 20.3 us -> 32.9 us
  local copies, waits for them, and re-layouts: 5.07 us -> 8.66 us
    dot_general x6 -> x0, matrix products: 76.2 us -> none  [the longest x1 32.3 us: per_device(): jnp.einsum('glm,ma->gla', request_onehot, local_model_block[:, 0, :], pre...]
    ppermute x2 -> x14, waiting for transfers between devices: 68 us -> 25.3 us  [moved(): lax.ppermute(value, axis, [(i, (i + by) % count) for i in range(count)])]
    all_to_all x1 -> x0, blocking collectives: 20 us -> none  [per_device(): lax.all_to_all(request_table, 'sub', split_axis=0, concat_axis=0, tiled=T...]
    pallas_call x0 -> x2, Pallas kernels: none -> 17.9 us  [the longest x1 15.1 us: partial_sums(): pl.pallas_call(functools.partial(partials_kernel, cap), grid_spec=pltpu.P...]
    all_gather x1, waiting for transfers between devices: 1.51 us -> 17.8 us  [log_conductivity(): lax.all_gather(model, ('z', 'c'), axis=0, tiled=True).reshape(-1, block)]
    ppermute x2 -> x14, starting transfers between devices: 7.89 us -> 16.1 us  [moved(): lax.ppermute(value, axis, [(i, (i + by) % count) for i in range(count)])]
    ppermute x1 -> x3, starting transfers between devices: 1.92 us -> 9.59 us  [shifted(): return lax.ppermute(shard, axis, pairs)]
    unnamed x12 -> x15, local copies, waits for them, and re-layouts: 2.14 us -> 7.5 us
  transfers between devices with their start and end apart: 5 -> 19, of which waited for: 3 -> 15; matrix products, arithmetic and copies ran while one was open for 13% -> 4% of each run, Pallas kernels for 0% -> 2%
where the time goes in v1:
time: 135 us; the launch traced here: 134 us
  waiting for transfers between devices  53.7 us (40%)
  starting transfers between devices  32.9 us (24%)
  Pallas kernels  17.9 us (13%)
  between operations  14.4 us (11%)
  local copies, waits for them, and re-layouts  8.66 us (6%)
  other arithmetic  6.37 us (5%)
    ppermute x14, waiting for transfers between devices, moved(): lax.ppermute(value, axis, [(i, (i + by) % count) for i in range(count)])  25.3 us
    all_gather x1, waiting for transfers between devices, log_conductivity(): lax.all_gather(model, ('z', 'c'), axis=0, tiled=True).reshape(-1, block)  17.8 us
    ppermute x14, starting transfers between devices, moved(): lax.ppermute(value, axis, [(i, (i + by) % count) for i in range(count)])  16.1 us
    pallas_call x1, Pallas kernels, partial_sums(): pl.pallas_call(functools.partial(partials_kernel, cap), grid_spec=pltpu.P...  15.1 us
    ppermute x3, waiting for transfers between devices, shifted(): return lax.ppermute(shard, axis, pairs)  9.94 us
    ppermute x3, starting transfers between devices, shifted(): return lax.ppermute(shard, axis, pairs)  9.59 us
    unnamed x15, local copies, waits for them, and re-layouts  7.5 us
    all_to_all x1, starting transfers between devices, log_conductivity(): lax.all_to_all(lists, ('y', 'x'), split_axis=0, concat_axis=0, tiled=True)  7.16 us
  transfers between devices with their start and end apart: 19, of which 15 were waited for; matrix products, arithmetic and copies ran while one was open for 4% of the time, Pallas kernels for 2%

profile of v1, /device:TPU:56, one launch (start us, length us, event | category | flops | bytes accessed | tf_op | source)
XLA Modules:
  0.0 134.0 jit_solution(14347180181983692571)
XLA Ops:
  6.5 0.7 all-gather.2.cloned.1.call-update
  7.3 0.7 copy-done.1
  8.0 0.7 copy-done.2
  8.7 0.7 copy-done.3
  9.4 2.8 %shard_map.73 = f32[16,56,128]{2,1,0:T(8,128)} custom-call(s32[8,512]{1,0:T(8,128)S(1)} %bitcast.167, s32[8,512]{1,0:T(8,128)S(1)} %bitcast.168, f32[8,512]{1,0:T(8,128)S(1)} %bitcast.169), custom_call_target="tpu_custom_call" | custom-call | tf_op jit(solution)/shard_map/pallas_call | solution.py:111
  12.2 7.2 %all-to-all-start = ((f32[16,56,128]{2,1,0:T(8,128)}), f32[16,56,128]{2,1,0:T(8,128)S(1)}, u32[]{:S(2)}, u32[]{:S(2)}) async-start(f32[16,56,128]{2,1,0:T(8,128)} %shard_map.73), calls=%async_computation | async-start | bytes 917504 | tf_op jit(solution)/shard_map/all_to_all | solution.py:261
  19.4 1.5 %copy.74 = f32[1,2,3,8,64,128]{5,4,3,1,2,0:T(8,128)S(1)} copy(f32[1,2,3,8,64,128]{5,4,3,2,1,0:T(8,128)} %param.11) | data formatting | bytes 3145728 | tf_op args[4]
  20.9 1.9 %collective-permute-start = (f32[2,3,1,64,128]{4,3,2,0,1:T(8,128)S(1)}, f32[2,3,1,64,128]{4,3,2,0,1:T(8,128)S(1)}, u32[]{:S(2)}, u32[]{:S(2)}) collective-permute-start(f32[2,3,1,64,128]{4,3,2,0,1:T(8,128)S(1)} %get-tuple-element.24), channel_id=1, source_target_pairs={{0,1},{1,2},{2,3},{3,4},{4,5},{5,6},{6,7},{7,8},{8,9},{9,10},{10,1... | collective-permute-start | bytes 589832 | tf_op jit(solution)/shard_map/ppermute | solution.py:205
  22.9 5.8 %collective-permute-start.1 = (f32[2,3,1,64,128]{4,3,2,0,1:T(8,128)S(1)}, f32[2,3,1,64,128]{4,3,2,0,1:T(8,128)S(1)}, u32[]{:S(2)}, u32[]{:S(2)}) collective-permute-start(f32[2,3,1,64,128]{4,3,2,0,1:T(8,128)S(1)} %get-tuple-element.25), channel_id=1, source_target_pairs={{1,0},{2,1},{3,2},{4,3},{5,4},{6,5},{7,6},{8,7},{9,8},{10,9},{11,1... | collective-permute-start | bytes 589832 | tf_op jit(solution)/shard_map/ppermute | solution.py:205
  29.3 1.5 %collective-permute-done = f32[2,3,1,64,128]{4,3,2,0,1:T(8,128)S(1)} collective-permute-done((f32[2,3,1,64,128]{4,3,2,0,1:T(8,128)S(1)}, f32[2,3,1,64,128]{4,3,2,0,1:T(8,128)S(1)}, u32[]{:S(2)}, u32[]{:S(2)}) %collective-permute-start) | collective-permute-done | bytes 196640 | tf_op jit(solution)/shard_map/ppermute | solution.py:205
  30.8 3.2 %collective-permute-done.1 = f32[2,3,1,64,128]{4,3,2,0,1:T(8,128)S(1)} collective-permute-done((f32[2,3,1,64,128]{4,3,2,0,1:T(8,128)S(1)}, f32[2,3,1,64,128]{4,3,2,0,1:T(8,128)S(1)}, u32[]{:S(2)}, u32[]{:S(2)}) %collective-permute-start.1) | collective-permute-done | bytes 196640 | tf_op jit(solution)/shard_map/ppermute | solution.py:205
  34.0 1.5 %pad_maximum_fusion = f32[2,3,10,64,128]{4,3,2,0,1:T(8,128)} fusion(f32[2,3,1,64,128]{4,3,2,0,1:T(8,128)S(1)} %collective-permute-done.1, f32[2,3,8,64,128]{4,3,2,0,1:T(8,128)S(1)} %bitcast.180, f32[2,3,1,64,128]{4,3,2,0,1:T(8,128)S(1)} %collective-permute-done), kind=kLoop, calls=%fused_computation | loop fusion | flops 983040 | bytes 3932160 | tf_op jit(solution)/shard_map/concatenate | solution.py:214
  35.4 0.4 fusion.39.count_ref
  35.9 17.8 %all-gather.2.cloned.1.call-done = f32[8192,1,128]{2,0,1:T(8,128)} async-done(((f32[512,1,128]{2,0,1:T(8,128)}), f32[8192,1,128]{2,0,1:T(8,128)}) %all-gather.2.cloned.1.call-update) | async-done | bytes 4194320 | tf_op jit(solution)/shard_map/all_gather | solution.py:256
  53.6 2.2 %copy-done = f32[8192,1,128]{2,0,1:T(8,128)S(1)} copy-done((f32[8192,1,128]{2,0,1:T(8,128)S(1)}, f32[8192,1,128]{2,0,1:T(8,128)}, u32[]{:S(2)}) %copy-start) | copy-done | bytes 4194328
  55.8 15.1 %shard_map.74 = f32[16,512,128]{2,1,0:T(8,128)S(1)} custom-call(s32[16]{0:T(128)S(1)} %fusion.42.where_ref, s32[16]{0:T(128)S(1)} %fusion.39.count_ref, s32[16,1,2048]{2,1,0:T(1,128)S(1)} %bitcast.166, f32[16,1,2048]{2,1,0:T(1,128)S(1)} %bitcast.165, f32[16,56,128]{2,1,0:T(8,128)S(1)} %all-to-all-done.list_ref, f32[8192,128]{1,0:T(8,128)S(1)} %bitcast.164), custom_call_target="tpu_custom_call" | custom-call | tf_op jit(solution)/shard_map/pallas_call | solution.py:167
  71.1 2.5 %collective-permute-start.11 = (f32[2,256,128]{2,1,0:T(8,128)S(1)}, f32[2,256,128]{2,1,0:T(8,128)S(1)}, u32[]{:S(2)}, u32[]{:S(2)}) collective-permute-start(f32[2,256,128]{2,1,0:T(8,128)S(1)} %get-tuple-element.20), channel_id=1, source_target_pairs={{0,6},{2,0},{4,2},{6,4},{1,7},{3,1},{5,3},{7,5},{8,14},{10,8},{12,... | collective-permute-start | bytes 786440 | tf_op jit(solution)/shard_map/ppermute | solution.py:188
  73.6 0.6 collective-permute-start.2
  74.3 1.4 %collective-permute-start.4 = (f32[2,256,128]{2,1,0:T(8,128)S(1)}, f32[2,256,128]{2,1,0:T(8,128)S(1)}, u32[]{:S(2)}, u32[]{:S(2)}) collective-permute-start(f32[2,256,128]{2,1,0:T(8,128)S(1)} %get-tuple-element.14), channel_id=1, source_target_pairs={{0,192},{64,0},{128,64},{192,128},{1,193},{65,1},{129,65},{193,129... | collective-permute-start | bytes 786440 | tf_op jit(solution)/shard_map/ppermute | solution.py:188
  75.9 0.2 slice.371
  76.2 0.2 slice.378
  76.4 3.4 %collective-permute-done.11 = f32[2,256,128]{2,1,0:T(8,128)S(1)} collective-permute-done((f32[2,256,128]{2,1,0:T(8,128)S(1)}, f32[2,256,128]{2,1,0:T(8,128)S(1)}, u32[]{:S(2)}, u32[]{:S(2)}) %collective-permute-start.11) | collective-permute-done | bytes 262176 | tf_op jit(solution)/shard_map/ppermute | solution.py:188
  79.8 2.2 %collective-permute-done.2 = f32[2,256,128]{2,1,0:T(8,128)S(1)} collective-permute-done((f32[2,256,128]{2,1,0:T(8,128)S(1)}, f32[2,256,128]{2,1,0:T(8,128)S(1)}, u32[]{:S(2)}, u32[]{:S(2)}) %collective-permute-start.2) | collective-permute-done | bytes 262176 | tf_op jit(solution)/shard_map/ppermute | solution.py:188
  81.9 1.2 collective-permute-done.4
  83.1 1.5 %collective-permute-done.9 = f32[2,256,128]{2,1,0:T(8,128)S(1)} collective-permute-done((f32[2,256,128]{2,1,0:T(8,128)S(1)}, f32[2,256,128]{2,1,0:T(8,128)S(1)}, u32[]{:S(2)}, u32[]{:S(2)}) %collective-permute-start.9) | collective-permute-done | bytes 262176 | tf_op jit(solution)/shard_map/ppermute | solution.py:188
  84.9 3.3 %collective-permute-start.12 = (f32[4,256,128]{2,1,0:T(8,128)S(1)}, f32[4,256,128]{2,1,0:T(8,128)S(1)}, u32[]{:S(2)}, u32[]{:S(2)}) collective-permute-start(f32[4,256,128]{2,1,0:T(8,128)S(1)} %pad_maximum_fusion.6), channel_id=1, source_target_pairs={{0,6},{2,0},{4,2},{6,4},{1,7},{3,1},{5,3},{7,5},{8,14},{10,8},{12,... | collective-permute-start | bytes 1572872 | tf_op jit(solution)/shard_map/ppermute | solution.py:188
  88.3 1.6 %collective-permute-start.3 = (f32[4,256,128]{2,1,0:T(8,128)S(1)}, f32[4,256,128]{2,1,0:T(8,128)S(1)}, u32[]{:S(2)}, u32[]{:S(2)}) collective-permute-start(f32[4,256,128]{2,1,0:T(8,128)S(1)} %pad_maximum_fusion.3), channel_id=1, source_target_pairs={{0,64},{64,128},{128,192},{192,0},{1,65},{65,129},{129,193},{193,1... | collective-permute-start | bytes 1572872 | tf_op jit(solution)/shard_map/ppermute | solution.py:188
  89.9 0.6 collective-permute-start.5
  90.5 0.7 fusion.5
  91.4 0.6 subtract_bitcast_fusion
  92.1 6.4 %collective-permute-done.10 = f32[4,256,128]{2,1,0:T(8,128)S(1)} collective-permute-done((f32[4,256,128]{2,1,0:T(8,128)S(1)}, f32[4,256,128]{2,1,0:T(8,128)S(1)}, u32[]{:S(2)}, u32[]{:S(2)}) %collective-permute-start.10) | collective-permute-done | bytes 524320 | tf_op jit(solution)/shard_map/ppermute | solution.py:188
  98.5 1.7 %collective-permute-done.3 = f32[4,256,128]{2,1,0:T(8,128)S(1)} collective-permute-done((f32[4,256,128]{2,1,0:T(8,128)S(1)}, f32[4,256,128]{2,1,0:T(8,128)S(1)}, u32[]{:S(2)}, u32[]{:S(2)}) %collective-permute-start.3) | collective-permute-done | bytes 524320 | tf_op jit(solution)/shard_map/ppermute | solution.py:188
  100.2 2.2 %collective-permute-done.5 = f32[4,256,128]{2,1,0:T(8,128)S(1)} collective-permute-done((f32[4,256,128]{2,1,0:T(8,128)S(1)}, f32[4,256,128]{2,1,0:T(8,128)S(1)}, u32[]{:S(2)}, u32[]{:S(2)}) %collective-permute-start.5) | collective-permute-done | bytes 524320 | tf_op jit(solution)/shard_map/ppermute | solution.py:188
  102.4 0.2 fusion.9
  102.8 1.1 collective-permute-start.7
  103.9 2.3 %collective-permute-start.8 = (f32[256,128]{1,0:T(8,128)S(1)}, f32[256,128]{1,0:T(8,128)S(1)}, u32[]{:S(2)}, u32[]{:S(2)}) collective-permute-start(f32[256,128]{1,0:T(8,128)S(1)} %get-tuple-element.33), channel_id=1, source_target_pairs={{0,6},{2,0},{4,2},{6,4},{1,7},{3,1},{5,3},{7,5},{8,14},{10,8},{12,... | collective-permute-start | bytes 393224 | tf_op jit(solution)/shard_map/ppermute | solution.py:188
  106.3 0.6 collective-permute-start.13
  106.9 1.8 %collective-permute-start.14 = (f32[256,128]{1,0:T(8,128)S(1)}, f32[256,128]{1,0:T(8,128)S(1)}, u32[]{:S(2)}, u32[]{:S(2)}) collective-permute-start(f32[256,128]{1,0:T(8,128)S(1)} %get-tuple-element.37), channel_id=1, source_target_pairs={{0,64},{64,128},{128,192},{192,0},{1,65},{65,129},{129,193},{193,1... | collective-permute-start | bytes 393224 | tf_op jit(solution)/shard_map/ppermute | solution.py:188
  108.7 0.6 collective-permute-done.6
  109.3 1.3 collective-permute-done.7
  110.6 2.2 %collective-permute-done.13 = f32[256,128]{1,0:T(8,128)S(1)} collective-permute-done((f32[256,128]{1,0:T(8,128)S(1)}, f32[256,128]{1,0:T(8,128)S(1)}, u32[]{:S(2)}, u32[]{:S(2)}) %collective-permute-start.13) | collective-permute-done | bytes 131104 | tf_op jit(solution)/shard_map/ppermute | solution.py:188
  112.9 2.7 %collective-permute-done.15 = f32[256,128]{1,0:T(8,128)S(1)} collective-permute-done((f32[256,128]{1,0:T(8,128)S(1)}, f32[256,128]{1,0:T(8,128)S(1)}, u32[]{:S(2)}, u32[]{:S(2)}) %collective-permute-start.15) | collective-permute-done | bytes 131104 | tf_op jit(solution)/shard_map/ppermute | solution.py:188
  115.8 1.9 %collective-permute-start.16 = (f32[1,64,128]{2,1,0:T(8,128)S(1)}, f32[1,64,128]{2,1,0:T(8,128)S(1)}, u32[]{:S(2)}, u32[]{:S(2)}) collective-permute-start(f32[1,64,128]{2,1,0:T(8,128)S(1)} %slice_bitcast_fusion.27), channel_id=1, source_target_pairs={{0,1},{1,2},{2,3},{3,4},{4,5},{5,6},{6,7},{7,8},{8,9},{9,10},{10,1... | collective-permute-start | bytes 98312 | tf_op jit(solution)/shard_map/ppermute | solution.py:205
  117.9 5.3 %collective-permute-done.16 = f32[1,64,128]{2,1,0:T(8,128)S(1)} collective-permute-done((f32[1,64,128]{2,1,0:T(8,128)S(1)}, f32[1,64,128]{2,1,0:T(8,128)S(1)}, u32[]{:S(2)}, u32[]{:S(2)}) %collective-permute-start.16) | collective-permute-done | bytes 32800 | tf_op jit(solution)/shard_map/ppermute | solution.py:205
  123.5 1.2 copy-done.5
  124.6 0.5 copy-done.6
  125.1 0.7 fusion.1
  125.9 1.2 maximum_bitcast_fusion
  (55 shorter events, 2.0 us)
Async XLA Ops:
  6.5 47.1 %all-gather.2.cloned.1.call-start = ((), (), s32[]{:S(2)}) async-start(), calls=%async_computation.1 | async-start | bytes 4456448 | tf_op jit(solution)/shard_map/all_gather | solution.py:256
  7.3 0.7 copy-start.1
  8.0 0.7 copy-start.2
  8.7 0.7 copy-start.3
  12.2 23.2 %all-to-all-start = ((f32[16,56,128]{2,1,0:T(8,128)}), f32[16,56,128]{2,1,0:T(8,128)S(1)}, u32[]{:S(2)}, u32[]{:S(2)}) async-start(f32[16,56,128]{2,1,0:T(8,128)} %shard_map.73), calls=%async_computation | async-start | bytes 917504 | tf_op jit(solution)/shard_map/all_to_all | solution.py:261
  20.9 9.9 %collective-permute-start = (f32[2,3,1,64,128]{4,3,2,0,1:T(8,128)S(1)}, f32[2,3,1,64,128]{4,3,2,0,1:T(8,128)S(1)}, u32[]{:S(2)}, u32[]{:S(2)}) collective-permute-start(f32[2,3,1,64,128]{4,3,2,0,1:T(8,128)S(1)} %get-tuple-element.24), channel_id=1, source_target_pairs={{0,1},{1,2},{2,3},{3,4},{4,5},{5,6},{6,7},{7,8},{8,9},{9,10},{10,1... | collective-permute-start | bytes 589832 | tf_op jit(solution)/shard_map/ppermute | solution.py:205
  22.9 11.1 %collective-permute-start.1 = (f32[2,3,1,64,128]{4,3,2,0,1:T(8,128)S(1)}, f32[2,3,1,64,128]{4,3,2,0,1:T(8,128)S(1)}, u32[]{:S(2)}, u32[]{:S(2)}) collective-permute-start(f32[2,3,1,64,128]{4,3,2,0,1:T(8,128)S(1)} %get-tuple-element.25), channel_id=1, source_target_pairs={{1,0},{2,1},{3,2},{4,3},{5,4},{6,5},{7,6},{8,7},{9,8},{10,9},{11,1... | collective-permute-start | bytes 589832 | tf_op jit(solution)/shard_map/ppermute | solution.py:205
  53.6 2.2 %copy-start = (f32[8192,1,128]{2,0,1:T(8,128)S(1)}, f32[8192,1,128]{2,0,1:T(8,128)}, u32[]{:S(2)}) copy-start(f32[8192,1,128]{2,0,1:T(8,128)} %all-gather.2.cloned.1.call-done) | copy-start | bytes 12582916
  71.0 4.7 %copy-start.4 = (f32[2,3,10,64,128]{4,3,2,0,1:T(8,128)S(1)}, f32[2,3,10,64,128]{4,3,2,0,1:T(8,128)}, u32[]{:S(2)}) copy-start(f32[2,3,10,64,128]{4,3,2,0,1:T(8,128)} %pad_maximum_fusion) | copy-start | bytes 5898244
  71.1 8.7 %collective-permute-start.11 = (f32[2,256,128]{2,1,0:T(8,128)S(1)}, f32[2,256,128]{2,1,0:T(8,128)S(1)}, u32[]{:S(2)}, u32[]{:S(2)}) collective-permute-start(f32[2,256,128]{2,1,0:T(8,128)S(1)} %get-tuple-element.20), channel_id=1, source_target_pairs={{0,6},{2,0},{4,2},{6,4},{1,7},{3,1},{5,3},{7,5},{8,14},{10,8},{12,... | collective-permute-start | bytes 786440 | tf_op jit(solution)/shard_map/ppermute | solution.py:188
  73.6 8.3 %collective-permute-start.2 = (f32[2,256,128]{2,1,0:T(8,128)S(1)}, f32[2,256,128]{2,1,0:T(8,128)S(1)}, u32[]{:S(2)}, u32[]{:S(2)}) collective-permute-start(f32[2,256,128]{2,1,0:T(8,128)S(1)} %get-tuple-element.13), channel_id=1, source_target_pairs={{0,64},{64,128},{128,192},{192,0},{1,65},{65,129},{129,193},{193,1... | collective-permute-start | bytes 786440 | tf_op jit(solution)/shard_map/ppermute | solution.py:188
  74.3 8.9 %collective-permute-start.4 = (f32[2,256,128]{2,1,0:T(8,128)S(1)}, f32[2,256,128]{2,1,0:T(8,128)S(1)}, u32[]{:S(2)}, u32[]{:S(2)}) collective-permute-start(f32[2,256,128]{2,1,0:T(8,128)S(1)} %get-tuple-element.14), channel_id=1, source_target_pairs={{0,192},{64,0},{128,64},{192,128},{1,193},{65,1},{129,65},{193,129... | collective-permute-start | bytes 786440 | tf_op jit(solution)/shard_map/ppermute | solution.py:188
  75.7 8.9 %collective-permute-start.9 = (f32[2,256,128]{2,1,0:T(8,128)S(1)}, f32[2,256,128]{2,1,0:T(8,128)S(1)}, u32[]{:S(2)}, u32[]{:S(2)}) collective-permute-start(f32[2,256,128]{2,1,0:T(8,128)S(1)} %get-tuple-element.17), channel_id=1, source_target_pairs={{0,2},{2,4},{4,6},{6,0},{1,3},{3,5},{5,7},{7,1},{8,10},{10,12},{12... | collective-permute-start | bytes 786440 | tf_op jit(solution)/shard_map/ppermute | solution.py:188
  84.8 13.7 %collective-permute-start.10 = (f32[4,256,128]{2,1,0:T(8,128)S(1)}, f32[4,256,128]{2,1,0:T(8,128)S(1)}, u32[]{:S(2)}, u32[]{:S(2)}) collective-permute-start(f32[4,256,128]{2,1,0:T(8,128)S(1)} %pad_maximum_fusion.5), channel_id=1, source_target_pairs={{0,2},{2,4},{4,6},{6,0},{1,3},{3,5},{5,7},{7,1},{8,10},{10,12},{12... | collective-permute-start | bytes 1572872 | tf_op jit(solution)/shard_map/ppermute | solution.py:188
  84.9 13.6 %collective-permute-start.12 = (f32[4,256,128]{2,1,0:T(8,128)S(1)}, f32[4,256,128]{2,1,0:T(8,128)S(1)}, u32[]{:S(2)}, u32[]{:S(2)}) collective-permute-start(f32[4,256,128]{2,1,0:T(8,128)S(1)} %pad_maximum_fusion.6), channel_id=1, source_target_pairs={{0,6},{2,0},{4,2},{6,4},{1,7},{3,1},{5,3},{7,5},{8,14},{10,8},{12,... | collective-permute-start | bytes 1572872 | tf_op jit(solution)/shard_map/ppermute | solution.py:188
  88.3 11.9 %collective-permute-start.3 = (f32[4,256,128]{2,1,0:T(8,128)S(1)}, f32[4,256,128]{2,1,0:T(8,128)S(1)}, u32[]{:S(2)}, u32[]{:S(2)}) collective-permute-start(f32[4,256,128]{2,1,0:T(8,128)S(1)} %pad_maximum_fusion.3), channel_id=1, source_target_pairs={{0,64},{64,128},{128,192},{192,0},{1,65},{65,129},{129,193},{193,1... | collective-permute-start | bytes 1572872 | tf_op jit(solution)/shard_map/ppermute | solution.py:188
  89.9 12.5 %collective-permute-start.5 = (f32[4,256,128]{2,1,0:T(8,128)S(1)}, f32[4,256,128]{2,1,0:T(8,128)S(1)}, u32[]{:S(2)}, u32[]{:S(2)}) collective-permute-start(f32[4,256,128]{2,1,0:T(8,128)S(1)} %pad_maximum_fusion.4), channel_id=1, source_target_pairs={{0,192},{64,0},{128,64},{192,128},{1,193},{65,1},{129,65},{193,129... | collective-permute-start | bytes 1572872 | tf_op jit(solution)/shard_map/ppermute | solution.py:188
  102.7 6.7 %collective-permute-start.6 = (f32[256,128]{1,0:T(8,128)S(1)}, f32[256,128]{1,0:T(8,128)S(1)}, u32[]{:S(2)}, u32[]{:S(2)}) collective-permute-start(f32[256,128]{1,0:T(8,128)S(1)} %get-tuple-element.32), channel_id=1, source_target_pairs={{0,4},{2,6},{4,0},{6,2},{1,5},{3,7},{5,1},{7,3},{8,12},{10,14},{12... | collective-permute-start | bytes 393224 | tf_op jit(solution)/shard_map/ppermute | solution.py:188
  102.8 7.8 %collective-permute-start.7 = (f32[256,128]{1,0:T(8,128)S(1)}, f32[256,128]{1,0:T(8,128)S(1)}, u32[]{:S(2)}, u32[]{:S(2)}) collective-permute-start(f32[256,128]{1,0:T(8,128)S(1)} %get-tuple-element.34), channel_id=1, source_target_pairs={{0,2},{2,4},{4,6},{6,0},{1,3},{3,5},{5,7},{7,1},{8,10},{10,12},{12... | collective-permute-start | bytes 393224 | tf_op jit(solution)/shard_map/ppermute | solution.py:188
  103.9 6.7 %collective-permute-start.8 = (f32[256,128]{1,0:T(8,128)S(1)}, f32[256,128]{1,0:T(8,128)S(1)}, u32[]{:S(2)}, u32[]{:S(2)}) collective-permute-start(f32[256,128]{1,0:T(8,128)S(1)} %get-tuple-element.33), channel_id=1, source_target_pairs={{0,6},{2,0},{4,2},{6,4},{1,7},{3,1},{5,3},{7,5},{8,14},{10,8},{12,... | collective-permute-start | bytes 393224 | tf_op jit(solution)/shard_map/ppermute | solution.py:188
  106.3 6.6 %collective-permute-start.13 = (f32[256,128]{1,0:T(8,128)S(1)}, f32[256,128]{1,0:T(8,128)S(1)}, u32[]{:S(2)}, u32[]{:S(2)}) collective-permute-start(f32[256,128]{1,0:T(8,128)S(1)} %get-tuple-element.35), channel_id=1, source_target_pairs={{0,128},{64,192},{128,0},{192,64},{1,129},{65,193},{129,1},{193,65... | collective-permute-start | bytes 393224 | tf_op jit(solution)/shard_map/ppermute | solution.py:188
  106.9 5.9 %collective-permute-start.14 = (f32[256,128]{1,0:T(8,128)S(1)}, f32[256,128]{1,0:T(8,128)S(1)}, u32[]{:S(2)}, u32[]{:S(2)}) collective-permute-start(f32[256,128]{1,0:T(8,128)S(1)} %get-tuple-element.37), channel_id=1, source_target_pairs={{0,64},{64,128},{128,192},{192,0},{1,65},{65,129},{129,193},{193,1... | collective-permute-start | bytes 393224 | tf_op jit(solution)/shard_map/ppermute | solution.py:188
  109.3 6.2 %collective-permute-start.15 = (f32[256,128]{1,0:T(8,128)S(1)}, f32[256,128]{1,0:T(8,128)S(1)}, u32[]{:S(2)}, u32[]{:S(2)}) collective-permute-start(f32[256,128]{1,0:T(8,128)S(1)} %get-tuple-element.36), channel_id=1, source_target_pairs={{0,192},{64,0},{128,64},{192,128},{1,193},{65,1},{129,65},{193,129... | collective-permute-start | bytes 393224 | tf_op jit(solution)/shard_map/ppermute | solution.py:188
  115.8 7.3 %collective-permute-start.16 = (f32[1,64,128]{2,1,0:T(8,128)S(1)}, f32[1,64,128]{2,1,0:T(8,128)S(1)}, u32[]{:S(2)}, u32[]{:S(2)}) collective-permute-start(f32[1,64,128]{2,1,0:T(8,128)S(1)} %slice_bitcast_fusion.27), channel_id=1, source_target_pairs={{0,1},{1,2},{2,3},{3,4},{4,5},{5,6},{6,7},{7,8},{8,9},{9,10},{10,1... | collective-permute-start | bytes 98312 | tf_op jit(solution)/shard_map/ppermute | solution.py:205
  123.2 1.4 %copy-start.5 = (f32[1,2,3,8,64,128]{5,4,3,2,1,0:T(8,128)S(1)}, f32[1,2,3,8,64,128]{5,4,3,2,1,0:T(8,128)}, u32[]{:S(2)}) copy-start(f32[1,2,3,8,64,128]{5,4,3,2,1,0:T(8,128)} %param.11) | copy-start | bytes 4718596
  123.2 1.9 %copy-start.6 = (f32[1,2,3,8,64,128]{5,4,3,2,1,0:T(8,128)S(1)}, f32[1,2,3,8,64,128]{5,4,3,2,1,0:T(8,128)}, u32[]{:S(2)}) copy-start(f32[1,2,3,8,64,128]{5,4,3,2,1,0:T(8,128)} %param.12) | copy-start | bytes 4718596
Sparse Core Ops, SparseCore 0:
  9.2 44.3 all-gather.1

commit v2 on v1

--- a/solution.py
+++ b/solution.py
@@ -9,6 +9,8 @@
 
 CHUNK = 256
 FIELDS = 3
+STEP = 16
+NEAR = 512
 
 
 def shift_of(count):
@@ -35,7 +37,7 @@
         high,
         middle,
         weight - high - middle,
-        jnp.ones((top, columns), jnp.float32),
+        jnp.zeros((top, columns), jnp.float32),
     ]
     iota_kind = lax.broadcasted_iota(jnp.int32, (classes, columns), 0)
     marks = []
@@ -47,9 +49,10 @@
     marks = jnp.concatenate(marks, 0)
     marks_low = marks.astype(jnp.bfloat16)
     rows = top * classes
-    before = lax.broadcasted_iota(jnp.int32, (columns, columns), 0) < lax.broadcasted_iota(
-        jnp.int32, (columns, columns), 1
-    )
+    half = columns // 2
+    column_i = lax.broadcasted_iota(jnp.int32, (columns, columns), 0)
+    column_j = lax.broadcasted_iota(jnp.int32, (columns, columns), 1)
+    before = (column_i < column_j) & ((column_i >= half) == (column_j >= half))
     prefix = jnp.dot(
         marks_low,
         jnp.where(before, 1.0, 0.0).astype(jnp.bfloat16),
@@ -63,21 +66,32 @@
         marks_low,
         preferred_element_type=jnp.float32,
     )
-    offset = jnp.sum(above, axis=1, keepdims=True)
-    placed = marks * (prefix + offset)
+    over = lambda value: jnp.sum(value, axis=1, keepdims=True)
+
+    def per_kind(value):
+        sums = over(value)
+        total = sums[:classes]
+        for k in range(1, top):
+            total = total + sums[k * classes : (k + 1) * classes]
+        return total
+
+    count_a, count_b = per_kind(marks[:, :half]), per_kind(marks[:, half:])
+    begin_b = ((count_a.astype(jnp.int32) + 127) >> 7) << 7
+    most = jnp.max(begin_b + count_b.astype(jnp.int32))
+    begin_rows = jnp.concatenate([begin_b.astype(jnp.float32)] * top, 0)
+    base_a, base_b = over(above[:, :half]), over(above[:, half:]) + begin_rows
+    lanes = lax.broadcasted_iota(jnp.int32, (rows, columns), 1)
+    placed = marks * (prefix + jnp.where(lanes < half, base_a, base_b))
     ranks = [
         jnp.sum(placed[k * classes : (k + 1) * classes], axis=0, keepdims=True).astype(jnp.int32)
         for k in range(top)
     ]
-    totals = jnp.sum(marks, axis=1, keepdims=True)
-    total = totals[:classes]
-    for k in range(1, top):
-        total = total + totals[k * classes : (k + 1) * classes]
-    most = jnp.max(total.astype(jnp.int32))
     lane_rows = cap // 128
-    spread = jnp.broadcast_to(total, (classes, 128))
-    for c in range(classes):
-        out_ref[c, FIELDS * lane_rows : FIELDS * lane_rows + 1, :] = spread[c : c + 1, :]
+    for f, total in enumerate((count_a, count_b)):
+        spread = jnp.broadcast_to(total, (classes, 128))
+        for c in range(classes):
+            at = FIELDS * lane_rows + f
+            out_ref[c, at : at + 1, :] = spread[c : c + 1, :]
     iota_rank = lax.broadcasted_iota(jnp.int32, (CHUNK, columns), 0)
 
     def one_chunk(j, carry):
@@ -92,7 +106,7 @@
         fields = [
             part(0) * 128.0 + part(1),
             part(4) + part(5) + part(6),
-            part(2) * 256.0 + part(3) + part(7) - 1.0,
+            part(2) * 256.0 + part(3),
         ]
         for f in range(FIELDS):
             for h in range(CHUNK // 128):
@@ -110,7 +124,7 @@
     lane_rows = cap // 128
     return pl.pallas_call(
         functools.partial(lists_kernel, sizes),
-        out_shape=jax.ShapeDtypeStruct((classes, FIELDS * lane_rows + 8, 128), jnp.float32),
+        out_shape=jax.ShapeDtypeStruct((classes, -(-(FIELDS * lane_rows + 2) // 8) * 8, 128), jnp.float32),
         in_specs=[pl.BlockSpec(memory_space=pltpu.VMEM)] * 3,
         out_specs=pl.BlockSpec(memory_space=pltpu.VMEM),
         scratch_shapes=[pltpu.VMEM((top, 8 * classes, columns), jnp.bfloat16)],
@@ -118,85 +132,112 @@
     )(owner, slot, weight)
 
 
-STEP = 16
-
-
-def partials_kernel(cap, where_ref, count_ref, row_ref, weight_ref, list_ref, table_ref, out_ref, picked):
-    step = pl.program_id(0)
-    columns = out_ref.shape[1]
-
-    @pl.when(step == 0)
-    def _():
-        picked[...] = jnp.zeros_like(picked)
-
-    count = count_ref[where_ref[step]]
-
-    def gather(i, carry):
-        base = pl.multiple_of(i * STEP, STEP)
-        for u in range(STEP):
-            picked[pl.ds(base + u, 1), :] = (
-                table_ref[pl.ds(row_ref[0, 0, base + u], 1), :] * weight_ref[0, 0, base + u]
-            )
-        return carry
-
-    lax.fori_loop(0, (count + STEP - 1) // STEP, gather, 0)
-    out_ref[...] = jnp.zeros_like(out_ref)
+def partials_kernel(
+    jobs, sizes, place_ref, count_ref, row_ref, weight_ref, rows_far, weights_far, list_ref, table_ref, *rest
+):
+    ny, nx, cap = sizes
+    outs, (picked, row_chunk, weight_chunk, sems) = rest[: len(jobs)], rest[len(jobs) :]
+    columns = outs[0].shape[1]
     lane_rows = cap // 128
     iota = lax.broadcasted_iota(jnp.int32, (columns, 128), 0)
-
-    def combine(j, carry):
-        rows = picked[pl.ds(pl.multiple_of(j * CHUNK, CHUNK), CHUNK), :]
+    lanes = lax.broadcasted_iota(jnp.int32, (1, 128), 1)
+    picked[...] = jnp.zeros_like(picked)
+
+    def gather(rows, weights, first, count):
+        def some(i, carry):
+            base = pl.multiple_of(i * STEP, STEP)
+            for u in range(STEP):
+                picked[pl.ds(base + u, 1), :] = (
+                    table_ref[pl.ds(rows[first + base + u], 1), :] * weights[first + base + u]
+                )
+            return carry
+
+        lax.fori_loop(0, (count + STEP - 1) // STEP, some, 0)
+
+    def chunk_sum(half, at, begin, count, j):
+        first = begin + j * CHUNK
+        left = jnp.minimum(count - j * CHUNK, CHUNK)
+        near = first + CHUNK <= NEAR
+
+        @pl.when(near)
+        def _():
+            gather(row_ref, weight_ref, at * NEAR + first, left)
+
+        @pl.when(jnp.logical_not(near))
+        def _():
+            span = pl.ds(pl.multiple_of(first, 128), CHUNK)
+            one = pltpu.make_async_copy(rows_far.at[at, 0, span], row_chunk, sems.at[0])
+            two = pltpu.make_async_copy(weights_far.at[at, 0, span], weight_chunk, sems.at[1])
+            one.start()
+            two.start()
+            one.wait()
+            two.wait()
+            gather(row_chunk, weight_chunk, 0, left)
+
+        rows = picked[...]
         high = rows.astype(jnp.bfloat16)
         low = (rows - high.astype(jnp.float32)).astype(jnp.bfloat16)
-        both = jnp.concatenate([high, low], 1)
         hot = []
         for h in range(CHUNK // 128):
-            at = 2 * lane_rows + j * (CHUNK // 128) + h
-            place = list_ref[0, pl.ds(at, 1), :].astype(jnp.int32)
+            line = 2 * lane_rows + lax.shift_right_logical(first, 7) + h
+            place = list_ref[at, pl.ds(line, 1), :].astype(jnp.int32) - half * columns
+            place = jnp.where(lanes < left - h * 128, place, -1)
             hot.append(jnp.where(iota == place, 1.0, 0.0).astype(jnp.bfloat16))
-        summed = jnp.dot(jnp.concatenate(hot, 1), both, preferred_element_type=jnp.float32)
-        out_ref[0] += summed[:, :128] + summed[:, 128:]
-        return carry
-
-    lax.fori_loop(0, (count + CHUNK - 1) // CHUNK, combine, 0)
-
-
-def partial_sums(cap, columns, order, counts, rows, weights, lists, table):
-    steps = order.shape[0]
-    places = rows.shape[0]
+        summed = jnp.dot(
+            jnp.concatenate(hot, 1), jnp.concatenate([high, low], 1), preferred_element_type=jnp.float32
+        )
+        return summed[:, :128] + summed[:, 128:]
+
+    for (half, dy, dx), out_ref in zip(jobs, outs):
+
+        def one(t, carry):
+            y = (place_ref[0] + (t if dy is None else dy)) % ny
+            x = (place_ref[1] + (t if dx is None else dx)) % nx
+            at = y * nx + x
+            count_a = count_ref[at]
+            count = count_ref[ny * nx + at] if half else count_a
+            begin = lax.shift_left(lax.shift_right_logical(count_a + 127, 7), 7) if half else 0
+            out_ref[t] = chunk_sum(half, at, begin, count, 0)
+
+            def more(j, carry):
+                out_ref[t] += chunk_sum(half, at, begin, count, j)
+                return carry
+
+            lax.fori_loop(1, (count + CHUNK - 1) // CHUNK, more, 0)
+            return carry
+
+        lax.fori_loop(0, out_ref.shape[0], one, 0)
+
+
+def partial_sums(jobs, sizes, half, place, counts, near_rows, near_weights, rows, weights, lists, table):
+    ny, nx, cap = sizes
+    vmem = pl.BlockSpec(memory_space=pltpu.VMEM)
+    smem = pl.BlockSpec(memory_space=pltpu.SMEM)
+    anywhere = pl.BlockSpec(memory_space=pl.ANY)
     return pl.pallas_call(
-        functools.partial(partials_kernel, cap),
-        grid_spec=pltpu.PrefetchScalarGridSpec(
-            num_scalar_prefetch=2,
-            grid=(steps,),
-            in_specs=[
-                pl.BlockSpec((1, 1, cap), lambda s, at, n: (at[s], 0, 0), memory_space=pltpu.SMEM),
-                pl.BlockSpec((1, 1, cap), lambda s, at, n: (at[s], 0, 0), memory_space=pltpu.SMEM),
-                pl.BlockSpec((1,) + lists.shape[1:], lambda s, at, n: (at[s], 0, 0)),
-                pl.BlockSpec(table.shape, lambda s, at, n: (0, 0)),
-            ],
-            out_specs=pl.BlockSpec((1, columns, 128), lambda s, at, n: (s, 0, 0)),
-            scratch_shapes=[pltpu.VMEM((cap, 128), jnp.float32)],
+        functools.partial(partials_kernel, jobs, sizes),
+        in_specs=[smem, smem, smem, smem, anywhere, anywhere, vmem, vmem],
+        out_specs=[vmem] * len(jobs),
+        scratch_shapes=[
+            pltpu.VMEM((CHUNK, 128), jnp.float32),
+            pltpu.SMEM((CHUNK,), jnp.int32),
+            pltpu.SMEM((CHUNK,), jnp.float32),
+            pltpu.SemaphoreType.DMA((2,)),
+        ],
+        out_shape=[
+            jax.ShapeDtypeStruct((nx if dx is None else ny, half, 128), jnp.float32)
+            for _, dy, dx in jobs
+        ],
+        compiler_params=pltpu.CompilerParams(vmem_limit_bytes=24 * 1024 * 1024),
+        cost_estimate=pl.CostEstimate(
+            flops=0, bytes_accessed=len(jobs) * 5 * 1024 * 1024, transcendentals=0
         ),
-        out_shape=jax.ShapeDtypeStruct((steps, columns, 128), jnp.float32),
-        compiler_params=pltpu.CompilerParams(vmem_limit_bytes=32 * 1024 * 1024),
-    )(order, counts, rows, weights, lists, table)
+    )(place, counts, near_rows, near_weights, rows, weights, lists, table)
 
 
 def moved(value, axis, by):
     count = lax.axis_size(axis)
     return lax.ppermute(value, axis, [(i, (i + by) % count) for i in range(count)])
-
-
-def ring_sum(get, axis):
-    far = get(2)
-    half = far.shape[0] // 2
-    up = moved(far[:half], axis, 1)
-    down = moved(far[half:], axis, -1)
-    near_up, near_down = get(1), get(3)
-    near_up = jnp.concatenate([near_up[:half] + up, near_up[half:]], 0)
-    near_down = jnp.concatenate([near_down[:half], near_down[half:] + down], 0)
-    return get(0) + moved(near_up, axis, 1) + moved(near_down, axis, -1)
 
 
 def shifted(shard, axis, by):
@@ -255,21 +296,30 @@
     columns, top = weights.shape[1:]
     table = lax.all_gather(model, ("z", "c"), axis=0, tiled=True).reshape(-1, block)
     classes = ny * nx
-    cap = min(columns * top, nz * nc * 128)
+    cap = min(columns * top, nz * nc * 128) + CHUNK
     sizes = (nz, nx, nc, quarter, classes, cap)
     lists = build_lists(sizes, block_owner_rank[0].T, source_slot[0].T, weights[0].T)
     lists = lax.all_to_all(lists, ("y", "x"), split_axis=0, concat_axis=0, tiled=True)
-    lane_rows = cap // 128
+    lane_rows, near = cap // 128, NEAR // 128
     rows = lists[:, :lane_rows].reshape(classes, 1, cap).astype(jnp.int32)
     factors = lists[:, lane_rows : 2 * lane_rows].reshape(classes, 1, cap)
-    counts = lists[:, FIELDS * lane_rows, 0].astype(jnp.int32)
-    step = jnp.arange(classes, dtype=jnp.int32)
-    order = (lax.axis_index("y") + step // nx) % ny * nx + (lax.axis_index("x") + step % nx) % nx
-    sums = partial_sums(cap, columns, order, counts, rows, factors, lists, table)
-    sums = sums.reshape(ny, nx, columns, block)
-    half = columns // 2
-    first = ring_sum(lambda d: sums[d, :, :half], "y")
-    second = ring_sum(lambda d: sums[:, d, half:], "x")
+    near_rows = lists[:, :near].reshape(-1).astype(jnp.int32)
+    near_factors = lists[:, lane_rows : lane_rows + near].reshape(-1)
+    counts = lists[:, FIELDS * lane_rows : FIELDS * lane_rows + 2, 0].T.reshape(-1).astype(jnp.int32)
+    place = jnp.stack([lax.axis_index("y"), lax.axis_index("x")]).astype(jnp.int32)
+
+    def sums(*jobs):
+        return partial_sums(
+            jobs, (ny, nx, cap), columns // 2, place, counts, near_rows, near_factors, rows, factors, lists, table
+        )
+
+    a2, b2 = sums((0, 2, None), (1, None, 2))
+    a1, a3, b1, b3 = sums((0, 1, None), (0, 3, None), (1, None, 1), (1, None, 3))
+    a0, b0 = sums((0, 0, None), (1, None, 0))
+    from_a = [moved(a2, "y", 2), moved(a1, "y", 1), moved(a3, "y", 3)]
+    from_b = [moved(b2, "x", 2), moved(b1, "x", 1), moved(b3, "x", 3)]
+    first = [a0[d] + from_a[0][d] + from_a[1][d] + from_a[2][d] for d in range(nx)]
+    second = [b0[d] + from_b[0][d] + from_b[1][d] + from_b[2][d] for d in range(ny)]
     first = sum((moved(first[d], "x", d) for d in (2, 1, 3)), first[0])
     second = sum((moved(second[d], "y", d) for d in (2, 1, 3)), second[0])
     return jnp.concatenate([first, second], 0)

time: 135 us -> 136 us (level)
  waiting for transfers between devices: 53.7 us -> 43.9 us
  starting transfers between devices: 32.9 us -> 40.9 us
  Pallas kernels: 17.9 us -> 22.2 us
    ppermute x14 -> x12, waiting for transfers between devices: 25.3 us -> 14.9 us  [moved(): lax.ppermute(value, axis, [(i, (i + by) % count) for i in range(count)])]
    ppermute x14 -> x12, starting transfers between devices: 16.1 us -> 24.1 us  [moved(): lax.ppermute(value, axis, [(i, (i + by) % count) for i in range(count)])]
    pallas_call x1 -> x3, Pallas kernels: 15.1 us -> 19.4 us  [partial_sums(): pl.pallas_call(functools.partial(partials_kernel, jobs, sizes), in_specs=...]
    unnamed x15 -> x14, local copies, waits for them, and re-layouts: 7.5 us -> 5.53 us
  transfers between devices with their start and end apart: 19 -> 17, of which waited for: 15 -> 10; matrix products, arithmetic and copies ran while one was open for 4% -> 4% of each run, Pallas kernels for 2% -> 10%
where the time goes in v2:
time: 136 us; the launch traced here: 135 us
  waiting for transfers between devices  43.9 us (32%)
  starting transfers between devices  40.9 us (30%)
  Pallas kernels  22.2 us (16%)
  between operations  14.4 us (11%)
  local copies, waits for them, and re-layouts  8.02 us (6%)
  other arithmetic  5.51 us (4%)
    ppermute x12, starting transfers between devices, moved(): lax.ppermute(value, axis, [(i, (i + by) % count) for i in range(count)])  24.1 us
    pallas_call x3, Pallas kernels, partial_sums(): pl.pallas_call(functools.partial(partials_kernel, jobs, sizes), in_specs=...  19.4 us
    all_gather x1, waiting for transfers between devices, log_conductivity(): lax.all_gather(model, ('z', 'c'), axis=0, tiled=True).reshape(-1, block)  19 us
    ppermute x12, waiting for transfers between devices, moved(): lax.ppermute(value, axis, [(i, (i + by) % count) for i in range(count)])  14.9 us
    ppermute x3, starting transfers between devices, shifted(): return lax.ppermute(shard, axis, pairs)  9.59 us
    ppermute x3, waiting for transfers between devices, shifted(): return lax.ppermute(shard, axis, pairs)  9.29 us
    all_to_all x1, starting transfers between devices, log_conductivity(): lax.all_to_all(lists, ('y', 'x'), split_axis=0, concat_axis=0, tiled=True)  7.18 us
    unnamed x14, local copies, waits for them, and re-layouts  5.53 us
  transfers between devices with their start and end apart: 17, of which 10 were waited for; matrix products, arithmetic and copies ran while one was open for 4% of the time, Pallas kernels for 10%

profile of v2, /device:TPU:56, one launch (start us, length us, event | category | flops | bytes accessed | tf_op | source)
XLA Modules:
  0.0 134.9 jit_solution(4234626119695793222)
XLA Ops:
  6.5 0.7 all-gather.2.cloned.1.call-update
  7.3 0.7 copy-done.1
  8.0 0.7 copy-done.2
  8.7 0.7 copy-done.3
  9.4 2.8 %shard_map.73 = f32[16,56,128]{2,1,0:T(8,128)} custom-call(s32[8,512]{1,0:T(8,128)S(1)} %bitcast.119, s32[8,512]{1,0:T(8,128)S(1)} %bitcast.120, f32[8,512]{1,0:T(8,128)S(1)} %bitcast.121), custom_call_target="tpu_custom_call" | custom-call | tf_op jit(solution)/shard_map/pallas_call | solution.py:125
  12.3 7.2 %all-to-all-start = ((f32[16,56,128]{2,1,0:T(8,128)}), f32[16,56,128]{2,1,0:T(8,128)S(1)}, u32[]{:S(2)}, u32[]{:S(2)}) async-start(f32[16,56,128]{2,1,0:T(8,128)} %shard_map.73), calls=%async_computation | async-start | bytes 917504 | tf_op jit(solution)/shard_map/all_to_all | solution.py:302
  19.4 1.0 fusion.40
  20.5 1.9 %collective-permute-start = (f32[2,3,1,64,128]{4,3,2,1,0:T(8,128)S(1)}, f32[2,3,1,64,128]{4,3,2,1,0:T(8,128)S(1)}, u32[]{:S(2)}, u32[]{:S(2)}) collective-permute-start(f32[2,3,1,64,128]{4,3,2,1,0:T(8,128)S(1)} %get-tuple-element.32), channel_id=1, source_target_pairs={{0,1},{1,2},{2,3},{3,4},{4,5},{5,6},{6,7},{7,8},{8,9},{9,10},{10,1... | collective-permute-start | bytes 589832 | tf_op jit(solution)/shard_map/ppermute | solution.py:246
  22.4 5.8 %collective-permute-start.1 = (f32[2,3,1,64,128]{4,3,2,1,0:T(8,128)S(1)}, f32[2,3,1,64,128]{4,3,2,1,0:T(8,128)S(1)}, u32[]{:S(2)}, u32[]{:S(2)}) collective-permute-start(f32[2,3,1,64,128]{4,3,2,1,0:T(8,128)S(1)} %get-tuple-element.33), channel_id=1, source_target_pairs={{1,0},{2,1},{3,2},{4,3},{5,4},{6,5},{7,6},{8,7},{9,8},{10,9},{11,1... | collective-permute-start | bytes 589832 | tf_op jit(solution)/shard_map/ppermute | solution.py:246
  28.9 1.9 %collective-permute-done = f32[2,3,1,64,128]{4,3,2,1,0:T(8,128)S(1)} collective-permute-done((f32[2,3,1,64,128]{4,3,2,1,0:T(8,128)S(1)}, f32[2,3,1,64,128]{4,3,2,1,0:T(8,128)S(1)}, u32[]{:S(2)}, u32[]{:S(2)}) %collective-permute-start) | collective-permute-done | bytes 196640 | tf_op jit(solution)/shard_map/ppermute | solution.py:246
  30.8 2.2 %collective-permute-done.1 = f32[2,3,1,64,128]{4,3,2,1,0:T(8,128)S(1)} collective-permute-done((f32[2,3,1,64,128]{4,3,2,1,0:T(8,128)S(1)}, f32[2,3,1,64,128]{4,3,2,1,0:T(8,128)S(1)}, u32[]{:S(2)}, u32[]{:S(2)}) %collective-permute-start.1) | collective-permute-done | bytes 196640 | tf_op jit(solution)/shard_map/ppermute | solution.py:246
  33.0 1.5 %pad_maximum_fusion = f32[2,3,10,64,128]{4,3,2,1,0:T(8,128)} fusion(f32[2,3,1,64,128]{4,3,2,1,0:T(8,128)S(1)} %collective-permute-done.1, f32[2,3,8,64,128]{4,3,2,1,0:T(8,128)S(1)} %bitcast.132, f32[2,3,1,64,128]{4,3,2,1,0:T(8,128)S(1)} %collective-permute-done), kind=kLoop, calls=%fused_computation | loop fusion | flops 983040 | bytes 3932160 | tf_op jit(solution)/shard_map/concatenate | solution.py:255
  35.0 19.0 %all-gather.2.cloned.1.call-done = f32[8192,1,128]{2,0,1:T(8,128)} async-done(((f32[512,1,128]{2,0,1:T(8,128)}), f32[8192,1,128]{2,0,1:T(8,128)}) %all-gather.2.cloned.1.call-update) | async-done | bytes 4194320 | tf_op jit(solution)/shard_map/all_gather | solution.py:297
  54.0 2.2 %copy-done = f32[8192,1,128]{2,0,1:T(8,128)S(1)} copy-done((f32[8192,1,128]{2,0,1:T(8,128)S(1)}, f32[8192,1,128]{2,0,1:T(8,128)}, u32[]{:S(2)}) %copy-start) | copy-done | bytes 4194328
  56.2 8.9 %shard_map.76 = (f32[4,256,128]{2,1,0:T(8,128)S(1)}, f32[4,256,128]{2,1,0:T(8,128)S(1)}, f32[4,256,128]{2,1,0:T(8,128)S(1)}, f32[4,256,128]{2,1,0:T(8,128)S(1)}) custom-call(s32[2]{0:T(128)S(1)} %pad_add_fusion.place_ref, s32[32]{0:T(128)S(1)} %convert_element_type.22.count_ref, s32[8192]{0:T(1024)S(1)} %bitcast.116, f32[8192]{0:T(1024)S(1)} %bitcast.113, ...), custom_call_target="tpu_custom_call" | custom-call | bytes 20971520 | tf_op jit(solution)/shard_map/pallas_call | solution.py:217
  65.1 0.5 collective-permute-start.3
  65.6 0.2 slice_bitcast_fusion.2
  65.9 0.2 slice.353
  66.2 0.2 slice.360
  66.4 1.7 %collective-permute-start.4 = (f32[4,256,128]{2,1,0:T(8,128)S(1)}, f32[4,256,128]{2,1,0:T(8,128)S(1)}, u32[]{:S(2)}, u32[]{:S(2)}) collective-permute-start(f32[4,256,128]{2,1,0:T(8,128)S(1)} %get-tuple-element.16), channel_id=1, source_target_pairs={{0,192},{64,0},{128,64},{192,128},{1,193},{65,1},{129,65},{193,129... | collective-permute-start | bytes 1572872 | tf_op jit(solution)/shard_map/ppermute | solution.py:240
  68.0 5.3 %shard_map.75 = (f32[4,256,128]{2,1,0:T(8,128)S(1)}, f32[4,256,128]{2,1,0:T(8,128)S(1)}) custom-call(s32[2]{0:T(128)S(1)} %pad_add_fusion.place_ref, s32[32]{0:T(128)S(1)} %convert_element_type.22.count_ref, s32[8192]{0:T(1024)S(1)} %bitcast.117, f32[8192]{0:T(1024)S(1)} %bitcast.114, s32[16,1,2304]{2,1,0:T(1,128)S(1)} %convert_element_type.27.rows_far, ...), custom_call_target="tpu_custom_call" | custom-call | bytes 10485760 | tf_op jit(solution)/shard_map/pallas_call | solution.py:217
  73.3 1.5 %collective-permute-start.2 = (f32[4,256,128]{2,1,0:T(8,128)S(1)}, f32[4,256,128]{2,1,0:T(8,128)S(1)}, u32[]{:S(2)}, u32[]{:S(2)}) collective-permute-start(f32[4,256,128]{2,1,0:T(8,128)S(1)} %get-tuple-element.14), channel_id=1, source_target_pairs={{0,128},{64,192},{128,0},{192,64},{1,129},{65,193},{129,1},{193,65... | collective-permute-start | bytes 1572872 | tf_op jit(solution)/shard_map/ppermute | solution.py:240
  74.8 0.5 fusion.5
  75.5 1.8 %collective-permute-start.10 = (f32[4,256,128]{2,1,0:T(8,128)S(1)}, f32[4,256,128]{2,1,0:T(8,128)S(1)}, u32[]{:S(2)}, u32[]{:S(2)}) collective-permute-start(f32[4,256,128]{2,1,0:T(8,128)S(1)} %get-tuple-element.20), channel_id=1, source_target_pairs={{0,6},{2,0},{4,2},{6,4},{1,7},{3,1},{5,3},{7,5},{8,14},{10,8},{12,... | collective-permute-start | bytes 1572872 | tf_op jit(solution)/shard_map/ppermute | solution.py:240
  77.3 0.3 collective-permute-start.9
  77.6 2.3 %collective-permute-done.3 = f32[4,256,128]{2,1,0:T(8,128)S(1)} collective-permute-done((f32[4,256,128]{2,1,0:T(8,128)S(1)}, f32[4,256,128]{2,1,0:T(8,128)S(1)}, u32[]{:S(2)}, u32[]{:S(2)}) %collective-permute-start.3) | collective-permute-done | bytes 524320 | tf_op jit(solution)/shard_map/ppermute | solution.py:240
  80.0 1.8 %collective-permute-start.8 = (f32[4,256,128]{2,1,0:T(8,128)S(1)}, f32[4,256,128]{2,1,0:T(8,128)S(1)}, u32[]{:S(2)}, u32[]{:S(2)}) collective-permute-start(f32[4,256,128]{2,1,0:T(8,128)S(1)} %get-tuple-element.18), channel_id=1, source_target_pairs={{0,4},{2,6},{4,0},{6,2},{1,5},{3,7},{5,1},{7,3},{8,12},{10,14},{12... | collective-permute-start | bytes 1572872 | tf_op jit(solution)/shard_map/ppermute | solution.py:240
  81.8 0.6 subtract_bitcast_fusion
  82.4 0.2 pad_maximum_fusion.1
  82.5 5.2 %shard_map.74 = (f32[4,256,128]{2,1,0:T(8,128)S(1)}, f32[4,256,128]{2,1,0:T(8,128)S(1)}) custom-call(s32[2]{0:T(128)S(1)} %pad_add_fusion.place_ref, s32[32]{0:T(128)S(1)} %convert_element_type.22.count_ref, s32[8192]{0:T(1024)S(1)} %bitcast.118, f32[8192]{0:T(1024)S(1)} %bitcast.115, s32[16,1,2304]{2,1,0:T(1,128)S(1)} %convert_element_type.27.rows_far, ...), custom_call_target="tpu_custom_call" | custom-call | bytes 10485760 | tf_op jit(solution)/shard_map/pallas_call | solution.py:217
  87.7 4.9 %collective-permute-done.4 = f32[4,256,128]{2,1,0:T(8,128)S(1)} collective-permute-done((f32[4,256,128]{2,1,0:T(8,128)S(1)}, f32[4,256,128]{2,1,0:T(8,128)S(1)}, u32[]{:S(2)}, u32[]{:S(2)}) %collective-permute-start.4) | collective-permute-done | bytes 524320 | tf_op jit(solution)/shard_map/ppermute | solution.py:240
  92.7 2.0 %collective-permute-start.5 = (f32[256,128]{1,0:T(8,128)S(1)}, f32[256,128]{1,0:T(8,128)S(1)}, u32[]{:S(2)}, u32[]{:S(2)}) collective-permute-start(f32[256,128]{1,0:T(8,128)S(1)} %get-tuple-element.23), channel_id=1, source_target_pairs={{0,4},{2,6},{4,0},{6,2},{1,5},{3,7},{5,1},{7,3},{8,12},{10,14},{12... | collective-permute-start | bytes 393224 | tf_op jit(solution)/shard_map/ppermute | solution.py:240
  94.7 1.1 collective-permute-start.6
  95.9 8.4 %collective-permute-start.7 = (f32[256,128]{1,0:T(8,128)S(1)}, f32[256,128]{1,0:T(8,128)S(1)}, u32[]{:S(2)}, u32[]{:S(2)}) collective-permute-start(f32[256,128]{1,0:T(8,128)S(1)} %get-tuple-element.24), channel_id=1, source_target_pairs={{0,6},{2,0},{4,2},{6,4},{1,7},{3,1},{5,3},{7,5},{8,14},{10,8},{12,... | collective-permute-start | bytes 393224 | tf_op jit(solution)/shard_map/ppermute | solution.py:240
  104.3 2.0 %collective-permute-done.9 = f32[4,256,128]{2,1,0:T(8,128)S(1)} collective-permute-done((f32[4,256,128]{2,1,0:T(8,128)S(1)}, f32[4,256,128]{2,1,0:T(8,128)S(1)}, u32[]{:S(2)}, u32[]{:S(2)}) %collective-permute-start.9) | collective-permute-done | bytes 524320 | tf_op jit(solution)/shard_map/ppermute | solution.py:240
  106.3 3.0 %collective-permute-start.11 = (f32[256,128]{1,0:T(8,128)S(1)}, f32[256,128]{1,0:T(8,128)S(1)}, u32[]{:S(2)}, u32[]{:S(2)}) collective-permute-start(f32[256,128]{1,0:T(8,128)S(1)} %get-tuple-element.26), channel_id=1, source_target_pairs={{0,128},{64,192},{128,0},{192,64},{1,129},{65,193},{129,1},{193,65... | collective-permute-start | bytes 393224 | tf_op jit(solution)/shard_map/ppermute | solution.py:240
  109.3 1.6 %collective-permute-start.12 = (f32[256,128]{1,0:T(8,128)S(1)}, f32[256,128]{1,0:T(8,128)S(1)}, u32[]{:S(2)}, u32[]{:S(2)}) collective-permute-start(f32[256,128]{1,0:T(8,128)S(1)} %get-tuple-element.28), channel_id=1, source_target_pairs={{0,64},{64,128},{128,192},{192,0},{1,65},{65,129},{129,193},{193,1... | collective-permute-start | bytes 393224 | tf_op jit(solution)/shard_map/ppermute | solution.py:240
  110.8 0.5 collective-permute-start.13
  111.4 1.5 %collective-permute-done.11 = f32[256,128]{1,0:T(8,128)S(1)} collective-permute-done((f32[256,128]{1,0:T(8,128)S(1)}, f32[256,128]{1,0:T(8,128)S(1)}, u32[]{:S(2)}, u32[]{:S(2)}) %collective-permute-start.11) | collective-permute-done | bytes 131104 | tf_op jit(solution)/shard_map/ppermute | solution.py:240
  112.9 1.4 %collective-permute-done.12 = f32[256,128]{1,0:T(8,128)S(1)} collective-permute-done((f32[256,128]{1,0:T(8,128)S(1)}, f32[256,128]{1,0:T(8,128)S(1)}, u32[]{:S(2)}, u32[]{:S(2)}) %collective-permute-start.12) | collective-permute-done | bytes 131104 | tf_op jit(solution)/shard_map/ppermute | solution.py:240
  114.3 2.8 %collective-permute-done.13 = f32[256,128]{1,0:T(8,128)S(1)} collective-permute-done((f32[256,128]{1,0:T(8,128)S(1)}, f32[256,128]{1,0:T(8,128)S(1)}, u32[]{:S(2)}, u32[]{:S(2)}) %collective-permute-start.13) | collective-permute-done | bytes 131104 | tf_op jit(solution)/shard_map/ppermute | solution.py:240
  117.3 1.9 %collective-permute-start.14 = (f32[1,64,128]{2,1,0:T(8,128)S(1)}, f32[1,64,128]{2,1,0:T(8,128)S(1)}, u32[]{:S(2)}, u32[]{:S(2)}) collective-permute-start(f32[1,64,128]{2,1,0:T(8,128)S(1)} %slice_bitcast_fusion.5), channel_id=1, source_target_pairs={{0,1},{1,2},{2,3},{3,4},{4,5},{5,6},{6,7},{7,8},{8,9},{9,10},{10,1... | collective-permute-start | bytes 98312 | tf_op jit(solution)/shard_map/ppermute | solution.py:246
  119.2 0.1 fusion.22
  119.4 5.3 %collective-permute-done.14 = f32[1,64,128]{2,1,0:T(8,128)S(1)} collective-permute-done((f32[1,64,128]{2,1,0:T(8,128)S(1)}, f32[1,64,128]{2,1,0:T(8,128)S(1)}, u32[]{:S(2)}, u32[]{:S(2)}) %collective-permute-start.14) | collective-permute-done | bytes 32800 | tf_op jit(solution)/shard_map/ppermute | solution.py:246
  124.8 0.2 fusion.13
  125.0 1.2 copy-done.6
  126.2 0.6 fusion.1
  126.8 1.2 maximum_bitcast_fusion
  (49 shorter events, 1.5 us)
Async XLA Ops:
  6.5 47.5 %all-gather.2.cloned.1.call-start = ((), (), s32[]{:S(2)}) async-start(), calls=%async_computation.1 | async-start | bytes 4456448 | tf_op jit(solution)/shard_map/all_gather | solution.py:297
  7.3 0.7 copy-start.1
  8.0 0.7 copy-start.2
  8.7 0.7 copy-start.3
  9.4 23.5 %copy-start.4 = (f32[1,2,3,8,64,128]{5,4,3,2,1,0:T(8,128)S(1)}, f32[1,2,3,8,64,128]{5,4,3,2,1,0:T(8,128)}, u32[]{:S(2)}) copy-start(f32[1,2,3,8,64,128]{5,4,3,2,1,0:T(8,128)} %param.11) | copy-start | bytes 4718596
  12.3 22.2 %all-to-all-start = ((f32[16,56,128]{2,1,0:T(8,128)}), f32[16,56,128]{2,1,0:T(8,128)S(1)}, u32[]{:S(2)}, u32[]{:S(2)}) async-start(f32[16,56,128]{2,1,0:T(8,128)} %shard_map.73), calls=%async_computation | async-start | bytes 917504 | tf_op jit(solution)/shard_map/all_to_all | solution.py:302
  20.5 10.3 %collective-permute-start = (f32[2,3,1,64,128]{4,3,2,1,0:T(8,128)S(1)}, f32[2,3,1,64,128]{4,3,2,1,0:T(8,128)S(1)}, u32[]{:S(2)}, u32[]{:S(2)}) collective-permute-start(f32[2,3,1,64,128]{4,3,2,1,0:T(8,128)S(1)} %get-tuple-element.32), channel_id=1, source_target_pairs={{0,1},{1,2},{2,3},{3,4},{4,5},{5,6},{6,7},{7,8},{8,9},{9,10},{10,1... | collective-permute-start | bytes 589832 | tf_op jit(solution)/shard_map/ppermute | solution.py:246
  22.4 10.5 %collective-permute-start.1 = (f32[2,3,1,64,128]{4,3,2,1,0:T(8,128)S(1)}, f32[2,3,1,64,128]{4,3,2,1,0:T(8,128)S(1)}, u32[]{:S(2)}, u32[]{:S(2)}) collective-permute-start(f32[2,3,1,64,128]{4,3,2,1,0:T(8,128)S(1)} %get-tuple-element.33), channel_id=1, source_target_pairs={{1,0},{2,1},{3,2},{4,3},{5,4},{6,5},{7,6},{8,7},{9,8},{10,9},{11,1... | collective-permute-start | bytes 589832 | tf_op jit(solution)/shard_map/ppermute | solution.py:246
  54.0 2.2 %copy-start = (f32[8192,1,128]{2,0,1:T(8,128)S(1)}, f32[8192,1,128]{2,0,1:T(8,128)}, u32[]{:S(2)}) copy-start(f32[8192,1,128]{2,0,1:T(8,128)} %all-gather.2.cloned.1.call-done) | copy-start | bytes 12582916
  56.2 9.4 %copy-start.5 = (f32[2,3,10,64,128]{4,3,2,1,0:T(8,128)S(1)}, f32[2,3,10,64,128]{4,3,2,1,0:T(8,128)}, u32[]{:S(2)}) copy-start(f32[2,3,10,64,128]{4,3,2,1,0:T(8,128)} %pad_maximum_fusion) | copy-start | bytes 5898244
  65.1 14.9 %collective-permute-start.3 = (f32[4,256,128]{2,1,0:T(8,128)S(1)}, f32[4,256,128]{2,1,0:T(8,128)S(1)}, u32[]{:S(2)}, u32[]{:S(2)}) collective-permute-start(f32[4,256,128]{2,1,0:T(8,128)S(1)} %get-tuple-element.15), channel_id=1, source_target_pairs={{0,64},{64,128},{128,192},{192,0},{1,65},{65,129},{129,193},{193,1... | collective-permute-start | bytes 1572872 | tf_op jit(solution)/shard_map/ppermute | solution.py:240
  66.4 26.3 %collective-permute-start.4 = (f32[4,256,128]{2,1,0:T(8,128)S(1)}, f32[4,256,128]{2,1,0:T(8,128)S(1)}, u32[]{:S(2)}, u32[]{:S(2)}) collective-permute-start(f32[4,256,128]{2,1,0:T(8,128)S(1)} %get-tuple-element.16), channel_id=1, source_target_pairs={{0,192},{64,0},{128,64},{192,128},{1,193},{65,1},{129,65},{193,129... | collective-permute-start | bytes 1572872 | tf_op jit(solution)/shard_map/ppermute | solution.py:240
  73.3 19.3 %collective-permute-start.2 = (f32[4,256,128]{2,1,0:T(8,128)S(1)}, f32[4,256,128]{2,1,0:T(8,128)S(1)}, u32[]{:S(2)}, u32[]{:S(2)}) collective-permute-start(f32[4,256,128]{2,1,0:T(8,128)S(1)} %get-tuple-element.14), channel_id=1, source_target_pairs={{0,128},{64,192},{128,0},{192,64},{1,129},{65,193},{129,1},{193,65... | collective-permute-start | bytes 1572872 | tf_op jit(solution)/shard_map/ppermute | solution.py:240
  75.5 20.4 %collective-permute-start.10 = (f32[4,256,128]{2,1,0:T(8,128)S(1)}, f32[4,256,128]{2,1,0:T(8,128)S(1)}, u32[]{:S(2)}, u32[]{:S(2)}) collective-permute-start(f32[4,256,128]{2,1,0:T(8,128)S(1)} %get-tuple-element.20), channel_id=1, source_target_pairs={{0,6},{2,0},{4,2},{6,4},{1,7},{3,1},{5,3},{7,5},{8,14},{10,8},{12,... | collective-permute-start | bytes 1572872 | tf_op jit(solution)/shard_map/ppermute | solution.py:240
  77.3 28.9 %collective-permute-start.9 = (f32[4,256,128]{2,1,0:T(8,128)S(1)}, f32[4,256,128]{2,1,0:T(8,128)S(1)}, u32[]{:S(2)}, u32[]{:S(2)}) collective-permute-start(f32[4,256,128]{2,1,0:T(8,128)S(1)} %get-tuple-element.19), channel_id=1, source_target_pairs={{0,2},{2,4},{4,6},{6,0},{1,3},{3,5},{5,7},{7,1},{8,10},{10,12},{12... | collective-permute-start | bytes 1572872 | tf_op jit(solution)/shard_map/ppermute | solution.py:240
  80.0 26.3 %collective-permute-start.8 = (f32[4,256,128]{2,1,0:T(8,128)S(1)}, f32[4,256,128]{2,1,0:T(8,128)S(1)}, u32[]{:S(2)}, u32[]{:S(2)}) collective-permute-start(f32[4,256,128]{2,1,0:T(8,128)S(1)} %get-tuple-element.18), channel_id=1, source_target_pairs={{0,4},{2,6},{4,0},{6,2},{1,5},{3,7},{5,1},{7,3},{8,12},{10,14},{12... | collective-permute-start | bytes 1572872 | tf_op jit(solution)/shard_map/ppermute | solution.py:240
  92.7 18.1 %collective-permute-start.5 = (f32[256,128]{1,0:T(8,128)S(1)}, f32[256,128]{1,0:T(8,128)S(1)}, u32[]{:S(2)}, u32[]{:S(2)}) collective-permute-start(f32[256,128]{1,0:T(8,128)S(1)} %get-tuple-element.23), channel_id=1, source_target_pairs={{0,4},{2,6},{4,0},{6,2},{1,5},{3,7},{5,1},{7,3},{8,12},{10,14},{12... | collective-permute-start | bytes 393224 | tf_op jit(solution)/shard_map/ppermute | solution.py:240
  94.7 16.6 %collective-permute-start.6 = (f32[256,128]{1,0:T(8,128)S(1)}, f32[256,128]{1,0:T(8,128)S(1)}, u32[]{:S(2)}, u32[]{:S(2)}) collective-permute-start(f32[256,128]{1,0:T(8,128)S(1)} %get-tuple-element.25), channel_id=1, source_target_pairs={{0,2},{2,4},{4,6},{6,0},{1,3},{3,5},{5,7},{7,1},{8,10},{10,12},{12... | collective-permute-start | bytes 393224 | tf_op jit(solution)/shard_map/ppermute | solution.py:240
  95.9 15.5 %collective-permute-start.7 = (f32[256,128]{1,0:T(8,128)S(1)}, f32[256,128]{1,0:T(8,128)S(1)}, u32[]{:S(2)}, u32[]{:S(2)}) collective-permute-start(f32[256,128]{1,0:T(8,128)S(1)} %get-tuple-element.24), channel_id=1, source_target_pairs={{0,6},{2,0},{4,2},{6,4},{1,7},{3,1},{5,3},{7,5},{8,14},{10,8},{12,... | collective-permute-start | bytes 393224 | tf_op jit(solution)/shard_map/ppermute | solution.py:240
  106.3 6.6 %collective-permute-start.11 = (f32[256,128]{1,0:T(8,128)S(1)}, f32[256,128]{1,0:T(8,128)S(1)}, u32[]{:S(2)}, u32[]{:S(2)}) collective-permute-start(f32[256,128]{1,0:T(8,128)S(1)} %get-tuple-element.26), channel_id=1, source_target_pairs={{0,128},{64,192},{128,0},{192,64},{1,129},{65,193},{129,1},{193,65... | collective-permute-start | bytes 393224 | tf_op jit(solution)/shard_map/ppermute | solution.py:240
  109.3 5.0 %collective-permute-start.12 = (f32[256,128]{1,0:T(8,128)S(1)}, f32[256,128]{1,0:T(8,128)S(1)}, u32[]{:S(2)}, u32[]{:S(2)}) collective-permute-start(f32[256,128]{1,0:T(8,128)S(1)} %get-tuple-element.28), channel_id=1, source_target_pairs={{0,64},{64,128},{128,192},{192,0},{1,65},{65,129},{129,193},{193,1... | collective-permute-start | bytes 393224 | tf_op jit(solution)/shard_map/ppermute | solution.py:240
  110.8 6.2 %collective-permute-start.13 = (f32[256,128]{1,0:T(8,128)S(1)}, f32[256,128]{1,0:T(8,128)S(1)}, u32[]{:S(2)}, u32[]{:S(2)}) collective-permute-start(f32[256,128]{1,0:T(8,128)S(1)} %get-tuple-element.27), channel_id=1, source_target_pairs={{0,192},{64,0},{128,64},{192,128},{1,193},{65,1},{129,65},{193,129... | collective-permute-start | bytes 393224 | tf_op jit(solution)/shard_map/ppermute | solution.py:240
  117.3 7.3 %collective-permute-start.14 = (f32[1,64,128]{2,1,0:T(8,128)S(1)}, f32[1,64,128]{2,1,0:T(8,128)S(1)}, u32[]{:S(2)}, u32[]{:S(2)}) collective-permute-start(f32[1,64,128]{2,1,0:T(8,128)S(1)} %slice_bitcast_fusion.5), channel_id=1, source_target_pairs={{0,1},{1,2},{2,3},{3,4},{4,5},{5,6},{6,7},{7,8},{8,9},{9,10},{10,1... | collective-permute-start | bytes 98312 | tf_op jit(solution)/shard_map/ppermute | solution.py:246
  124.8 1.4 %copy-start.6 = (f32[1,2,3,8,64,128]{5,4,3,2,1,0:T(8,128)S(1)}, f32[1,2,3,8,64,128]{5,4,3,2,1,0:T(8,128)}, u32[]{:S(2)}) copy-start(f32[1,2,3,8,64,128]{5,4,3,2,1,0:T(8,128)} %param.12) | copy-start | bytes 4718596
Sparse Core Ops, SparseCore 0:
  9.2 44.7 all-gather.1

commit v3 on v2

v3 whole, which is shorter than its diff:
```python
import functools

import jax
import jax.numpy as jnp
from jax import lax
from jax.experimental import pallas as pl
from jax.experimental.pallas import tpu as pltpu
from jax.sharding import Mesh, PartitionSpec as P

CHUNK = 256
FIELDS = 3
STEP = 16
NEAR = 512


def shift_of(count):
    return (count - 1).bit_length()


def lists_kernel(sizes, here_ref, owner_far, slot_far, weight_far, after_ref, out_ref, values, *rest):
    nz, nx, nc, quarter, classes, cap = sizes
    top, columns = owner_far.shape
    owner_ref, slot_ref, weight_ref, sems = rest
    copies = [
        pltpu.make_async_copy(far, near, sems.at[i])
        for i, (far, near) in enumerate(
            ((owner_far, owner_ref), (slot_far, slot_ref), (weight_far, weight_ref))
        )
    ]
    for copy in copies:
        copy.start()
    for copy in copies:
        copy.wait()
    owner, slot, weight = owner_ref[...], slot_ref[...], weight_ref[...]
    bits_c, bits_x, bits_q = shift_of(nc), shift_of(nx), shift_of(quarter)
    kind = (slot >> bits_q) * nx + ((owner >> bits_c) & (nx - 1))
    layer = (((owner >> (bits_c + bits_x)) - here_ref[0]) * (2 * here_ref[1] - 1)) & (nz - 1)
    core = (owner - here_ref[1]) & (nc - 1)
    row = (core * nz + layer) * quarter + (slot & (quarter - 1))
    column = lax.broadcasted_iota(jnp.int32, (top, columns), 1)
    as_float = lambda value: value.astype(jnp.float32)
    rounded = lambda value: value.astype(jnp.bfloat16).astype(jnp.float32)
    high = rounded(weight)
    middle = rounded(weight - high)
    parts = [
        as_float(row >> 7),
        as_float(row & 127),
        as_float(column >> 8),
        as_float(column & 255),
        high,
        middle,
        weight - high - middle,
        jnp.zeros((top, columns), jnp.float32),
    ]
    iota_kind = lax.broadcasted_iota(jnp.int32, (classes, columns), 0)
    marks = []
    for k in range(top):
        mark = iota_kind == kind[k : k + 1, :]
        marks.append(jnp.where(mark, 1.0, 0.0))
        stacked = [jnp.where(mark, part[k : k + 1, :], 0.0) for part in parts]
        values[k] = jnp.concatenate(stacked, 0).astype(jnp.bfloat16)
    marks = jnp.concatenate(marks, 0)
    marks_low = marks.astype(jnp.bfloat16)
    rows = top * classes
    half = columns // 2
    column_i = lax.broadcasted_iota(jnp.int32, (columns, columns), 0)
    column_j = lax.broadcasted_iota(jnp.int32, (columns, columns), 1)
    before = (column_i < column_j) & ((column_i >= half) == (column_j >= half))
    prefix = jnp.dot(
        marks_low,
        jnp.where(before, 1.0, 0.0).astype(jnp.bfloat16),
        preferred_element_type=jnp.float32,
    )
    row_i = lax.broadcasted_iota(jnp.int32, (rows, rows), 0)
    row_j = lax.broadcasted_iota(jnp.int32, (rows, rows), 1)
    earlier = (row_j < row_i) & ((row_i & (classes - 1)) == (row_j & (classes - 1)))
    above = jnp.dot(
        jnp.where(earlier, 1.0, 0.0).astype(jnp.bfloat16),
        marks_low,
        preferred_element_type=jnp.float32,
    )
    over = lambda value: jnp.sum(value, axis=1, keepdims=True)

    def per_kind(value):
        sums = over(value)
        total = sums[:classes]
        for k in range(1, top):
            total = total + sums[k * classes : (k + 1) * classes]
        return total

    count_a, count_b = per_kind(marks[:, :half]), per_kind(marks[:, half:])
    begin_b = ((count_a.astype(jnp.int32) + 127) >> 7) << 7
    most = jnp.max(begin_b + count_b.astype(jnp.int32))
    begin_rows = jnp.concatenate([begin_b.astype(jnp.float32)] * top, 0)
    base_a, base_b = over(above[:, :half]), over(above[:, half:]) + begin_rows
    lanes = lax.broadcasted_iota(jnp.int32, (rows, columns), 1)
    placed = marks * (prefix + jnp.where(lanes < half, base_a, base_b))
    ranks = [
        jnp.sum(placed[k * classes : (k + 1) * classes], axis=0, keepdims=True).astype(jnp.int32)
        for k in range(top)
    ]
    lane_rows = cap // 128
    for f, total in enumerate((count_a, count_b)):
        spread = jnp.broadcast_to(total, (classes, 128))
        for c in range(classes):
            at = FIELDS * lane_rows + f
            out_ref[c, at : at + 1, :] = spread[c : c + 1, :]
    iota_rank = lax.broadcasted_iota(jnp.int32, (CHUNK, columns), 0)

    def one_chunk(j, carry):
        found = jnp.zeros((CHUNK, len(parts) * classes), jnp.float32)
        for k in range(top):
            hot = jnp.where(iota_rank == ranks[k] - j * CHUNK, 1.0, 0.0).astype(jnp.bfloat16)
            found = found + lax.dot_general(
                hot, values[k], (((1,), (1,)), ((), ())), preferred_element_type=jnp.float32
            )
        turned = found.T
        part = lambda p: turned[p * classes : (p + 1) * classes]
        fields = [
            part(0) * 128.0 + part(1),
            part(4) + part(5) + part(6),
            part(2) * 256.0 + part(3),
        ]
        for f in range(FIELDS):
            for h in range(CHUNK // 128):
                at = f * lane_rows + j * (CHUNK // 128) + h
                for c in range(classes):
                    out_ref[c, pl.ds(at, 1), :] = fields[f][c : c + 1, h * 128 : (h + 1) * 128]
        return carry

    lax.fori_loop(0, (most + CHUNK - 1) // CHUNK, one_chunk, 0)


def build_lists(sizes, here, owner, slot, weight, after):
    nz, nx, nc, quarter, classes, cap = sizes
    top, columns = owner.shape
    lane_rows = cap // 128
    return pl.pallas_call(
        functools.partial(lists_kernel, sizes),
        out_shape=jax.ShapeDtypeStruct((classes, -(-(FIELDS * lane_rows + 2) // 8) * 8, 128), jnp.float32),
        in_specs=[pl.BlockSpec(memory_space=pltpu.SMEM)] + [pl.BlockSpec(memory_space=pl.ANY)] * 4,
        out_specs=pl.BlockSpec(memory_space=pltpu.VMEM),
        scratch_shapes=[
            pltpu.VMEM((top, 8 * classes, columns), jnp.bfloat16),
            pltpu.VMEM((top, columns), jnp.int32),
            pltpu.VMEM((top, columns), jnp.int32),
            pltpu.VMEM((top, columns), jnp.float32),
            pltpu.SemaphoreType.DMA((3,)),
        ],
        cost_estimate=pl.CostEstimate(flops=0, bytes_accessed=12 * 1024 * 1024, transcendentals=0),
        compiler_params=pltpu.CompilerParams(vmem_limit_bytes=24 * 1024 * 1024),
    )(here, owner, slot, weight, after)


def partials_kernel(
    jobs, sizes, place_ref, count_ref, row_ref, weight_ref, list_ref, table_ref, after_ref, *rest
):
    ny, nx, cap = sizes
    outs, (picked,) = rest[: len(jobs)], rest[len(jobs) :]
    columns = outs[0].shape[1] // 2
    lane_rows = cap // 128
    iota = lax.broadcasted_iota(jnp.int32, (columns, 128), 0)
    lanes = lax.broadcasted_iota(jnp.int32, (1, 128), 1)
    picked[...] = jnp.zeros_like(picked)

    def gather(rows, weights, first, count):
        def some(i, carry):
            base = pl.multiple_of(i * STEP, STEP)
            for u in range(STEP):
                picked[pl.ds(base + u, 1), :] = (
                    table_ref[pl.ds(rows[first + base + u], 1), :] * weights[first + base + u]
                )
            return carry

        lax.fori_loop(0, (count + STEP - 1) // STEP, some, 0)

    def chunk_sum(half, at, begin, count, j):
        first = begin + j * CHUNK
        left = jnp.minimum(count - j * CHUNK, CHUNK)
        near = first + CHUNK <= NEAR

        @pl.when(near)
        def _():
            gather(row_ref, weight_ref, at * NEAR + first, left)

        @pl.when(jnp.logical_not(near))
        def _():
            def single(u, carry):
                line = lax.shift_right_logical(first + u, 7)
                here = lanes == jnp.bitwise_and(first + u, 127)
                pick = lambda f: jnp.sum(
                    jnp.where(here, list_ref[at, pl.ds(f * lane_rows + line, 1), :], 0.0)
                )
                row = pick(0).astype(jnp.int32)
                picked[pl.ds(u, 1), :] = table_ref[pl.ds(row, 1), :] * pick(1)
                return carry

            lax.fori_loop(0, left, single, 0)

        rows = picked[...]
        high = rows.astype(jnp.bfloat16)
        low = (rows - high.astype(jnp.float32)).astype(jnp.bfloat16)
        hot = []
        for h in range(CHUNK // 128):
            line = 2 * lane_rows + lax.shift_right_logical(first, 7) + h
            place = list_ref[at, pl.ds(line, 1), :].astype(jnp.int32) - half * columns
            place = jnp.where(lanes < left - h * 128, place, -1)
            hot.append(jnp.where(iota == place, 1.0, 0.0).astype(jnp.bfloat16))
        summed = jnp.dot(
            jnp.concatenate(hot, 1), jnp.concatenate([high, low], 1), preferred_element_type=jnp.float32
        )
        return summed[:, :128] + summed[:, 128:]

    for offset, out_ref in zip(jobs, outs):

        def one(t, carry):
            swap = place_ref[2]
            y = (place_ref[0] + jnp.where(swap == 0, offset, t)) % ny
            x = (place_ref[1] + jnp.where(swap == 0, t, offset)) % nx
            at = y * nx + x
            count_a = count_ref[at]
            begin_b = lax.shift_left(lax.shift_right_logical(count_a + 127, 7), 7)
            for half, count, begin in ((0, count_a, 0), (1, count_ref[ny * nx + at], begin_b)):
                span = pl.ds(half * columns, columns)
                out_ref[t, span, :] = chunk_sum(half, at, begin, count, 0)

                def more(j, carry):
                    out_ref[t, span, :] += chunk_sum(half, at, begin, count, j)
                    return carry

                lax.fori_loop(1, (count + CHUNK - 1) // CHUNK, more, 0)
            return carry

        lax.fori_loop(0, out_ref.shape[0], one, 0)


def partial_sums(jobs, sizes, columns, cost, place, counts, near_rows, near_weights, lists, table, after):
    ny, nx, cap = sizes
    vmem = pl.BlockSpec(memory_space=pltpu.VMEM)
    smem = pl.BlockSpec(memory_space=pltpu.SMEM)
    anywhere = pl.BlockSpec(memory_space=pl.ANY)
    return pl.pallas_call(
        functools.partial(partials_kernel, jobs, sizes),
        in_specs=[smem, smem, smem, smem, vmem, vmem, anywhere],
        out_specs=[vmem] * len(jobs),
        scratch_shapes=[
            pltpu.VMEM((CHUNK, 128), jnp.float32),
        ],
        out_shape=[
            jax.ShapeDtypeStruct((nx, columns, 128), jnp.float32) for _ in jobs
        ],
        compiler_params=pltpu.CompilerParams(vmem_limit_bytes=24 * 1024 * 1024),
        cost_estimate=pl.CostEstimate(
            flops=0, bytes_accessed=cost, transcendentals=0
        ),
    )(place, counts, near_rows, near_weights, lists, table, after)


def moved(value, axis, by):
    count = lax.axis_size(axis)
    return lax.ppermute(value, axis, [(i, (i + by) % count) for i in range(count)])


def ordered(value, earlier):
    probe = earlier.reshape(-1)[0]
    return jnp.where(probe != probe, probe, value)


def assemble_kernel(spots, *refs):
    sources, (out_ref, sems) = refs[:-2], refs[-2:]
    copies = [
        pltpu.make_async_copy(
            sources[source].at[pl.ds(begin, size)], out_ref.at[pl.ds(target, size)], sems.at[i]
        )
        for i, (source, begin, size, target) in enumerate(spots)
    ]
    for copy in copies:
        copy.start()
    for copy in copies:
        copy.wait()


def gathered(own, make_lists):
    rows, block = own.shape
    nz, nc = lax.axis_size("z"), lax.axis_size("c")
    onward = [(z * nc, (z + 1) % nz * nc) for z in range(nz)]
    onward += [(z * nc + 1, (z - 1) % nz * nc + 1) for z in range(nz)]
    swapped = lambda value: moved(value, "c", 1)
    mate = swapped(own)
    lists = make_lists(mate)
    arrays, spots = [own, mate], [(0, 0, rows, 0), (1, 0, rows, nz * rows)]
    pair = jnp.concatenate([own, mate], 0)
    for step in range(1, nz // 2 + 1):
        last = step == nz // 2
        if step == 2:
            pair = ordered(pair, lists[0, -2, :1])
        pair = lax.ppermute(pair[:rows] if last else pair, ("z", "c"), onward)
        arrays += [pair, swapped(pair)]
        place = len(arrays)
        spots.append((place - 2, 0, rows, step * rows))
        if last:
            spots.append((place - 1, 0, rows, (nz + step) * rows))
        else:
            spots.append((place - 2, rows, rows, (nz + step) * rows))
            spots.append((place - 1, 0, rows, (2 * nz - step) * rows))
            spots.append((place - 1, rows, rows, (nz - step) * rows))
    anywhere = pl.BlockSpec(memory_space=pl.ANY)
    table = pl.pallas_call(
        functools.partial(assemble_kernel, tuple(spots)),
        in_specs=[anywhere] * len(arrays),
        out_specs=pl.BlockSpec(memory_space=pltpu.VMEM),
        scratch_shapes=[pltpu.SemaphoreType.DMA((len(spots),))],
        out_shape=jax.ShapeDtypeStruct((nc * nz * rows, block), own.dtype),
        compiler_params=pltpu.CompilerParams(vmem_limit_bytes=16 * 1024 * 1024),
    )(*arrays)
    return table, lists


def shifted(shard, axis, by):
    devices = lax.axis_size(axis)
    pairs = [(i, i + by) for i in range(devices) if 0 <= i + by < devices]
    return lax.ppermute(shard, axis, pairs)


SUB = ("z", "x", "c")


def log_conductivity(model, block_owner_rank, source_slot, weights):
    ny, nz, nx, nc = (lax.axis_size(a) for a in ("y", "z", "x", "c"))
    quarter, block = model.shape[0], model.shape[2]
    columns, top = weights.shape[1:]
    here = jnp.stack([lax.axis_index("z"), lax.axis_index("c")]).astype(jnp.int32)
    classes = ny * nx
    cap = min(columns * top, nz * nc * 128) + CHUNK
    sizes = (nz, nx, nc, quarter, classes, cap)

    def make_lists(after):
        return build_lists(
            sizes, here, block_owner_rank[0].T, source_slot[0].T, weights[0].T, after
        )

    table, lists = gathered(model.reshape(quarter, block), make_lists)
    lists = lax.all_to_all(lists, ("y", "x"), split_axis=0, concat_axis=0, tiled=True)
    lane_rows, near = cap // 128, NEAR // 128
    near_rows = lists[:, :near].reshape(-1).astype(jnp.int32)
    near_factors = lists[:, lane_rows : lane_rows + near].reshape(-1)
    counts = lists[:, FIELDS * lane_rows : FIELDS * lane_rows + 2, 0].T.reshape(-1).astype(jnp.int32)
    place = jnp.stack([lax.axis_index(a) for a in ("y", "x", "c")]).astype(jnp.int32)

    def sums(after, cost, *offsets):
        return partial_sums(
            offsets, (ny, nx, cap), columns, cost, place, counts, near_rows, near_factors, lists, table, after
        )

    def sent(value, by, turn):
        pairs = []
        for i in range(ny * nx * nc):
            y, x, c = i // (nx * nc), i // nc % nx, i % nc
            to_y, to_x = ((y + by) % ny, x) if c == turn else (y, (x + by) % nx)
            pairs.append((i, (to_y * nx + to_x) * nc + c))
        return lax.ppermute(value, ("y", "x", "c"), pairs)

    mib = 1024 * 1024
    (far,) = sums(place, 10 * mib, 2)
    up, down = sums(far, 40 * mib, 1, 3)
    far = sent(far, 2, 0)
    (near,) = sums(far, 40 * mib, 0)
    got = [sent(up, 1, 0), sent(down, 3, 0)]
    joined = [near[d] + far[d] + got[0][d] + got[1][d] for d in range(nx)]
    return sum((sent(joined[d], d, 1) for d in (2, 1, 3)), joined[0]), near


def next_along(value, axis):
    length = value.shape[axis]
    place = lax.broadcasted_iota(jnp.int32, value.shape, axis)
    return jnp.where(place == length - 1, 0.0, pltpu.roll(value, length - 1, axis))


def last_along(value, axis, edge):
    place = lax.broadcasted_iota(jnp.int32, value.shape, axis)
    return jnp.where(place == 0, edge, pltpu.roll(value, 1, axis))


def ahead(value, axis):
    return next_along(value, axis) - value


def behind(value, axis):
    return value - last_along(value, axis, 0.0)


def mean_along(value, axis):
    return 0.5 * (value + last_along(value, axis, value))


def curl_kernel(rim_ref, field_ref, before_ref, after_ref, source_ref, earlier_ref, out_ref):
    planes = field_ref.shape[2]
    rim = rim_ref[0]
    for part in range(2):

        def edges(i):
            ref, at = (before_ref, 0) if i < 0 else (after_ref, 0) if i == planes else (field_ref, i)
            return [ref[part, comp, at] for comp in range(3)]

        now, held_y, held_z = edges(-1), None, None
        for i in range(-1, planes):
            later = edges(i + 1)
            ex, ey, ez = now
            hy = ahead(ex, 1) - (later[2] - ez)
            hz = (later[1] - ey) - ahead(ex, 0)
            if i < 0:
                hy, hz = hy * rim, hz * rim
            else:
                hx = ahead(ez, 0) - ahead(ey, 1)
                curl = (
                    behind(hz, 0) - behind(hy, 1),
                    behind(hx, 1) - (hz - held_z),
                    (hy - held_y) - behind(hx, 0),
                )
                for comp in range(3):
                    out_ref[part, comp, i] = curl[comp] - source_ref[part, comp, i]
            now, held_y, held_z = later, hy, hz


def curl_less_source(rim, field, before, after, source, earlier):
    vmem = pl.BlockSpec(memory_space=pltpu.VMEM)
    return pl.pallas_call(
        curl_kernel,
        in_specs=[pl.BlockSpec(memory_space=pltpu.SMEM)] + [vmem] * 4 + [pl.BlockSpec(memory_space=pl.ANY)],
        out_specs=vmem,
        out_shape=jax.ShapeDtypeStruct(field.shape, jnp.float32),
        compiler_params=pltpu.CompilerParams(vmem_limit_bytes=16 * 1024 * 1024),
        cost_estimate=pl.CostEstimate(flops=0, bytes_accessed=12 * 1024 * 1024, transcendentals=0),
    )(rim, field, before, after, source, earlier)


def residual_kernel(omega_ref, log_ref, prior_ref, rest_ref, field_ref, out_ref, held, sems):
    planes = field_ref.shape[2]
    omega = omega_ref[0]
    conduct = prior_ref[...]
    held_z, held_y = mean_along(conduct, 1), mean_along(conduct, 0)
    copies = []
    for i in range(planes):
        conduct = jnp.exp(log_ref[i])
        mean_z, mean_y = mean_along(conduct, 1), mean_along(conduct, 0)
        sigma = (mean_along(mean_z, 0), 0.5 * (mean_z + held_z), 0.5 * (mean_y + held_y))
        for comp in range(3):
            scaled = omega * sigma[comp]
            held[0, comp, i] = rest_ref[0, comp, i] - scaled * field_ref[1, comp, i]
            held[1, comp, i] = rest_ref[1, comp, i] + scaled * field_ref[0, comp, i]
        held_z, held_y = mean_z, mean_y
        copies.append(pltpu.make_async_copy(held.at[:, :, i], out_ref.at[:, :, i], sems.at[i]))
        copies[-1].start()
    for copy in copies:
        copy.wait()


def residual(omega, log_cond, prior, rest, field):
    vmem = pl.BlockSpec(memory_space=pltpu.VMEM)
    return pl.pallas_call(
        residual_kernel,
        in_specs=[pl.BlockSpec(memory_space=pltpu.SMEM)] + [vmem] * 4,
        out_specs=pl.BlockSpec(memory_space=pl.ANY),
        out_shape=jax.ShapeDtypeStruct(field.shape, jnp.float32),
        scratch_shapes=[
            pltpu.VMEM(field.shape, jnp.float32),
            pltpu.SemaphoreType.DMA((field.shape[2],)),
        ],
        compiler_params=pltpu.CompilerParams(vmem_limit_bytes=16 * 1024 * 1024),
    )(omega, log_cond, prior, rest, field)


def per_device(model, block_owner_rank, source_slot, weights, field, source, freq):
    efield = field[0]
    planes, cells_y = efield.shape[2:4]
    first_device = lax.axis_index(SUB) == 0

    halos = [shifted(efield[:, :, -1:], SUB, 1), shifted(efield[:, :, :1], SUB, -1)]
    log_cond, near = log_conductivity(model, block_owner_rank, source_slot, weights)
    log_cond = log_cond.reshape(planes, cells_y, -1)
    rim = jnp.where(first_device, 0.0, 1.0).astype(jnp.float32)[None]
    rest = curl_less_source(rim, efield, *halos, source[0], near)
    prior = shifted(jnp.exp(log_cond[-1]), SUB, 1)
    prior = jnp.where(first_device, jnp.exp(log_cond[0]), prior)
    return residual(freq, log_cond, prior, rest, efield)[None]


def solution(mesh):
    fine = Mesh(mesh.devices.reshape(4, 8, 4, 2), ("y",) + SUB)
    in_specs = (
        P("y", SUB, None),
        P("y", SUB, None),
        P("y", SUB, None),
        P("y", SUB, None),
        P("y", None, None, SUB, None, None),
        P("y", None, None, SUB, None, None),
        P("y"),
    )
    out_specs = P("y", None, None, SUB, None, None)
    return jax.shard_map(
        per_device, mesh=fine, in_specs=in_specs, out_specs=out_specs, check_vma=False
    )
```

time: 136 us -> 107 us (0.79)
  the two profiles are of different devices: /device:TPU:56 before, /device:TPU:103 now
where the time goes in v3:
time: 107 us; the launch traced here: 105 us
  starting transfers between devices  43.5 us (41%)
  Pallas kernels  25.7 us (24%)
  waiting for transfers between devices  25.3 us (24%)
  local copies, waits for them, and re-layouts  6.4 us (6%)
  between operations  2.32 us (2%)
  other arithmetic  2.2 us (2%)
    pallas_call x3, Pallas kernels, partial_sums(): pl.pallas_call(functools.partial(partials_kernel, jobs, sizes), in_specs=...  17.9 us
    ppermute x3, starting transfers between devices, shifted(): return lax.ppermute(shard, axis, pairs)  16.5 us
    ppermute x4, waiting for transfers between devices, gathered(): pair = lax.ppermute(pair[:rows] if last else pair, ('z', 'c'), onward)  12.8 us
    ppermute x5, starting transfers between devices, moved(): lax.ppermute(value, axis, [(i, (i + by) % count) for i in range(count)])  11.6 us
    ppermute x6, waiting for transfers between devices, sent(): return lax.ppermute(value, ('y', 'x', 'c'), pairs)  9.51 us
    ppermute x6, starting transfers between devices, sent(): return lax.ppermute(value, ('y', 'x', 'c'), pairs)  8.41 us
    all_to_all x1, starting transfers between devices, log_conductivity(): lax.all_to_all(lists, ('y', 'x'), split_axis=0, concat_axis=0, tiled=True)  6.86 us
    unnamed x12, local copies, waits for them, and re-layouts  3.57 us
  transfers between devices with their start and end apart: 19, of which 8 were waited for; matrix products, arithmetic and copies ran while one was open for 3% of the time, Pallas kernels for 17%

profile of v3, /device:TPU:103, one launch (start us, length us, event | category | flops | bytes accessed | tf_op | source)
XLA Modules:
  0.0 105.4 jit_solution(7215084527730865404)
XLA Ops:
  0.0 0.7 collective-permute-start
  0.7 1.4 %collective-permute-done.after_ref.refs_1_ = f32[512,128]{1,0:T(8,128)S(1)} collective-permute-done((f32[512,128]{1,0:T(8,128)}, f32[512,128]{1,0:T(8,128)S(1)}, u32[]{:S(2)}, u32[]{:S(2)}) %collective-permute-start) | collective-permute-done | bytes 262176 | tf_op jit(solution)/shard_map/ppermute | solution.py:261
  2.0 1.0 pad_maximum_fusion
  3.0 0.1 collective-permute-start.1
  3.1 0.1 pad_add_fusion.1.here_ref
  3.2 0.7 copy-done.3
  3.9 0.7 copy-done.4
  4.6 0.7 copy-done.5
  5.4 3.5 %shard_map.73 = f32[16,56,128]{2,1,0:T(8,128)} custom-call(s32[2]{0:T(128)S(1)} %pad_add_fusion.1.here_ref, s32[8,512]{1,0:T(8,128)S(1)} %bitcast.53, s32[8,512]{1,0:T(8,128)S(1)} %bitcast.54, f32[8,512]{1,0:T(8,128)S(1)} %bitcast.55, f32[512,128]{1,0:T(8,128)S(1)} %collective-permute-done.after_ref.refs_1_), custom_call_target="tpu_custom_call" | custom-call | bytes 12582912 | tf_op jit(solution)/shard_map/pallas_call | solution.py:138
  8.8 1.2 %slice.105 = f32[1,1,1]{2,1,0:T(1,128)} slice(f32[16,56,128]{2,1,0:T(8,128)} %shard_map.73), slice={[0:1], [54:55], [0:1]} | slice | bytes 8 | tf_op jit(solution)/shard_map/slice | solution.py:296
  11.3 1.2 %collective-permute-done.1.refs_2_ = f32[1024,128]{1,0:T(8,128)S(1)} collective-permute-done((f32[1024,128]{1,0:T(8,128)S(1)}, f32[1024,128]{1,0:T(8,128)S(1)}, u32[]{:S(2)}, u32[]{:S(2)}) %collective-permute-start.1) | collective-permute-done | bytes 524320 | tf_op jit(solution)/shard_map/ppermute | solution.py:297
  12.5 0.7 broadcast_select_fusion
  13.2 0.1 collective-permute-start.3
  13.3 9.2 %collective-permute-done.3.refs_4_ = f32[1024,128]{1,0:T(8,128)S(1)} collective-permute-done((f32[1024,128]{1,0:T(8,128)S(1)}, f32[1024,128]{1,0:T(8,128)S(1)}, u32[]{:S(2)}, u32[]{:S(2)}) %collective-permute-start.3) | collective-permute-done | bytes 524320 | tf_op jit(solution)/shard_map/ppermute | solution.py:297
  22.5 6.9 %all-to-all-start = ((f32[16,56,128]{2,1,0:T(8,128)}), f32[16,56,128]{2,1,0:T(8,128)S(1)}, u32[]{:S(2)}, u32[]{:S(2)}) async-start(f32[16,56,128]{2,1,0:T(8,128)} %shard_map.73), calls=%async_computation | async-start | bytes 917504 | tf_op jit(solution)/shard_map/all_to_all | solution.py:343
  29.4 2.4 %collective-permute-done.5.refs_6_ = f32[1024,128]{1,0:T(8,128)S(1)} collective-permute-done((f32[1024,128]{1,0:T(8,128)S(1)}, f32[1024,128]{1,0:T(8,128)S(1)}, u32[]{:S(2)}, u32[]{:S(2)}) %collective-permute-start.5) | collective-permute-done | bytes 524320 | tf_op jit(solution)/shard_map/ppermute | solution.py:297
  31.8 0.7 slice.106
  32.5 0.0 collective-permute-start.7
  32.5 6.8 %collective-permute-start.2 = (f32[1024,128]{1,0:T(8,128)S(1)}, f32[1024,128]{1,0:T(8,128)S(1)}, u32[]{:S(2)}, u32[]{:S(2)}) collective-permute-start(f32[1024,128]{1,0:T(8,128)S(1)} %collective-permute-done.1.refs_2_), channel_id=1, source_target_pairs={{0,1},{1,0},{2,3},{3,2},{4,5},{5,4},{6,7},{7,6},{8,9},{9,8},{10,11... | collective-permute-start | bytes 1572872 | tf_op jit(solution)/shard_map/ppermute | solution.py:261
  39.3 0.0 collective-permute-start.4
  39.3 0.5 collective-permute-start.6
  39.8 0.1 pad_add_fusion.place_ref.after_ref
  39.9 3.6 %collective-permute-start.8 = (f32[512,128]{1,0:T(8,128)S(1)}, f32[512,128]{1,0:T(8,128)}, u32[]{:S(2)}, u32[]{:S(2)}) collective-permute-start(f32[512,128]{1,0:T(8,128)S(1)} %collective-permute-done.7.refs_8_), channel_id=1, source_target_pairs={{0,1},{1,0},{2,3},{3,2},{4,5},{5,4},{6,7},{7,6},{8,9},{9,8},{10,11... | collective-permute-start | bytes 786440 | tf_op jit(solution)/shard_map/ppermute | solution.py:261
  43.5 0.1 copy.9
  43.6 0.1 convert_element_type.17.count_ref
  43.7 1.1 %collective-permute-done.8.refs_9_ = f32[512,128]{1,0:T(8,128)} collective-permute-done((f32[512,128]{1,0:T(8,128)S(1)}, f32[512,128]{1,0:T(8,128)}, u32[]{:S(2)}, u32[]{:S(2)}) %collective-permute-start.8) | collective-permute-done | bytes 262176 | tf_op jit(solution)/shard_map/ppermute | solution.py:261
  44.8 1.6 %shard_map.74.table_ref = f32[8192,128]{1,0:T(8,128)S(1)} custom-call(f32[512,128]{1,0:T(8,128)S(1)} %bitcast.46, f32[512,128]{1,0:T(8,128)S(1)} %collective-permute-done.after_ref.refs_1_, f32[1024,128]{1,0:T(8,128)S(1)} %collective-permute-done.1.refs_2_, f32[1024,128]{1,0:T(8,128)S(1)} %collective-permute-done.2.refs_3_, ...), custom_call_target="tpu_custom_call" | custom-call | tf_op jit(solution)/shard_map/pallas_call | solution.py:308
  46.3 4.9 %shard_map.75.after_ref = f32[4,512,128]{2,1,0:T(8,128)S(1)} custom-call(s32[3]{0:T(128)S(1)} %pad_add_fusion.place_ref.after_ref, s32[32]{0:T(128)S(1)} %convert_element_type.17.count_ref, s32[8192]{0:T(1024)S(1)} %bitcast.50, f32[8192]{0:T(1024)S(1)} %bitcast.47, f32[16,56,128]{2,1,0:T(8,128)S(1)} %all-to-all-done.list_ref, ...), custom_call_target="tpu_custom_call" | custom-call | bytes 10485760 | tf_op jit(solution)/shard_map/pallas_call | solution.py:242
  51.3 1.5 %collective-permute-start.9 = (f32[4,512,128]{2,1,0:T(8,128)S(1)}, f32[4,512,128]{2,1,0:T(8,128)S(1)}, u32[]{:S(2)}, u32[]{:S(2)}) collective-permute-start(f32[4,512,128]{2,1,0:T(8,128)S(1)} %shard_map.75.after_ref), channel_id=1, source_target_pairs={{0,128},{1,5},{2,130},{3,7},{4,132},{5,1},{6,134},{7,3},{64,192},{... | collective-permute-start | bytes 3145736 | tf_op jit(solution)/shard_map/ppermute | solution.py:361
  52.8 8.0 %shard_map.77 = (f32[4,512,128]{2,1,0:T(8,128)S(1)}, f32[4,512,128]{2,1,0:T(8,128)S(1)}) custom-call(s32[3]{0:T(128)S(1)} %pad_add_fusion.place_ref.after_ref, s32[32]{0:T(128)S(1)} %convert_element_type.17.count_ref, s32[8192]{0:T(1024)S(1)} %bitcast.51, f32[8192]{0:T(1024)S(1)} %bitcast.48, f32[16,56,128]{2,1,0:T(8,128)S(1)} %all-to-all-done.list_ref, ...), custom_call_target="tpu_custom_call" | custom-call | bytes 41943040 | tf_op jit(solution)/shard_map/pallas_call | solution.py:242
  60.8 0.1 collective-permute-start.11
  60.9 2.7 %collective-permute-start.10 = (f32[4,512,128]{2,1,0:T(8,128)S(1)}, f32[4,512,128]{2,1,0:T(8,128)S(1)}, u32[]{:S(2)}, u32[]{:S(2)}) collective-permute-start(f32[4,512,128]{2,1,0:T(8,128)S(1)} %get-tuple-element.7), channel_id=1, source_target_pairs={{0,64},{1,3},{2,66},{3,5},{4,68},{5,7},{6,70},{7,1},{64,128},{65,6... | collective-permute-start | bytes 3145736 | tf_op jit(solution)/shard_map/ppermute | solution.py:361
  63.6 3.3 %collective-permute-done.9.after_ref = f32[4,512,128]{2,1,0:T(8,128)S(1)} collective-permute-done((f32[4,512,128]{2,1,0:T(8,128)S(1)}, f32[4,512,128]{2,1,0:T(8,128)S(1)}, u32[]{:S(2)}, u32[]{:S(2)}) %collective-permute-start.9) | collective-permute-done | bytes 1048608 | tf_op jit(solution)/shard_map/ppermute | solution.py:361
  66.9 5.0 %shard_map.76.earlier_ref = f32[4,512,128]{2,1,0:T(8,128)S(1)} custom-call(s32[3]{0:T(128)S(1)} %pad_add_fusion.place_ref.after_ref, s32[32]{0:T(128)S(1)} %convert_element_type.17.count_ref, s32[8192]{0:T(1024)S(1)} %bitcast.52, f32[8192]{0:T(1024)S(1)} %bitcast.49, f32[16,56,128]{2,1,0:T(8,128)S(1)} %all-to-all-done.list_ref, ...), custom_call_target="tpu_custom_call" | custom-call | bytes 41943040 | tf_op jit(solution)/shard_map/pallas_call | solution.py:242
  71.8 0.0 copy-start
  71.8 6.2 %collective-permute-done.11 = f32[4,512,128]{2,1,0:T(8,128)S(1)} collective-permute-done((f32[4,512,128]{2,1,0:T(8,128)S(1)}, f32[4,512,128]{2,1,0:T(8,128)S(1)}, u32[]{:S(2)}, u32[]{:S(2)}) %collective-permute-start.11) | collective-permute-done | bytes 1048608 | tf_op jit(solution)/shard_map/ppermute | solution.py:361
  78.1 0.2 fusion.2
  78.3 2.8 %collective-permute-start.14 = (f32[512,128]{1,0:T(8,128)S(1)}, f32[512,128]{1,0:T(8,128)S(1)}, u32[]{:S(2)}, u32[]{:S(2)}) collective-permute-start(f32[512,128]{1,0:T(8,128)S(1)} %get-tuple-element.10), channel_id=1, source_target_pairs={{0,6},{1,193},{2,0},{3,195},{4,2},{5,197},{6,4},{7,199},{64,70},{6... | collective-permute-start | bytes 786440 | tf_op jit(solution)/shard_map/ppermute | solution.py:361
  81.1 1.3 %collective-permute-start.12 = (f32[512,128]{1,0:T(8,128)S(1)}, f32[512,128]{1,0:T(8,128)S(1)}, u32[]{:S(2)}, u32[]{:S(2)}) collective-permute-start(f32[512,128]{1,0:T(8,128)S(1)} %get-tuple-element.9), channel_id=1, source_target_pairs={{0,4},{1,129},{2,6},{3,131},{4,0},{5,133},{6,2},{7,135},{64,68},{6... | collective-permute-start | bytes 786440 | tf_op jit(solution)/shard_map/ppermute | solution.py:361
  82.4 0.7 fusion.8
  83.1 7.6 %collective-permute-start.16 = (f32[2,3,1,64,128]{4,3,2,1,0:T(8,128)}, f32[2,3,1,64,128]{4,3,2,1,0:T(8,128)S(1)}, u32[]{:S(2)}, u32[]{:S(2)}) collective-permute-start(f32[2,3,1,64,128]{4,3,2,1,0:T(8,128)} %get-tuple-element.13), channel_id=1, source_target_pairs={{0,1},{1,2},{2,3},{3,4},{4,5},{5,6},{6,7},{7,8},{8,9},{9,10},{10,1... | collective-permute-start | bytes 589832 | tf_op jit(solution)/shard_map/ppermute | solution.py:322
  90.7 1.9 %collective-permute-start.17 = (f32[2,3,1,64,128]{4,3,2,1,0:T(8,128)S(1)}, f32[2,3,1,64,128]{4,3,2,1,0:T(8,128)S(1)}, u32[]{:S(2)}, u32[]{:S(2)}) collective-permute-start(f32[2,3,1,64,128]{4,3,2,1,0:T(8,128)S(1)} %get-tuple-element.12), channel_id=1, source_target_pairs={{1,0},{2,1},{3,2},{4,3},{5,4},{6,5},{7,6},{8,7},{9,8},{10,9},{11,1... | collective-permute-start | bytes 589832 | tf_op jit(solution)/shard_map/ppermute | solution.py:322
  92.7 0.1 fusion.6
  92.8 7.0 %collective-permute-start.15 = (f32[64,128]{1,0:T(8,128)S(1)}, f32[64,128]{1,0:T(8,128)S(1)}, u32[]{:S(2)}, u32[]{:S(2)}) collective-permute-start(f32[64,128]{1,0:T(8,128)S(1)} %slice_exponential_fusion), channel_id=1, source_target_pairs={{0,1},{1,2},{2,3},{3,4},{4,5},{5,6},{6,7},{7,8},{8,9},{9,10},{10,1... | collective-permute-start | bytes 98312 | tf_op jit(solution)/shard_map/ppermute | solution.py:322
  100.5 0.6 collective-permute-done.17.after_ref
  101.0 1.4 %copy-done.1 = f32[1,2,3,8,64,128]{5,4,3,2,1,0:T(8,128)S(1)} copy-done((f32[1,2,3,8,64,128]{5,4,3,2,1,0:T(8,128)S(1)}, f32[1,2,3,8,64,128]{5,4,3,2,1,0:T(8,128)}, u32[]{:S(2)}) %copy-start.1) | copy-done | bytes 1572888
  102.5 1.4 %shard_map.78.rest_ref = f32[2,3,8,64,128]{4,3,2,1,0:T(8,128)S(1)} custom-call(f32[1]{0:T(128)} %bitcast.21.rim_ref, f32[2,3,8,64,128]{4,3,2,1,0:T(8,128)S(1)} %bitcast.40, f32[2,3,1,64,128]{4,3,2,1,0:T(8,128)S(1)} %collective-permute-done.16.before_ref, f32[2,3,1,64,128]{4,3,2,1,0:T(8,128)S(1)} %collective-permute-done.17.after_ref, ...), custom_call_target="tpu_custom_call" | custom-call | bytes 12582912 | tf_op jit(solution)/shard_map/pallas_call | solution.py:427
  103.8 1.4 %shard_map.79 = f32[2,3,8,64,128]{4,3,2,1,0:T(8,128)} custom-call(f32[1]{0:T(128)S(6)} %copy.10.omega_ref, f32[8,64,128]{2,1,0:T(8,128)S(1)} %bitcast.43, f32[64,128]{1,0:T(8,128)S(1)} %fusion.7.prior_ref, f32[2,3,8,64,128]{4,3,2,1,0:T(8,128)S(1)} %shard_map.78.rest_ref, f32[2,3,8,64,128]{4,3,2,1,0:T(8,128)S(1)} %bitcast.41), custom_call_target="tpu_custom_call" | custom-call | tf_op jit(solution)/shard_map/pallas_call | solution.py:460
  (24 shorter events, 0.1 us)
Async XLA Ops:
  0.0 2.0 %collective-permute-start = (f32[512,128]{1,0:T(8,128)}, f32[512,128]{1,0:T(8,128)S(1)}, u32[]{:S(2)}, u32[]{:S(2)}) collective-permute-start(f32[512,128]{1,0:T(8,128)} %bitcast.44), channel_id=1, source_target_pairs={{0,1},{1,0},{2,3},{3,2},{4,5},{5,4},{6,7},{7,6},{8,9},{9,8},{10,11... | collective-permute-start | bytes 786440 | tf_op jit(solution)/shard_map/ppermute | solution.py:261
  3.0 9.5 %collective-permute-start.1 = (f32[1024,128]{1,0:T(8,128)S(1)}, f32[1024,128]{1,0:T(8,128)S(1)}, u32[]{:S(2)}, u32[]{:S(2)}) collective-permute-start(f32[1024,128]{1,0:T(8,128)S(1)} %pad_maximum_fusion), channel_id=1, source_target_pairs={{0,8},{8,16},{16,24},{24,32},{32,40},{40,48},{48,56},{56,0},{1,57}... | collective-permute-start | bytes 1572872 | tf_op jit(solution)/shard_map/ppermute | solution.py:297
  3.2 0.7 copy-start.3
  3.9 0.7 copy-start.4
  4.6 0.7 copy-start.5
  5.4 39.4 %copy-start.2 = (f32[512,1,128]{2,1,0:T(1,128)S(1)}, f32[512,1,128]{2,1,0:T(1,128)}, u32[]{:S(2)}) copy-start(f32[512,1,128]{2,1,0:T(1,128)} %param.7) | copy-start | bytes 786436
  13.2 9.3 %collective-permute-start.3 = (f32[1024,128]{1,0:T(8,128)S(1)}, f32[1024,128]{1,0:T(8,128)S(1)}, u32[]{:S(2)}, u32[]{:S(2)}) collective-permute-start(f32[1024,128]{1,0:T(8,128)S(1)} %broadcast_select_fusion), channel_id=1, source_target_pairs={{0,8},{8,16},{16,24},{24,32},{32,40},{40,48},{48,56},{56,0},{1,57}... | collective-permute-start | bytes 1572872 | tf_op jit(solution)/shard_map/ppermute | solution.py:297
  22.5 9.2 %collective-permute-start.5 = (f32[1024,128]{1,0:T(8,128)S(1)}, f32[1024,128]{1,0:T(8,128)S(1)}, u32[]{:S(2)}, u32[]{:S(2)}) collective-permute-start(f32[1024,128]{1,0:T(8,128)S(1)} %collective-permute-done.3.refs_4_), channel_id=1, source_target_pairs={{0,8},{8,16},{16,24},{24,32},{32,40},{40,48},{48,56},{56,0},{1,57}... | collective-permute-start | bytes 1572872 | tf_op jit(solution)/shard_map/ppermute | solution.py:297
  22.5 20.9 %all-to-all-start = ((f32[16,56,128]{2,1,0:T(8,128)}), f32[16,56,128]{2,1,0:T(8,128)S(1)}, u32[]{:S(2)}, u32[]{:S(2)}) async-start(f32[16,56,128]{2,1,0:T(8,128)} %shard_map.73), calls=%async_computation | async-start | bytes 917504 | tf_op jit(solution)/shard_map/all_to_all | solution.py:343
  32.5 7.4 %collective-permute-start.7 = (f32[512,128]{1,0:T(8,128)}, f32[512,128]{1,0:T(8,128)S(1)}, u32[]{:S(2)}, u32[]{:S(2)}) collective-permute-start(f32[512,128]{1,0:T(8,128)} %slice.106), channel_id=1, source_target_pairs={{0,8},{8,16},{16,24},{24,32},{32,40},{40,48},{48,56},{56,0},{1,57}... | collective-permute-start | bytes 786440 | tf_op jit(solution)/shard_map/ppermute | solution.py:297
  32.5 11.2 %collective-permute-start.2 = (f32[1024,128]{1,0:T(8,128)S(1)}, f32[1024,128]{1,0:T(8,128)S(1)}, u32[]{:S(2)}, u32[]{:S(2)}) collective-permute-start(f32[1024,128]{1,0:T(8,128)S(1)} %collective-permute-done.1.refs_2_), channel_id=1, source_target_pairs={{0,1},{1,0},{2,3},{3,2},{4,5},{5,4},{6,7},{7,6},{8,9},{9,8},{10,11... | collective-permute-start | bytes 1572872 | tf_op jit(solution)/shard_map/ppermute | solution.py:261
  39.3 4.4 %collective-permute-start.4 = (f32[1024,128]{1,0:T(8,128)S(1)}, f32[1024,128]{1,0:T(8,128)}, u32[]{:S(2)}, u32[]{:S(2)}) collective-permute-start(f32[1024,128]{1,0:T(8,128)S(1)} %collective-permute-done.3.refs_4_), channel_id=1, source_target_pairs={{0,1},{1,0},{2,3},{3,2},{4,5},{5,4},{6,7},{7,6},{8,9},{9,8},{10,11... | collective-permute-start | bytes 1572872 | tf_op jit(solution)/shard_map/ppermute | solution.py:261
  39.3 5.5 %collective-permute-start.6 = (f32[1024,128]{1,0:T(8,128)S(1)}, f32[1024,128]{1,0:T(8,128)}, u32[]{:S(2)}, u32[]{:S(2)}) collective-permute-start(f32[1024,128]{1,0:T(8,128)S(1)} %collective-permute-done.5.refs_6_), channel_id=1, source_target_pairs={{0,1},{1,0},{2,3},{3,2},{4,5},{5,4},{6,7},{7,6},{8,9},{9,8},{10,11... | collective-permute-start | bytes 1572872 | tf_op jit(solution)/shard_map/ppermute | solution.py:261
  39.9 4.9 %collective-permute-start.8 = (f32[512,128]{1,0:T(8,128)S(1)}, f32[512,128]{1,0:T(8,128)}, u32[]{:S(2)}, u32[]{:S(2)}) collective-permute-start(f32[512,128]{1,0:T(8,128)S(1)} %collective-permute-done.7.refs_8_), channel_id=1, source_target_pairs={{0,1},{1,0},{2,3},{3,2},{4,5},{5,4},{6,7},{7,6},{8,9},{9,8},{10,11... | collective-permute-start | bytes 786440 | tf_op jit(solution)/shard_map/ppermute | solution.py:261
  51.3 15.6 %collective-permute-start.9 = (f32[4,512,128]{2,1,0:T(8,128)S(1)}, f32[4,512,128]{2,1,0:T(8,128)S(1)}, u32[]{:S(2)}, u32[]{:S(2)}) collective-permute-start(f32[4,512,128]{2,1,0:T(8,128)S(1)} %shard_map.75.after_ref), channel_id=1, source_target_pairs={{0,128},{1,5},{2,130},{3,7},{4,132},{5,1},{6,134},{7,3},{64,192},{... | collective-permute-start | bytes 3145736 | tf_op jit(solution)/shard_map/ppermute | solution.py:361
  60.8 17.2 %collective-permute-start.11 = (f32[4,512,128]{2,1,0:T(8,128)S(1)}, f32[4,512,128]{2,1,0:T(8,128)S(1)}, u32[]{:S(2)}, u32[]{:S(2)}) collective-permute-start(f32[4,512,128]{2,1,0:T(8,128)S(1)} %get-tuple-element.8), channel_id=1, source_target_pairs={{0,192},{1,7},{2,194},{3,1},{4,196},{5,3},{6,198},{7,5},{64,0},{65... | collective-permute-start | bytes 3145736 | tf_op jit(solution)/shard_map/ppermute | solution.py:361
  60.9 17.1 %collective-permute-start.10 = (f32[4,512,128]{2,1,0:T(8,128)S(1)}, f32[4,512,128]{2,1,0:T(8,128)S(1)}, u32[]{:S(2)}, u32[]{:S(2)}) collective-permute-start(f32[4,512,128]{2,1,0:T(8,128)S(1)} %get-tuple-element.7), channel_id=1, source_target_pairs={{0,64},{1,3},{2,66},{3,5},{4,68},{5,7},{6,70},{7,1},{64,128},{65,6... | collective-permute-start | bytes 3145736 | tf_op jit(solution)/shard_map/ppermute | solution.py:361
  71.8 10.6 %copy-start = (f32[1,2,3,8,64,128]{5,4,3,2,1,0:T(8,128)S(1)}, f32[1,2,3,8,64,128]{5,4,3,2,1,0:T(8,128)}, u32[]{:S(2)}) copy-start(f32[1,2,3,8,64,128]{5,4,3,2,1,0:T(8,128)} %param.11) | copy-start | bytes 4718596
  78.3 14.4 %collective-permute-start.14 = (f32[512,128]{1,0:T(8,128)S(1)}, f32[512,128]{1,0:T(8,128)S(1)}, u32[]{:S(2)}, u32[]{:S(2)}) collective-permute-start(f32[512,128]{1,0:T(8,128)S(1)} %get-tuple-element.10), channel_id=1, source_target_pairs={{0,6},{1,193},{2,0},{3,195},{4,2},{5,197},{6,4},{7,199},{64,70},{6... | collective-permute-start | bytes 786440 | tf_op jit(solution)/shard_map/ppermute | solution.py:361
  81.1 11.5 %collective-permute-start.13 = (f32[512,128]{1,0:T(8,128)S(1)}, f32[512,128]{1,0:T(8,128)S(1)}, u32[]{:S(2)}, u32[]{:S(2)}) collective-permute-start(f32[512,128]{1,0:T(8,128)S(1)} %get-tuple-element.11), channel_id=1, source_target_pairs={{0,2},{1,65},{2,4},{3,67},{4,6},{5,69},{6,0},{7,71},{64,66},{65,12... | collective-permute-start | bytes 786440 | tf_op jit(solution)/shard_map/ppermute | solution.py:361
  81.1 11.6 %collective-permute-start.12 = (f32[512,128]{1,0:T(8,128)S(1)}, f32[512,128]{1,0:T(8,128)S(1)}, u32[]{:S(2)}, u32[]{:S(2)}) collective-permute-start(f32[512,128]{1,0:T(8,128)S(1)} %get-tuple-element.9), channel_id=1, source_target_pairs={{0,4},{1,129},{2,6},{3,131},{4,0},{5,133},{6,2},{7,135},{64,68},{6... | collective-permute-start | bytes 786440 | tf_op jit(solution)/shard_map/ppermute | solution.py:361
  83.1 17.4 %collective-permute-start.16 = (f32[2,3,1,64,128]{4,3,2,1,0:T(8,128)}, f32[2,3,1,64,128]{4,3,2,1,0:T(8,128)S(1)}, u32[]{:S(2)}, u32[]{:S(2)}) collective-permute-start(f32[2,3,1,64,128]{4,3,2,1,0:T(8,128)} %get-tuple-element.13), channel_id=1, source_target_pairs={{0,1},{1,2},{2,3},{3,4},{4,5},{5,6},{6,7},{7,8},{8,9},{9,10},{10,1... | collective-permute-start | bytes 589832 | tf_op jit(solution)/shard_map/ppermute | solution.py:322
  90.7 10.3 %collective-permute-start.17 = (f32[2,3,1,64,128]{4,3,2,1,0:T(8,128)S(1)}, f32[2,3,1,64,128]{4,3,2,1,0:T(8,128)S(1)}, u32[]{:S(2)}, u32[]{:S(2)}) collective-permute-start(f32[2,3,1,64,128]{4,3,2,1,0:T(8,128)S(1)} %get-tuple-element.12), channel_id=1, source_target_pairs={{1,0},{2,1},{3,2},{4,3},{5,4},{6,5},{7,6},{8,7},{9,8},{10,9},{11,1... | collective-permute-start | bytes 589832 | tf_op jit(solution)/shard_map/ppermute | solution.py:322
  92.8 11.0 %collective-permute-start.15 = (f32[64,128]{1,0:T(8,128)S(1)}, f32[64,128]{1,0:T(8,128)S(1)}, u32[]{:S(2)}, u32[]{:S(2)}) collective-permute-start(f32[64,128]{1,0:T(8,128)S(1)} %slice_exponential_fusion), channel_id=1, source_target_pairs={{0,1},{1,2},{2,3},{3,4},{4,5},{5,6},{6,7},{7,8},{8,9},{9,10},{10,1... | collective-permute-start | bytes 98312 | tf_op jit(solution)/shard_map/ppermute | solution.py:322
  101.0 1.4 %copy-start.1 = (f32[1,2,3,8,64,128]{5,4,3,2,1,0:T(8,128)S(1)}, f32[1,2,3,8,64,128]{5,4,3,2,1,0:T(8,128)}, u32[]{:S(2)}) copy-start(f32[1,2,3,8,64,128]{5,4,3,2,1,0:T(8,128)} %param.12) | copy-start | bytes 4718596

commit v4 on v3

--- a/solution.py
+++ b/solution.py
@@ -153,35 +153,34 @@
 
 
 def partials_kernel(
-    jobs, sizes, place_ref, count_ref, row_ref, weight_ref, list_ref, table_ref, after_ref, *rest
+    jobs, sizes, place_ref, count_ref, row_ref, weight_ref, list_ref, table_ref, *rest
 ):
     ny, nx, cap = sizes
-    outs, (picked,) = rest[: len(jobs)], rest[len(jobs) :]
+    outs, picked = rest[-1 - len(jobs) : -1], rest[-1]
     columns = outs[0].shape[1] // 2
     lane_rows = cap // 128
     iota = lax.broadcasted_iota(jnp.int32, (columns, 128), 0)
     lanes = lax.broadcasted_iota(jnp.int32, (1, 128), 1)
     picked[...] = jnp.zeros_like(picked)
 
-    def gather(rows, weights, first, count):
-        def some(i, carry):
-            base = pl.multiple_of(i * STEP, STEP)
-            for u in range(STEP):
-                picked[pl.ds(base + u, 1), :] = (
-                    table_ref[pl.ds(rows[first + base + u], 1), :] * weights[first + base + u]
-                )
-            return carry
-
-        lax.fori_loop(0, (count + STEP - 1) // STEP, some, 0)
-
-    def chunk_sum(half, at, begin, count, j):
+    def gather(slot, at, begin, count, j):
         first = begin + j * CHUNK
         left = jnp.minimum(count - j * CHUNK, CHUNK)
         near = first + CHUNK <= NEAR
 
         @pl.when(near)
         def _():
-            gather(row_ref, weight_ref, at * NEAR + first, left)
+            start = at * NEAR + first
+
+            def some(i, carry):
+                base = pl.multiple_of(i * STEP, STEP)
+                for u in range(STEP):
+                    picked[slot, pl.ds(base + u, 1), :] = (
+                        table_ref[pl.ds(row_ref[start + base + u], 1), :] * weight_ref[start + base + u]
+                    )
+                return carry
+
+            lax.fori_loop(0, (left + STEP - 1) // STEP, some, 0)
 
         @pl.when(jnp.logical_not(near))
         def _():
@@ -192,12 +191,15 @@
                     jnp.where(here, list_ref[at, pl.ds(f * lane_rows + line, 1), :], 0.0)
                 )
                 row = pick(0).astype(jnp.int32)
-                picked[pl.ds(u, 1), :] = table_ref[pl.ds(row, 1), :] * pick(1)
+                picked[slot, pl.ds(u, 1), :] = table_ref[pl.ds(row, 1), :] * pick(1)
                 return carry
 
             lax.fori_loop(0, left, single, 0)
 
-        rows = picked[...]
+    def combine(slot, half, at, begin, count, j):
+        first = begin + j * CHUNK
+        left = count - j * CHUNK
+        rows = picked[slot]
         high = rows.astype(jnp.bfloat16)
         low = (rows - high.astype(jnp.float32)).astype(jnp.bfloat16)
         hot = []
@@ -211,27 +213,29 @@
         )
         return summed[:, :128] + summed[:, 128:]
 
-    for offset, out_ref in zip(jobs, outs):
-
-        def one(t, carry):
-            swap = place_ref[2]
+    tasks = []
+    for (offset, begin_t), out_ref in zip(jobs, outs):
+        for step in range(out_ref.shape[0]):
+            t, swap = begin_t + step, place_ref[2]
             y = (place_ref[0] + jnp.where(swap == 0, offset, t)) % ny
             x = (place_ref[1] + jnp.where(swap == 0, t, offset)) % nx
             at = y * nx + x
             count_a = count_ref[at]
             begin_b = lax.shift_left(lax.shift_right_logical(count_a + 127, 7), 7)
-            for half, count, begin in ((0, count_a, 0), (1, count_ref[ny * nx + at], begin_b)):
-                span = pl.ds(half * columns, columns)
-                out_ref[t, span, :] = chunk_sum(half, at, begin, count, 0)
-
-                def more(j, carry):
-                    out_ref[t, span, :] += chunk_sum(half, at, begin, count, j)
-                    return carry
-
-                lax.fori_loop(1, (count + CHUNK - 1) // CHUNK, more, 0)
+            tasks.append((out_ref, step, 0, at, 0, count_a))
+            tasks.append((out_ref, step, 1, at, begin_b, count_ref[ny * nx + at]))
+    for slot, (_, _, _, at, begin, count) in enumerate(tasks):
+        gather(slot, at, begin, count, 0)
+    for slot, (out_ref, step, half, at, begin, count) in enumerate(tasks):
+        out_ref[step, half * columns : (half + 1) * columns, :] = combine(slot, half, at, begin, count, 0)
+    for out_ref, step, half, at, begin, count in tasks:
+
+        def more(j, carry):
+            gather(0, at, begin, count, j)
+            out_ref[step, half * columns : (half + 1) * columns, :] += combine(0, half, at, begin, count, j)
             return carry
 
-        lax.fori_loop(0, out_ref.shape[0], one, 0)
+        lax.fori_loop(1, (count + CHUNK - 1) // CHUNK, more, 0)
 
 
 def partial_sums(jobs, sizes, columns, cost, place, counts, near_rows, near_weights, lists, table, after):
@@ -240,20 +244,20 @@
     smem = pl.BlockSpec(memory_space=pltpu.SMEM)
     anywhere = pl.BlockSpec(memory_space=pl.ANY)
     return pl.pallas_call(
-        functools.partial(partials_kernel, jobs, sizes),
-        in_specs=[smem, smem, smem, smem, vmem, vmem, anywhere],
+        functools.partial(partials_kernel, [job[:2] for job in jobs], sizes),
+        in_specs=[smem, smem, smem, smem, vmem, vmem] + [anywhere] * len(after),
         out_specs=[vmem] * len(jobs),
         scratch_shapes=[
-            pltpu.VMEM((CHUNK, 128), jnp.float32),
+            pltpu.VMEM((2 * sum(job[2] for job in jobs), CHUNK, 128), jnp.float32),
         ],
         out_shape=[
-            jax.ShapeDtypeStruct((nx, columns, 128), jnp.float32) for _ in jobs
+            jax.ShapeDtypeStruct((job[2], columns, 128), jnp.float32) for job in jobs
         ],
         compiler_params=pltpu.CompilerParams(vmem_limit_bytes=24 * 1024 * 1024),
         cost_estimate=pl.CostEstimate(
             flops=0, bytes_accessed=cost, transcendentals=0
         ),
-    )(place, counts, near_rows, near_weights, lists, table, after)
+    )(place, counts, near_rows, near_weights, lists, table, *after)
 
 
 def moved(value, axis, by):
@@ -288,22 +292,24 @@
     swapped = lambda value: moved(value, "c", 1)
     mate = swapped(own)
     lists = make_lists(mate)
-    arrays, spots = [own, mate], [(0, 0, rows, 0), (1, 0, rows, nz * rows)]
-    pair = jnp.concatenate([own, mate], 0)
+    arrays, spots = [], []
+
+    def take(array, spot):
+        spots.append((len(arrays), 0, array.shape[0], spot * rows))
+        arrays.append(array)
+
+    take(own, 0)
+    take(mate, nz)
+    pair = [own, mate]
     for step in range(1, nz // 2 + 1):
-        last = step == nz // 2
         if step == 2:
-            pair = ordered(pair, lists[0, -2, :1])
-        pair = lax.ppermute(pair[:rows] if last else pair, ("z", "c"), onward)
-        arrays += [pair, swapped(pair)]
-        place = len(arrays)
-        spots.append((place - 2, 0, rows, step * rows))
-        if last:
-            spots.append((place - 1, 0, rows, (nz + step) * rows))
-        else:
-            spots.append((place - 2, rows, rows, (nz + step) * rows))
-            spots.append((place - 1, 0, rows, (2 * nz - step) * rows))
-            spots.append((place - 1, rows, rows, (nz - step) * rows))
+            pair[0] = ordered(pair[0], lists[0, -2, :1])
+        if step == nz // 2:
+            pair = pair[:1]
+        pair = [lax.ppermute(one, ("z", "c"), onward) for one in pair]
+        for core, one in enumerate(pair):
+            take(one, core * nz + step)
+            take(swapped(one), (1 - core) * nz + nz - step)
     anywhere = pl.BlockSpec(memory_space=pl.ANY)
     table = pl.pallas_call(
         functools.partial(assemble_kernel, tuple(spots)),
@@ -361,12 +367,12 @@
         return lax.ppermute(value, ("y", "x", "c"), pairs)
 
     mib = 1024 * 1024
-    (far,) = sums(place, 10 * mib, 2)
-    up, down = sums(far, 40 * mib, 1, 3)
+    (far,) = sums((), 10 * mib, (2, 0, nx))
+    up, down = sums((far,), 40 * mib, (1, 0, nx), (3, 0, nx))
     far = sent(far, 2, 0)
-    (near,) = sums(far, 40 * mib, 0)
-    got = [sent(up, 1, 0), sent(down, 3, 0)]
-    joined = [near[d] + far[d] + got[0][d] + got[1][d] for d in range(nx)]
+    (near,) = sums((far,), 40 * mib, (0, 0, nx))
+    got = [far, sent(up, 1, 0), sent(down, 3, 0)]
+    joined = [near[d] + got[0][d] + got[1][d] + got[2][d] for d in range(nx)]
     return sum((sent(joined[d], d, 1) for d in (2, 1, 3)), joined[0]), near
 
 

time: 107 us -> 101 us (0.944)
  the two profiles are of different devices: /device:TPU:103 before, /device:TPU:71 now
where the time goes in v4:
time: 101 us
  starting transfers between devices  47.2 us (47%)
  Pallas kernels  23.3 us (23%)
  waiting for transfers between devices  21.1 us (21%)
  local copies, waits for them, and re-layouts  5.65 us (6%)
  between operations  2.2 us (2%)
  other arithmetic  1.12 us (1%)
    ppermute x3, starting transfers between devices, shifted(): return lax.ppermute(shard, axis, pairs)  15.8 us
    pallas_call x3, Pallas kernels, partial_sums(): pl.pallas_call(functools.partial(partials_kernel, [job[:2] for job in job...  15.5 us
    ppermute x6, waiting for transfers between devices, sent(): return lax.ppermute(value, ('y', 'x', 'c'), pairs)  11.7 us
    ppermute x7, starting transfers between devices, gathered(): pair = [lax.ppermute(one, ('z', 'c'), onward) for one in pair]  8.53 us
    ppermute x8, starting transfers between devices, moved(): lax.ppermute(value, axis, [(i, (i + by) % count) for i in range(count)])  8.03 us
    ppermute x6, starting transfers between devices, sent(): return lax.ppermute(value, ('y', 'x', 'c'), pairs)  7.93 us
    ppermute x7, waiting for transfers between devices, gathered(): pair = [lax.ppermute(one, ('z', 'c'), onward) for one in pair]  7.09 us
    all_to_all x1, starting transfers between devices, log_conductivity(): lax.all_to_all(lists, ('y', 'x'), split_axis=0, concat_axis=0, tiled=True)  6.87 us
  transfers between devices with their start and end apart: 25, of which 8 were waited for; matrix products, arithmetic and copies ran while one was open for 3% of the time, Pallas kernels for 16%

profile of v4, /device:TPU:71, one launch (start us, length us, event | category | flops | bytes accessed | tf_op | source)
XLA Modules:
  0.0 100.6 jit_solution(14239190476216583848)
XLA Ops:
  0.0 0.7 collective-permute-start
  0.8 1.3 %collective-permute-done.after_ref.refs_1_ = f32[512,128]{1,0:T(8,128)S(1)} collective-permute-done((f32[512,128]{1,0:T(8,128)}, f32[512,128]{1,0:T(8,128)S(1)}, u32[]{:S(2)}, u32[]{:S(2)}) %collective-permute-start) | collective-permute-done | bytes 262176 | tf_op jit(solution)/shard_map/ppermute | solution.py:265
  2.1 0.7 copy-done.3
  2.8 0.7 copy-done.4
  3.5 0.7 copy-done.5
  4.2 3.5 %shard_map.73 = f32[16,56,128]{2,1,0:T(8,128)} custom-call(s32[2]{0:T(128)S(1)} %pad_add_fusion.1.here_ref, s32[8,512]{1,0:T(8,128)S(1)} %bitcast.53, s32[8,512]{1,0:T(8,128)S(1)} %bitcast.54, f32[8,512]{1,0:T(8,128)S(1)} %bitcast.55, f32[512,128]{1,0:T(8,128)S(1)} %collective-permute-done.after_ref.refs_1_), custom_call_target="tpu_custom_call" | custom-call | bytes 12582912 | tf_op jit(solution)/shard_map/pallas_call | solution.py:138
  7.7 1.2 %slice.101 = f32[1,1,1]{2,1,0:T(1,128)} slice(f32[16,56,128]{2,1,0:T(8,128)} %shard_map.73), slice={[0:1], [54:55], [0:1]} | slice | bytes 8 | tf_op jit(solution)/shard_map/slice | solution.py:306
  10.0 0.1 collective-permute-start.3
  10.1 0.6 broadcast_select_fusion
  10.7 4.0 %collective-permute-start.5 = (f32[512,128]{1,0:T(8,128)S(1)}, f32[512,128]{1,0:T(8,128)S(1)}, u32[]{:S(2)}, u32[]{:S(2)}) collective-permute-start(f32[512,128]{1,0:T(8,128)S(1)} %broadcast_select_fusion), channel_id=1, source_target_pairs={{0,8},{8,16},{16,24},{24,32},{32,40},{40,48},{48,56},{56,0},{1,57}... | collective-permute-start | bytes 786440 | tf_op jit(solution)/shard_map/ppermute | solution.py:309
  14.7 1.1 %collective-permute-done.3.refs_4_ = f32[512,128]{1,0:T(8,128)S(1)} collective-permute-done((f32[512,128]{1,0:T(8,128)S(1)}, f32[512,128]{1,0:T(8,128)S(1)}, u32[]{:S(2)}, u32[]{:S(2)}) %collective-permute-start.3) | collective-permute-done | bytes 262176 | tf_op jit(solution)/shard_map/ppermute | solution.py:309
  15.8 1.6 %collective-permute-start.7 = (f32[512,128]{1,0:T(8,128)S(1)}, f32[512,128]{1,0:T(8,128)S(1)}, u32[]{:S(2)}, u32[]{:S(2)}) collective-permute-start(f32[512,128]{1,0:T(8,128)S(1)} %collective-permute-done.3.refs_4_), channel_id=1, source_target_pairs={{0,8},{8,16},{16,24},{24,32},{32,40},{40,48},{48,56},{56,0},{1,57}... | collective-permute-start | bytes 786440 | tf_op jit(solution)/shard_map/ppermute | solution.py:309
  17.3 1.2 %collective-permute-done.5.refs_6_ = f32[512,128]{1,0:T(8,128)S(1)} collective-permute-done((f32[512,128]{1,0:T(8,128)S(1)}, f32[512,128]{1,0:T(8,128)S(1)}, u32[]{:S(2)}, u32[]{:S(2)}) %collective-permute-start.5) | collective-permute-done | bytes 262176 | tf_op jit(solution)/shard_map/ppermute | solution.py:309
  18.6 1.6 %collective-permute-start.9 = (f32[512,128]{1,0:T(8,128)S(1)}, f32[512,128]{1,0:T(8,128)S(1)}, u32[]{:S(2)}, u32[]{:S(2)}) collective-permute-start(f32[512,128]{1,0:T(8,128)S(1)} %collective-permute-done.5.refs_6_), channel_id=1, source_target_pairs={{0,8},{8,16},{16,24},{24,32},{32,40},{40,48},{48,56},{56,0},{1,57}... | collective-permute-start | bytes 786440 | tf_op jit(solution)/shard_map/ppermute | solution.py:309
  20.1 6.9 %all-to-all-start = ((f32[16,56,128]{2,1,0:T(8,128)}), f32[16,56,128]{2,1,0:T(8,128)S(1)}, u32[]{:S(2)}, u32[]{:S(2)}) async-start(f32[16,56,128]{2,1,0:T(8,128)} %shard_map.73), calls=%async_computation | async-start | bytes 917504 | tf_op jit(solution)/shard_map/all_to_all | solution.py:349
  27.0 3.5 %collective-permute-start.2 = (f32[512,128]{1,0:T(8,128)S(1)}, f32[512,128]{1,0:T(8,128)S(1)}, u32[]{:S(2)}, u32[]{:S(2)}) collective-permute-start(f32[512,128]{1,0:T(8,128)S(1)} %collective-permute-done.1.refs_2_), channel_id=1, source_target_pairs={{0,1},{1,0},{2,3},{3,2},{4,5},{5,4},{6,7},{7,6},{8,9},{9,8},{10,11... | collective-permute-start | bytes 786440 | tf_op jit(solution)/shard_map/ppermute | solution.py:265
  30.5 0.1 collective-permute-start.4
  30.6 1.3 %collective-permute-start.13 = (f32[512,128]{1,0:T(8,128)S(1)}, f32[512,128]{1,0:T(8,128)S(1)}, u32[]{:S(2)}, u32[]{:S(2)}) collective-permute-start(f32[512,128]{1,0:T(8,128)S(1)} %collective-permute-done.9.refs_10_), channel_id=1, source_target_pairs={{0,8},{8,16},{16,24},{24,32},{32,40},{40,48},{48,56},{56,0},{1,57}... | collective-permute-start | bytes 786440 | tf_op jit(solution)/shard_map/ppermute | solution.py:309
  32.0 2.0 %collective-permute-start.6 = (f32[512,128]{1,0:T(8,128)S(1)}, f32[512,128]{1,0:T(8,128)}, u32[]{:S(2)}, u32[]{:S(2)}) collective-permute-start(f32[512,128]{1,0:T(8,128)S(1)} %collective-permute-done.5.refs_6_), channel_id=1, source_target_pairs={{0,1},{1,0},{2,3},{3,2},{4,5},{5,4},{6,7},{7,6},{8,9},{9,8},{10,11... | collective-permute-start | bytes 786440 | tf_op jit(solution)/shard_map/ppermute | solution.py:265
  34.0 0.1 collective-permute-start.8
  34.1 0.4 collective-permute-start.10
  34.5 2.7 %collective-permute-done.11.refs_12_ = f32[512,128]{1,0:T(8,128)S(1)} collective-permute-done((f32[512,128]{1,0:T(8,128)S(1)}, f32[512,128]{1,0:T(8,128)S(1)}, u32[]{:S(2)}, u32[]{:S(2)}) %collective-permute-start.11) | collective-permute-done | bytes 262176 | tf_op jit(solution)/shard_map/ppermute | solution.py:309
  37.2 0.5 collective-permute-start.12
  37.7 2.1 %collective-permute-done.13.refs_14_ = f32[512,128]{1,0:T(8,128)S(1)} collective-permute-done((f32[512,128]{1,0:T(8,128)S(1)}, f32[512,128]{1,0:T(8,128)S(1)}, u32[]{:S(2)}, u32[]{:S(2)}) %collective-permute-start.13) | collective-permute-done | bytes 262176 | tf_op jit(solution)/shard_map/ppermute | solution.py:309
  39.8 0.7 collective-permute-start.14
  40.5 0.1 copy.9
  40.6 0.1 convert_element_type.17.count_ref
  40.8 1.0 %collective-permute-done.14.refs_15_ = f32[512,128]{1,0:T(8,128)} collective-permute-done((f32[512,128]{1,0:T(8,128)S(1)}, f32[512,128]{1,0:T(8,128)}, u32[]{:S(2)}, u32[]{:S(2)}) %collective-permute-start.14) | collective-permute-done | bytes 262176 | tf_op jit(solution)/shard_map/ppermute | solution.py:265
  41.8 1.6 %shard_map.74.table_ref = f32[8192,128]{1,0:T(8,128)S(1)} custom-call(f32[512,128]{1,0:T(8,128)S(1)} %bitcast.52, f32[512,128]{1,0:T(8,128)S(1)} %collective-permute-done.after_ref.refs_1_, f32[512,128]{1,0:T(8,128)S(1)} %collective-permute-done.1.refs_2_, f32[512,128]{1,0:T(8,128)S(1)} %collective-permute-done.2.refs_3_, ...), custom_call_target="tpu_custom_call" | custom-call | tf_op jit(solution)/shard_map/pallas_call | solution.py:314
  43.4 4.4 %shard_map.75.rest_0_ = f32[4,512,128]{2,1,0:T(8,128)S(1)} custom-call(s32[3]{0:T(128)S(1)} %pad_add_fusion.place_ref, s32[32]{0:T(128)S(1)} %convert_element_type.17.count_ref, s32[8192]{0:T(1024)S(1)} %bitcast.47, f32[8192]{0:T(1024)S(1)} %bitcast.44, f32[16,56,128]{2,1,0:T(8,128)S(1)} %all-to-all-done.list_ref, f32[8192,128]{1,0:T(8,128)S(1)} %shard_map.74.table_ref), custom_call_target="tpu_custom_call" | custom-call | bytes 10485760 | tf_op jit(solution)/shard_map/pallas_call | solution.py:246
  47.8 1.2 %collective-permute-start.15 = (f32[4,512,128]{2,1,0:T(8,128)S(1)}, f32[4,512,128]{2,1,0:T(8,128)S(1)}, u32[]{:S(2)}, u32[]{:S(2)}) collective-permute-start(f32[4,512,128]{2,1,0:T(8,128)S(1)} %shard_map.75.rest_0_), channel_id=1, source_target_pairs={{0,128},{1,5},{2,130},{3,7},{4,132},{5,1},{6,134},{7,3},{64,192},{... | collective-permute-start | bytes 3145736 | tf_op jit(solution)/shard_map/ppermute | solution.py:367
  49.0 6.9 %shard_map.77 = (f32[4,512,128]{2,1,0:T(8,128)S(1)}, f32[4,512,128]{2,1,0:T(8,128)S(1)}) custom-call(s32[3]{0:T(128)S(1)} %pad_add_fusion.place_ref, s32[32]{0:T(128)S(1)} %convert_element_type.17.count_ref, s32[8192]{0:T(1024)S(1)} %bitcast.48, f32[8192]{0:T(1024)S(1)} %bitcast.45, f32[16,56,128]{2,1,0:T(8,128)S(1)} %all-to-all-done.list_ref, ...), custom_call_target="tpu_custom_call" | custom-call | bytes 41943040 | tf_op jit(solution)/shard_map/pallas_call | solution.py:246
  55.8 0.1 collective-permute-start.17
  55.9 2.7 %collective-permute-start.16 = (f32[4,512,128]{2,1,0:T(8,128)S(1)}, f32[4,512,128]{2,1,0:T(8,128)S(1)}, u32[]{:S(2)}, u32[]{:S(2)}) collective-permute-start(f32[4,512,128]{2,1,0:T(8,128)S(1)} %get-tuple-element.7), channel_id=1, source_target_pairs={{0,64},{1,3},{2,66},{3,5},{4,68},{5,7},{6,70},{7,1},{64,128},{65,6... | collective-permute-start | bytes 3145736 | tf_op jit(solution)/shard_map/ppermute | solution.py:367
  58.6 4.8 %collective-permute-done.15.rest_0_ = f32[4,512,128]{2,1,0:T(8,128)S(1)} collective-permute-done((f32[4,512,128]{2,1,0:T(8,128)S(1)}, f32[4,512,128]{2,1,0:T(8,128)S(1)}, u32[]{:S(2)}, u32[]{:S(2)}) %collective-permute-start.15) | collective-permute-done | bytes 1048608 | tf_op jit(solution)/shard_map/ppermute | solution.py:367
  63.4 4.3 %shard_map.76.earlier_ref = f32[4,512,128]{2,1,0:T(8,128)S(1)} custom-call(s32[3]{0:T(128)S(1)} %pad_add_fusion.place_ref, s32[32]{0:T(128)S(1)} %convert_element_type.17.count_ref, s32[8192]{0:T(1024)S(1)} %bitcast.49, f32[8192]{0:T(1024)S(1)} %bitcast.46, f32[16,56,128]{2,1,0:T(8,128)S(1)} %all-to-all-done.list_ref, f32[8192,128]{1,0:T(8,128)S(1)} %shard_map.74.table_ref, ...), custom_call_target="tpu_custom_call" | custom-call | bytes 41943040 | tf_op jit(solution)/shard_map/pallas_call | solution.py:246
  67.7 6.9 %collective-permute-done.17 = f32[4,512,128]{2,1,0:T(8,128)S(1)} collective-permute-done((f32[4,512,128]{2,1,0:T(8,128)S(1)}, f32[4,512,128]{2,1,0:T(8,128)S(1)}, u32[]{:S(2)}, u32[]{:S(2)}) %collective-permute-start.17) | collective-permute-done | bytes 1048608 | tf_op jit(solution)/shard_map/ppermute | solution.py:367
  74.6 0.2 fusion.2
  74.8 2.4 %collective-permute-start.20 = (f32[512,128]{1,0:T(8,128)S(1)}, f32[512,128]{1,0:T(8,128)S(1)}, u32[]{:S(2)}, u32[]{:S(2)}) collective-permute-start(f32[512,128]{1,0:T(8,128)S(1)} %get-tuple-element.10), channel_id=1, source_target_pairs={{0,6},{1,193},{2,0},{3,195},{4,2},{5,197},{6,4},{7,199},{64,70},{6... | collective-permute-start | bytes 786440 | tf_op jit(solution)/shard_map/ppermute | solution.py:367
  77.2 1.6 %collective-permute-start.18 = (f32[512,128]{1,0:T(8,128)S(1)}, f32[512,128]{1,0:T(8,128)S(1)}, u32[]{:S(2)}, u32[]{:S(2)}) collective-permute-start(f32[512,128]{1,0:T(8,128)S(1)} %get-tuple-element.9), channel_id=1, source_target_pairs={{0,4},{1,129},{2,6},{3,131},{4,0},{5,133},{6,2},{7,135},{64,68},{6... | collective-permute-start | bytes 786440 | tf_op jit(solution)/shard_map/ppermute | solution.py:367
  78.8 0.7 fusion.8
  79.5 6.2 %collective-permute-start.22 = (f32[2,3,1,64,128]{4,3,2,1,0:T(8,128)}, f32[2,3,1,64,128]{4,3,2,1,0:T(8,128)S(1)}, u32[]{:S(2)}, u32[]{:S(2)}) collective-permute-start(f32[2,3,1,64,128]{4,3,2,1,0:T(8,128)} %get-tuple-element.13), channel_id=1, source_target_pairs={{0,1},{1,2},{2,3},{3,4},{4,5},{5,6},{6,7},{7,8},{8,9},{9,10},{10,1... | collective-permute-start | bytes 589832 | tf_op jit(solution)/shard_map/ppermute | solution.py:328
  85.7 1.9 %collective-permute-start.23 = (f32[2,3,1,64,128]{4,3,2,1,0:T(8,128)S(1)}, f32[2,3,1,64,128]{4,3,2,1,0:T(8,128)S(1)}, u32[]{:S(2)}, u32[]{:S(2)}) collective-permute-start(f32[2,3,1,64,128]{4,3,2,1,0:T(8,128)S(1)} %get-tuple-element.12), channel_id=1, source_target_pairs={{1,0},{2,1},{3,2},{4,3},{5,4},{6,5},{7,6},{8,7},{9,8},{10,9},{11,1... | collective-permute-start | bytes 589832 | tf_op jit(solution)/shard_map/ppermute | solution.py:328
  87.7 0.1 fusion.6
  87.8 7.8 %collective-permute-start.21 = (f32[64,128]{1,0:T(8,128)S(1)}, f32[64,128]{1,0:T(8,128)S(1)}, u32[]{:S(2)}, u32[]{:S(2)}) collective-permute-start(f32[64,128]{1,0:T(8,128)S(1)} %slice_exponential_fusion), channel_id=1, source_target_pairs={{0,1},{1,2},{2,3},{3,4},{4,5},{5,6},{6,7},{7,8},{8,9},{9,10},{10,1... | collective-permute-start | bytes 98312 | tf_op jit(solution)/shard_map/ppermute | solution.py:328
  96.3 1.4 %copy-done.1 = f32[1,2,3,8,64,128]{5,4,3,2,1,0:T(8,128)S(1)} copy-done((f32[1,2,3,8,64,128]{5,4,3,2,1,0:T(8,128)S(1)}, f32[1,2,3,8,64,128]{5,4,3,2,1,0:T(8,128)}, u32[]{:S(2)}) %copy-start.1) | copy-done | bytes 1572888
  97.7 1.4 %shard_map.78.rest_ref = f32[2,3,8,64,128]{4,3,2,1,0:T(8,128)S(1)} custom-call(f32[1]{0:T(128)} %bitcast.21.rim_ref, f32[2,3,8,64,128]{4,3,2,1,0:T(8,128)S(1)} %bitcast.40, f32[2,3,1,64,128]{4,3,2,1,0:T(8,128)S(1)} %collective-permute-done.22.before_ref, f32[2,3,1,64,128]{4,3,2,1,0:T(8,128)S(1)} %collective-permute-done.23.after_ref, ...), custom_call_target="tpu_custom_call" | custom-call | bytes 12582912 | tf_op jit(solution)/shard_map/pallas_call | solution.py:433
  99.1 1.4 %shard_map.79 = f32[2,3,8,64,128]{4,3,2,1,0:T(8,128)} custom-call(f32[1]{0:T(128)S(6)} %copy.10.omega_ref, f32[8,64,128]{2,1,0:T(8,128)S(1)} %bitcast.43, f32[64,128]{1,0:T(8,128)S(1)} %fusion.7.prior_ref, f32[2,3,8,64,128]{4,3,2,1,0:T(8,128)S(1)} %shard_map.78.rest_ref, f32[2,3,8,64,128]{4,3,2,1,0:T(8,128)S(1)} %bitcast.41), custom_call_target="tpu_custom_call" | custom-call | tf_op jit(solution)/shard_map/pallas_call | solution.py:466
  (34 shorter events, 0.3 us)
Async XLA Ops:
  0.0 41.8 %copy-start.2 = (f32[512,1,128]{2,1,0:T(1,128)S(1)}, f32[512,1,128]{2,1,0:T(1,128)}, u32[]{:S(2)}) copy-start(f32[512,1,128]{2,1,0:T(1,128)} %param.7) | copy-start | bytes 786436
  0.0 2.0 %collective-permute-start = (f32[512,128]{1,0:T(8,128)}, f32[512,128]{1,0:T(8,128)S(1)}, u32[]{:S(2)}, u32[]{:S(2)}) collective-permute-start(f32[512,128]{1,0:T(8,128)} %bitcast.50), channel_id=1, source_target_pairs={{0,1},{1,0},{2,3},{3,2},{4,5},{5,4},{6,7},{7,6},{8,9},{9,8},{10,11... | collective-permute-start | bytes 786440 | tf_op jit(solution)/shard_map/ppermute | solution.py:265
  0.7 9.4 %collective-permute-start.1 = (f32[512,128]{1,0:T(8,128)}, f32[512,128]{1,0:T(8,128)S(1)}, u32[]{:S(2)}, u32[]{:S(2)}) collective-permute-start(f32[512,128]{1,0:T(8,128)} %bitcast.51), channel_id=1, source_target_pairs={{0,8},{8,16},{16,24},{24,32},{32,40},{40,48},{48,56},{56,0},{1,57}... | collective-permute-start | bytes 786440 | tf_op jit(solution)/shard_map/ppermute | solution.py:309
  2.1 0.7 copy-start.3
  2.8 0.7 copy-start.4
  3.5 0.7 copy-start.5
  10.0 5.8 %collective-permute-start.3 = (f32[512,128]{1,0:T(8,128)S(1)}, f32[512,128]{1,0:T(8,128)S(1)}, u32[]{:S(2)}, u32[]{:S(2)}) collective-permute-start(f32[512,128]{1,0:T(8,128)S(1)} %collective-permute-done.after_ref.refs_1_), channel_id=1, source_target_pairs={{0,8},{8,16},{16,24},{24,32},{32,40},{40,48},{48,56},{56,0},{1,57}... | collective-permute-start | bytes 786440 | tf_op jit(solution)/shard_map/ppermute | solution.py:309
  10.7 7.9 %collective-permute-start.5 = (f32[512,128]{1,0:T(8,128)S(1)}, f32[512,128]{1,0:T(8,128)S(1)}, u32[]{:S(2)}, u32[]{:S(2)}) collective-permute-start(f32[512,128]{1,0:T(8,128)S(1)} %broadcast_select_fusion), channel_id=1, source_target_pairs={{0,8},{8,16},{16,24},{24,32},{32,40},{40,48},{48,56},{56,0},{1,57}... | collective-permute-start | bytes 786440 | tf_op jit(solution)/shard_map/ppermute | solution.py:309
  15.8 14.8 %collective-permute-start.7 = (f32[512,128]{1,0:T(8,128)S(1)}, f32[512,128]{1,0:T(8,128)S(1)}, u32[]{:S(2)}, u32[]{:S(2)}) collective-permute-start(f32[512,128]{1,0:T(8,128)S(1)} %collective-permute-done.3.refs_4_), channel_id=1, source_target_pairs={{0,8},{8,16},{16,24},{24,32},{32,40},{40,48},{48,56},{56,0},{1,57}... | collective-permute-start | bytes 786440 | tf_op jit(solution)/shard_map/ppermute | solution.py:309
  18.6 12.0 %collective-permute-start.9 = (f32[512,128]{1,0:T(8,128)S(1)}, f32[512,128]{1,0:T(8,128)S(1)}, u32[]{:S(2)}, u32[]{:S(2)}) collective-permute-start(f32[512,128]{1,0:T(8,128)S(1)} %collective-permute-done.5.refs_6_), channel_id=1, source_target_pairs={{0,8},{8,16},{16,24},{24,32},{32,40},{40,48},{48,56},{56,0},{1,57}... | collective-permute-start | bytes 786440 | tf_op jit(solution)/shard_map/ppermute | solution.py:309
  20.1 20.4 %all-to-all-start = ((f32[16,56,128]{2,1,0:T(8,128)}), f32[16,56,128]{2,1,0:T(8,128)S(1)}, u32[]{:S(2)}, u32[]{:S(2)}) async-start(f32[16,56,128]{2,1,0:T(8,128)} %shard_map.73), calls=%async_computation | async-start | bytes 917504 | tf_op jit(solution)/shard_map/all_to_all | solution.py:349
  27.0 7.0 %collective-permute-start.2 = (f32[512,128]{1,0:T(8,128)S(1)}, f32[512,128]{1,0:T(8,128)S(1)}, u32[]{:S(2)}, u32[]{:S(2)}) collective-permute-start(f32[512,128]{1,0:T(8,128)S(1)} %collective-permute-done.1.refs_2_), channel_id=1, source_target_pairs={{0,1},{1,0},{2,3},{3,2},{4,5},{5,4},{6,7},{7,6},{8,9},{9,8},{10,11... | collective-permute-start | bytes 786440 | tf_op jit(solution)/shard_map/ppermute | solution.py:265
  30.5 3.6 %collective-permute-start.4 = (f32[512,128]{1,0:T(8,128)S(1)}, f32[512,128]{1,0:T(8,128)S(1)}, u32[]{:S(2)}, u32[]{:S(2)}) collective-permute-start(f32[512,128]{1,0:T(8,128)S(1)} %collective-permute-done.3.refs_4_), channel_id=1, source_target_pairs={{0,1},{1,0},{2,3},{3,2},{4,5},{5,4},{6,7},{7,6},{8,9},{9,8},{10,11... | collective-permute-start | bytes 786440 | tf_op jit(solution)/shard_map/ppermute | solution.py:265
  30.6 6.6 %collective-permute-start.11 = (f32[512,128]{1,0:T(8,128)S(1)}, f32[512,128]{1,0:T(8,128)S(1)}, u32[]{:S(2)}, u32[]{:S(2)}) collective-permute-start(f32[512,128]{1,0:T(8,128)S(1)} %collective-permute-done.7.refs_8_), channel_id=1, source_target_pairs={{0,8},{8,16},{16,24},{24,32},{32,40},{40,48},{48,56},{56,0},{1,57}... | collective-permute-start | bytes 786440 | tf_op jit(solution)/shard_map/ppermute | solution.py:309
  30.6 9.2 %collective-permute-start.13 = (f32[512,128]{1,0:T(8,128)S(1)}, f32[512,128]{1,0:T(8,128)S(1)}, u32[]{:S(2)}, u32[]{:S(2)}) collective-permute-start(f32[512,128]{1,0:T(8,128)S(1)} %collective-permute-done.9.refs_10_), channel_id=1, source_target_pairs={{0,8},{8,16},{16,24},{24,32},{32,40},{40,48},{48,56},{56,0},{1,57}... | collective-permute-start | bytes 786440 | tf_op jit(solution)/shard_map/ppermute | solution.py:309
  32.0 8.7 %collective-permute-start.6 = (f32[512,128]{1,0:T(8,128)S(1)}, f32[512,128]{1,0:T(8,128)}, u32[]{:S(2)}, u32[]{:S(2)}) collective-permute-start(f32[512,128]{1,0:T(8,128)S(1)} %collective-permute-done.5.refs_6_), channel_id=1, source_target_pairs={{0,1},{1,0},{2,3},{3,2},{4,5},{5,4},{6,7},{7,6},{8,9},{9,8},{10,11... | collective-permute-start | bytes 786440 | tf_op jit(solution)/shard_map/ppermute | solution.py:265
  34.0 6.7 %collective-permute-start.8 = (f32[512,128]{1,0:T(8,128)S(1)}, f32[512,128]{1,0:T(8,128)}, u32[]{:S(2)}, u32[]{:S(2)}) collective-permute-start(f32[512,128]{1,0:T(8,128)S(1)} %collective-permute-done.7.refs_8_), channel_id=1, source_target_pairs={{0,1},{1,0},{2,3},{3,2},{4,5},{5,4},{6,7},{7,6},{8,9},{9,8},{10,11... | collective-permute-start | bytes 786440 | tf_op jit(solution)/shard_map/ppermute | solution.py:265
  34.1 6.6 %collective-permute-start.10 = (f32[512,128]{1,0:T(8,128)S(1)}, f32[512,128]{1,0:T(8,128)}, u32[]{:S(2)}, u32[]{:S(2)}) collective-permute-start(f32[512,128]{1,0:T(8,128)S(1)} %collective-permute-done.9.refs_10_), channel_id=1, source_target_pairs={{0,1},{1,0},{2,3},{3,2},{4,5},{5,4},{6,7},{7,6},{8,9},{9,8},{10,11... | collective-permute-start | bytes 786440 | tf_op jit(solution)/shard_map/ppermute | solution.py:265
  37.2 3.6 %collective-permute-start.12 = (f32[512,128]{1,0:T(8,128)S(1)}, f32[512,128]{1,0:T(8,128)}, u32[]{:S(2)}, u32[]{:S(2)}) collective-permute-start(f32[512,128]{1,0:T(8,128)S(1)} %collective-permute-done.11.refs_12_), channel_id=1, source_target_pairs={{0,1},{1,0},{2,3},{3,2},{4,5},{5,4},{6,7},{7,6},{8,9},{9,8},{10,11... | collective-permute-start | bytes 786440 | tf_op jit(solution)/shard_map/ppermute | solution.py:265
  39.8 2.0 %collective-permute-start.14 = (f32[512,128]{1,0:T(8,128)S(1)}, f32[512,128]{1,0:T(8,128)}, u32[]{:S(2)}, u32[]{:S(2)}) collective-permute-start(f32[512,128]{1,0:T(8,128)S(1)} %collective-permute-done.13.refs_14_), channel_id=1, source_target_pairs={{0,1},{1,0},{2,3},{3,2},{4,5},{5,4},{6,7},{7,6},{8,9},{9,8},{10,11... | collective-permute-start | bytes 786440 | tf_op jit(solution)/shard_map/ppermute | solution.py:265
  47.8 15.6 %collective-permute-start.15 = (f32[4,512,128]{2,1,0:T(8,128)S(1)}, f32[4,512,128]{2,1,0:T(8,128)S(1)}, u32[]{:S(2)}, u32[]{:S(2)}) collective-permute-start(f32[4,512,128]{2,1,0:T(8,128)S(1)} %shard_map.75.rest_0_), channel_id=1, source_target_pairs={{0,128},{1,5},{2,130},{3,7},{4,132},{5,1},{6,134},{7,3},{64,192},{... | collective-permute-start | bytes 3145736 | tf_op jit(solution)/shard_map/ppermute | solution.py:367
  55.8 18.7 %collective-permute-start.17 = (f32[4,512,128]{2,1,0:T(8,128)S(1)}, f32[4,512,128]{2,1,0:T(8,128)S(1)}, u32[]{:S(2)}, u32[]{:S(2)}) collective-permute-start(f32[4,512,128]{2,1,0:T(8,128)S(1)} %get-tuple-element.8), channel_id=1, source_target_pairs={{0,192},{1,7},{2,194},{3,1},{4,196},{5,3},{6,198},{7,5},{64,0},{65... | collective-permute-start | bytes 3145736 | tf_op jit(solution)/shard_map/ppermute | solution.py:367
  55.9 18.6 %collective-permute-start.16 = (f32[4,512,128]{2,1,0:T(8,128)S(1)}, f32[4,512,128]{2,1,0:T(8,128)S(1)}, u32[]{:S(2)}, u32[]{:S(2)}) collective-permute-start(f32[4,512,128]{2,1,0:T(8,128)S(1)} %get-tuple-element.7), channel_id=1, source_target_pairs={{0,64},{1,3},{2,66},{3,5},{4,68},{5,7},{6,70},{7,1},{64,128},{65,6... | collective-permute-start | bytes 3145736 | tf_op jit(solution)/shard_map/ppermute | solution.py:367
  67.6 11.2 %copy-start = (f32[1,2,3,8,64,128]{5,4,3,2,1,0:T(8,128)S(1)}, f32[1,2,3,8,64,128]{5,4,3,2,1,0:T(8,128)}, u32[]{:S(2)}) copy-start(f32[1,2,3,8,64,128]{5,4,3,2,1,0:T(8,128)} %param.11) | copy-start | bytes 4718596
  74.8 12.8 %collective-permute-start.20 = (f32[512,128]{1,0:T(8,128)S(1)}, f32[512,128]{1,0:T(8,128)S(1)}, u32[]{:S(2)}, u32[]{:S(2)}) collective-permute-start(f32[512,128]{1,0:T(8,128)S(1)} %get-tuple-element.10), channel_id=1, source_target_pairs={{0,6},{1,193},{2,0},{3,195},{4,2},{5,197},{6,4},{7,199},{64,70},{6... | collective-permute-start | bytes 786440 | tf_op jit(solution)/shard_map/ppermute | solution.py:367
  77.2 10.4 %collective-permute-start.19 = (f32[512,128]{1,0:T(8,128)S(1)}, f32[512,128]{1,0:T(8,128)S(1)}, u32[]{:S(2)}, u32[]{:S(2)}) collective-permute-start(f32[512,128]{1,0:T(8,128)S(1)} %get-tuple-element.11), channel_id=1, source_target_pairs={{0,2},{1,65},{2,4},{3,67},{4,6},{5,69},{6,0},{7,71},{64,66},{65,12... | collective-permute-start | bytes 786440 | tf_op jit(solution)/shard_map/ppermute | solution.py:367
  77.2 10.4 %collective-permute-start.18 = (f32[512,128]{1,0:T(8,128)S(1)}, f32[512,128]{1,0:T(8,128)S(1)}, u32[]{:S(2)}, u32[]{:S(2)}) collective-permute-start(f32[512,128]{1,0:T(8,128)S(1)} %get-tuple-element.9), channel_id=1, source_target_pairs={{0,4},{1,129},{2,6},{3,131},{4,0},{5,133},{6,2},{7,135},{64,68},{6... | collective-permute-start | bytes 786440 | tf_op jit(solution)/shard_map/ppermute | solution.py:367
  79.5 16.7 %collective-permute-start.22 = (f32[2,3,1,64,128]{4,3,2,1,0:T(8,128)}, f32[2,3,1,64,128]{4,3,2,1,0:T(8,128)S(1)}, u32[]{:S(2)}, u32[]{:S(2)}) collective-permute-start(f32[2,3,1,64,128]{4,3,2,1,0:T(8,128)} %get-tuple-element.13), channel_id=1, source_target_pairs={{0,1},{1,2},{2,3},{3,4},{4,5},{5,6},{6,7},{7,8},{8,9},{9,10},{10,1... | collective-permute-start | bytes 589832 | tf_op jit(solution)/shard_map/ppermute | solution.py:328
  85.7 10.5 %collective-permute-start.23 = (f32[2,3,1,64,128]{4,3,2,1,0:T(8,128)S(1)}, f32[2,3,1,64,128]{4,3,2,1,0:T(8,128)S(1)}, u32[]{:S(2)}, u32[]{:S(2)}) collective-permute-start(f32[2,3,1,64,128]{4,3,2,1,0:T(8,128)S(1)} %get-tuple-element.12), channel_id=1, source_target_pairs={{1,0},{2,1},{3,2},{4,3},{5,4},{6,5},{7,6},{8,7},{9,8},{10,9},{11,1... | collective-permute-start | bytes 589832 | tf_op jit(solution)/shard_map/ppermute | solution.py:328
  87.8 11.2 %collective-permute-start.21 = (f32[64,128]{1,0:T(8,128)S(1)}, f32[64,128]{1,0:T(8,128)S(1)}, u32[]{:S(2)}, u32[]{:S(2)}) collective-permute-start(f32[64,128]{1,0:T(8,128)S(1)} %slice_exponential_fusion), channel_id=1, source_target_pairs={{0,1},{1,2},{2,3},{3,4},{4,5},{5,6},{6,7},{7,8},{8,9},{9,10},{10,1... | collective-permute-start | bytes 98312 | tf_op jit(solution)/shard_map/ppermute | solution.py:328
  96.3 1.4 %copy-start.1 = (f32[1,2,3,8,64,128]{5,4,3,2,1,0:T(8,128)S(1)}, f32[1,2,3,8,64,128]{5,4,3,2,1,0:T(8,128)}, u32[]{:S(2)}) copy-start(f32[1,2,3,8,64,128]{5,4,3,2,1,0:T(8,128)} %param.12) | copy-start | bytes 4718596

commit v5 on v4

--- a/solution.py
+++ b/solution.py
@@ -265,9 +265,16 @@
     return lax.ppermute(value, axis, [(i, (i + by) % count) for i in range(count)])
 
 
-def ordered(value, earlier):
-    probe = earlier.reshape(-1)[0]
-    return jnp.where(probe != probe, probe, value)
+def ordered(value, *earlier):
+    anywhere = pl.BlockSpec(memory_space=pl.ANY)
+    return pl.pallas_call(
+        lambda *refs: None,
+        in_specs=[anywhere] * (1 + len(earlier)),
+        out_specs=anywhere,
+        out_shape=jax.ShapeDtypeStruct(value.shape, value.dtype),
+        input_output_aliases={0: 0},
+        compiler_params=pltpu.CompilerParams(vmem_limit_bytes=1024 * 1024),
+    )(value, *earlier)
 
 
 def assemble_kernel(spots, *refs):
@@ -302,11 +309,14 @@
     take(mate, nz)
     pair = [own, mate]
     for step in range(1, nz // 2 + 1):
-        if step == 2:
-            pair[0] = ordered(pair[0], lists[0, -2, :1])
         if step == nz // 2:
             pair = pair[:1]
         pair = [lax.ppermute(one, ("z", "c"), onward) for one in pair]
+        if step == 1:
+            pair[0] = ordered(pair[0], lists)
+        elif step < nz // 2:
+            pair[0] = ordered(pair[0], mates)
+        mates = pair[-1]
         for core, one in enumerate(pair):
             take(one, core * nz + step)
             take(swapped(one), (1 - core) * nz + nz - step)

time: 101 us -> 96.9 us (0.959)
  the two profiles are of different devices: /device:TPU:71 before, /device:TPU:56 now
where the time goes in v5:
time: 96.9 us; the launch traced here: 95.8 us
  starting transfers between devices  42.3 us (44%)
  waiting for transfers between devices  24.5 us (25%)
  Pallas kernels  22.9 us (24%)
  local copies, waits for them, and re-layouts  4.46 us (5%)
  between operations  1.07 us (1%)
    pallas_call x3, Pallas kernels, partial_sums(): pl.pallas_call(functools.partial(partials_kernel, [job[:2] for job in job...  15.1 us
    ppermute x7, starting transfers between devices, gathered(): pair = [lax.ppermute(one, ('z', 'c'), onward) for one in pair]  15.1 us
    ppermute x6, waiting for transfers between devices, sent(): return lax.ppermute(value, ('y', 'x', 'c'), pairs)  14.3 us
    ppermute x3, starting transfers between devices, shifted(): return lax.ppermute(shard, axis, pairs)  9.58 us
    ppermute x6, starting transfers between devices, sent(): return lax.ppermute(value, ('y', 'x', 'c'), pairs)  9.39 us
    all_to_all x1, starting transfers between devices, log_conductivity(): lax.all_to_all(lists, ('y', 'x'), split_axis=0, concat_axis=0, tiled=True)  7.17 us
    ppermute x7, waiting for transfers between devices, gathered(): pair = [lax.ppermute(one, ('z', 'c'), onward) for one in pair]  6.81 us
    unnamed x12, local copies, waits for them, and re-layouts  3.57 us
  transfers between devices with their start and end apart: 25, of which 8 were waited for; matrix products, arithmetic and copies ran while one was open for 1% of the time, Pallas kernels for 16%

profile of v5, /device:TPU:56, one launch (start us, length us, event | category | flops | bytes accessed | tf_op | source)
XLA Modules:
  0.0 95.8 jit_solution(6019622219705169504)
XLA Ops:
  0.0 1.9 %collective-permute-start.1 = (f32[512,128]{1,0:T(8,128)}, f32[512,128]{1,0:T(8,128)S(1)}, u32[]{:S(2)}, u32[]{:S(2)}) collective-permute-start(f32[512,128]{1,0:T(8,128)} %bitcast.50), channel_id=1, source_target_pairs={{0,8},{8,16},{16,24},{24,32},{32,40},{40,48},{48,56},{56,0},{1,57}... | collective-permute-start | bytes 786440 | tf_op jit(solution)/shard_map/ppermute | solution.py:314
  1.9 0.1 pad_add_fusion.1.here_ref
  2.0 1.9 %collective-permute-start.3 = (f32[512,128]{1,0:T(8,128)S(1)}, f32[512,128]{1,0:T(8,128)S(1)}, u32[]{:S(2)}, u32[]{:S(2)}) collective-permute-start(f32[512,128]{1,0:T(8,128)S(1)} %collective-permute-done.after_ref.refs_1_), channel_id=1, source_target_pairs={{0,8},{8,16},{16,24},{24,32},{32,40},{40,48},{48,56},{56,0},{1,57}... | collective-permute-start | bytes 786440 | tf_op jit(solution)/shard_map/ppermute | solution.py:314
  3.9 0.7 copy-done.3
  4.7 0.7 copy-done.4
  5.4 0.7 copy-done.5
  6.1 3.5 %shard_map.73.refs_1_ = f32[16,56,128]{2,1,0:T(8,128)} custom-call(s32[2]{0:T(128)S(1)} %pad_add_fusion.1.here_ref, s32[8,512]{1,0:T(8,128)S(1)} %bitcast.52, s32[8,512]{1,0:T(8,128)S(1)} %bitcast.53, f32[8,512]{1,0:T(8,128)S(1)} %bitcast.54, f32[512,128]{1,0:T(8,128)S(1)} %collective-permute-done.after_ref.refs_1_), custom_call_target="tpu_custom_call" | custom-call | bytes 12582912 | tf_op jit(solution)/shard_map/pallas_call | solution.py:138
  9.6 0.0 copy-start.2
  9.6 3.2 %collective-permute-start.5 = (f32[512,128]{1,0:T(8,128)S(1)}, f32[512,128]{1,0:T(8,128)S(1)}, u32[]{:S(2)}, u32[]{:S(2)}) collective-permute-start(f32[512,128]{1,0:T(8,128)S(1)} %shard_map.74.refs_2_), channel_id=1, source_target_pairs={{0,8},{8,16},{16,24},{24,32},{32,40},{40,48},{48,56},{56,0},{1,57}... | collective-permute-start | bytes 786440 | tf_op jit(solution)/shard_map/ppermute | solution.py:314
  12.8 1.7 %collective-permute-start.7 = (f32[512,128]{1,0:T(8,128)S(1)}, f32[512,128]{1,0:T(8,128)S(1)}, u32[]{:S(2)}, u32[]{:S(2)}) collective-permute-start(f32[512,128]{1,0:T(8,128)S(1)} %collective-permute-done.3.refs_1_.refs_4_), channel_id=1, source_target_pairs={{0,8},{8,16},{16,24},{24,32},{32,40},{40,48},{48,56},{56,0},{1,57}... | collective-permute-start | bytes 786440 | tf_op jit(solution)/shard_map/ppermute | solution.py:314
  14.5 2.2 %collective-permute-done.5.refs_0_ = f32[512,128]{1,0:T(8,128)S(1)} collective-permute-done((f32[512,128]{1,0:T(8,128)S(1)}, f32[512,128]{1,0:T(8,128)S(1)}, u32[]{:S(2)}, u32[]{:S(2)}) %collective-permute-start.5) | collective-permute-done | bytes 262176 | tf_op jit(solution)/shard_map/ppermute | solution.py:314
  16.7 2.5 %collective-permute-start.9 = (f32[512,128]{1,0:T(8,128)S(1)}, f32[512,128]{1,0:T(8,128)S(1)}, u32[]{:S(2)}, u32[]{:S(2)}) collective-permute-start(f32[512,128]{1,0:T(8,128)S(1)} %shard_map.75.refs_6_), channel_id=1, source_target_pairs={{0,8},{8,16},{16,24},{24,32},{32,40},{40,48},{48,56},{56,0},{1,57}... | collective-permute-start | bytes 786440 | tf_op jit(solution)/shard_map/ppermute | solution.py:314
  19.2 7.2 %all-to-all-start = ((f32[16,56,128]{2,1,0:T(8,128)}), f32[16,56,128]{2,1,0:T(8,128)S(1)}, u32[]{:S(2)}, u32[]{:S(2)}) async-start(f32[16,56,128]{2,1,0:T(8,128)} %shard_map.73.refs_1_), calls=%async_computation | async-start | bytes 917504 | tf_op jit(solution)/shard_map/all_to_all | solution.py:359
  26.4 0.5 collective-permute-start.4
  26.9 1.7 %collective-permute-start.11 = (f32[512,128]{1,0:T(8,128)S(1)}, f32[512,128]{1,0:T(8,128)S(1)}, u32[]{:S(2)}, u32[]{:S(2)}) collective-permute-start(f32[512,128]{1,0:T(8,128)S(1)} %collective-permute-done.7.refs_1_.refs_8_), channel_id=1, source_target_pairs={{0,8},{8,16},{16,24},{24,32},{32,40},{40,48},{48,56},{56,0},{1,57}... | collective-permute-start | bytes 786440 | tf_op jit(solution)/shard_map/ppermute | solution.py:314
  28.5 2.2 %collective-permute-start.13 = (f32[512,128]{1,0:T(8,128)S(1)}, f32[512,128]{1,0:T(8,128)S(1)}, u32[]{:S(2)}, u32[]{:S(2)}) collective-permute-start(f32[512,128]{1,0:T(8,128)S(1)} %shard_map.76.refs_10_), channel_id=1, source_target_pairs={{0,8},{8,16},{16,24},{24,32},{32,40},{40,48},{48,56},{56,0},{1,57}... | collective-permute-start | bytes 786440 | tf_op jit(solution)/shard_map/ppermute | solution.py:314
  30.7 0.1 pad_add_fusion.place_ref
  30.8 0.0 collective-permute-start.6
  30.9 0.5 collective-permute-start.10
  31.4 0.1 collective-permute-start.8
  31.5 1.8 %collective-permute-done.11.refs_12_ = f32[512,128]{1,0:T(8,128)S(1)} collective-permute-done((f32[512,128]{1,0:T(8,128)S(1)}, f32[512,128]{1,0:T(8,128)S(1)}, u32[]{:S(2)}, u32[]{:S(2)}) %collective-permute-start.11) | collective-permute-done | bytes 262176 | tf_op jit(solution)/shard_map/ppermute | solution.py:314
  33.2 2.8 %collective-permute-done.13.refs_14_ = f32[512,128]{1,0:T(8,128)S(1)} collective-permute-done((f32[512,128]{1,0:T(8,128)S(1)}, f32[512,128]{1,0:T(8,128)S(1)}, u32[]{:S(2)}, u32[]{:S(2)}) %collective-permute-start.13) | collective-permute-done | bytes 262176 | tf_op jit(solution)/shard_map/ppermute | solution.py:314
  36.1 0.1 copy.12
  36.2 0.1 convert_element_type.17.count_ref
  36.3 1.4 %collective-permute-done.14.refs_15_ = f32[512,128]{1,0:T(8,128)} collective-permute-done((f32[512,128]{1,0:T(8,128)S(1)}, f32[512,128]{1,0:T(8,128)}, u32[]{:S(2)}, u32[]{:S(2)}) %collective-permute-start.14) | collective-permute-done | bytes 262176 | tf_op jit(solution)/shard_map/ppermute | solution.py:265
  37.7 1.6 %shard_map.77.table_ref = f32[8192,128]{1,0:T(8,128)S(1)} custom-call(f32[512,128]{1,0:T(8,128)S(1)} %bitcast.51, f32[512,128]{1,0:T(8,128)S(1)} %collective-permute-done.after_ref.refs_1_, f32[512,128]{1,0:T(8,128)S(1)} %shard_map.74.refs_2_, f32[512,128]{1,0:T(8,128)S(1)} %collective-permute-done.2.refs_3_, ...), custom_call_target="tpu_custom_call" | custom-call | tf_op jit(solution)/shard_map/pallas_call | solution.py:324
  39.3 4.4 %shard_map.78.rest_0_ = f32[4,512,128]{2,1,0:T(8,128)S(1)} custom-call(s32[3]{0:T(128)S(1)} %pad_add_fusion.place_ref, s32[32]{0:T(128)S(1)} %convert_element_type.17.count_ref, s32[8192]{0:T(1024)S(1)} %bitcast.46, f32[8192]{0:T(1024)S(1)} %bitcast.43, f32[16,56,128]{2,1,0:T(8,128)S(1)} %all-to-all-done.list_ref, f32[8192,128]{1,0:T(8,128)S(1)} %shard_map.77.table_ref), custom_call_target="tpu_custom_call" | custom-call | bytes 10485760 | tf_op jit(solution)/shard_map/pallas_call | solution.py:246
  43.7 1.4 %collective-permute-start.15 = (f32[4,512,128]{2,1,0:T(8,128)S(1)}, f32[4,512,128]{2,1,0:T(8,128)S(1)}, u32[]{:S(2)}, u32[]{:S(2)}) collective-permute-start(f32[4,512,128]{2,1,0:T(8,128)S(1)} %shard_map.78.rest_0_), channel_id=1, source_target_pairs={{0,128},{1,5},{2,130},{3,7},{4,132},{5,1},{6,134},{7,3},{64,192},{... | collective-permute-start | bytes 3145736 | tf_op jit(solution)/shard_map/ppermute | solution.py:377
  45.1 6.6 %shard_map.80 = (f32[4,512,128]{2,1,0:T(8,128)S(1)}, f32[4,512,128]{2,1,0:T(8,128)S(1)}) custom-call(s32[3]{0:T(128)S(1)} %pad_add_fusion.place_ref, s32[32]{0:T(128)S(1)} %convert_element_type.17.count_ref, s32[8192]{0:T(1024)S(1)} %bitcast.47, f32[8192]{0:T(1024)S(1)} %bitcast.44, f32[16,56,128]{2,1,0:T(8,128)S(1)} %all-to-all-done.list_ref, ...), custom_call_target="tpu_custom_call" | custom-call | bytes 41943040 | tf_op jit(solution)/shard_map/pallas_call | solution.py:246
  51.7 0.1 collective-permute-start.17
  51.8 3.2 %collective-permute-start.16 = (f32[4,512,128]{2,1,0:T(8,128)S(1)}, f32[4,512,128]{2,1,0:T(8,128)S(1)}, u32[]{:S(2)}, u32[]{:S(2)}) collective-permute-start(f32[4,512,128]{2,1,0:T(8,128)S(1)} %get-tuple-element.7), channel_id=1, source_target_pairs={{0,64},{1,3},{2,66},{3,5},{4,68},{5,7},{6,70},{7,1},{64,128},{65,6... | collective-permute-start | bytes 3145736 | tf_op jit(solution)/shard_map/ppermute | solution.py:377
  55.1 5.1 %collective-permute-done.15.rest_0_ = f32[4,512,128]{2,1,0:T(8,128)S(1)} collective-permute-done((f32[4,512,128]{2,1,0:T(8,128)S(1)}, f32[4,512,128]{2,1,0:T(8,128)S(1)}, u32[]{:S(2)}, u32[]{:S(2)}) %collective-permute-start.15) | collective-permute-done | bytes 1048608 | tf_op jit(solution)/shard_map/ppermute | solution.py:377
  60.2 4.1 %shard_map.79.earlier_ref = f32[4,512,128]{2,1,0:T(8,128)S(1)} custom-call(s32[3]{0:T(128)S(1)} %pad_add_fusion.place_ref, s32[32]{0:T(128)S(1)} %convert_element_type.17.count_ref, s32[8192]{0:T(1024)S(1)} %bitcast.48, f32[8192]{0:T(1024)S(1)} %bitcast.45, f32[16,56,128]{2,1,0:T(8,128)S(1)} %all-to-all-done.list_ref, f32[8192,128]{1,0:T(8,128)S(1)} %shard_map.77.table_ref, ...), custom_call_target="tpu_custom_call" | custom-call | bytes 41943040 | tf_op jit(solution)/shard_map/pallas_call | solution.py:246
  64.3 7.0 %collective-permute-done.17 = f32[4,512,128]{2,1,0:T(8,128)S(1)} collective-permute-done((f32[4,512,128]{2,1,0:T(8,128)S(1)}, f32[4,512,128]{2,1,0:T(8,128)S(1)}, u32[]{:S(2)}, u32[]{:S(2)}) %collective-permute-start.17) | collective-permute-done | bytes 1048608 | tf_op jit(solution)/shard_map/ppermute | solution.py:377
  71.3 0.2 fusion.2
  71.5 2.7 %collective-permute-start.20 = (f32[512,128]{1,0:T(8,128)S(1)}, f32[512,128]{1,0:T(8,128)S(1)}, u32[]{:S(2)}, u32[]{:S(2)}) collective-permute-start(f32[512,128]{1,0:T(8,128)S(1)} %get-tuple-element.10), channel_id=1, source_target_pairs={{0,6},{1,193},{2,0},{3,195},{4,2},{5,197},{6,4},{7,199},{64,70},{6... | collective-permute-start | bytes 786440 | tf_op jit(solution)/shard_map/ppermute | solution.py:377
  74.3 1.9 %collective-permute-start.18 = (f32[512,128]{1,0:T(8,128)S(1)}, f32[512,128]{1,0:T(8,128)S(1)}, u32[]{:S(2)}, u32[]{:S(2)}) collective-permute-start(f32[512,128]{1,0:T(8,128)S(1)} %get-tuple-element.9), channel_id=1, source_target_pairs={{0,4},{1,129},{2,6},{3,131},{4,0},{5,133},{6,2},{7,135},{64,68},{6... | collective-permute-start | bytes 786440 | tf_op jit(solution)/shard_map/ppermute | solution.py:377
  76.2 0.7 fusion.8
  76.9 1.9 %collective-permute-start.22 = (f32[2,3,1,64,128]{4,3,2,1,0:T(8,128)}, f32[2,3,1,64,128]{4,3,2,1,0:T(8,128)S(1)}, u32[]{:S(2)}, u32[]{:S(2)}) collective-permute-start(f32[2,3,1,64,128]{4,3,2,1,0:T(8,128)} %get-tuple-element.13), channel_id=1, source_target_pairs={{0,1},{1,2},{2,3},{3,4},{4,5},{5,6},{6,7},{7,8},{8,9},{9,10},{10,1... | collective-permute-start | bytes 589832 | tf_op jit(solution)/shard_map/ppermute | solution.py:338
  78.8 5.8 %collective-permute-start.23 = (f32[2,3,1,64,128]{4,3,2,1,0:T(8,128)S(1)}, f32[2,3,1,64,128]{4,3,2,1,0:T(8,128)S(1)}, u32[]{:S(2)}, u32[]{:S(2)}) collective-permute-start(f32[2,3,1,64,128]{4,3,2,1,0:T(8,128)S(1)} %get-tuple-element.12), channel_id=1, source_target_pairs={{1,0},{2,1},{3,2},{4,3},{5,4},{6,5},{7,6},{8,7},{9,8},{10,9},{11,1... | collective-permute-start | bytes 589832 | tf_op jit(solution)/shard_map/ppermute | solution.py:338
  84.6 2.2 %collective-permute-done.19 = f32[512,128]{1,0:T(8,128)S(1)} collective-permute-done((f32[512,128]{1,0:T(8,128)S(1)}, f32[512,128]{1,0:T(8,128)S(1)}, u32[]{:S(2)}, u32[]{:S(2)}) %collective-permute-start.19) | collective-permute-done | bytes 262176 | tf_op jit(solution)/shard_map/ppermute | solution.py:377
  86.8 0.1 fusion.6
  86.9 1.9 %collective-permute-start.21 = (f32[64,128]{1,0:T(8,128)S(1)}, f32[64,128]{1,0:T(8,128)S(1)}, u32[]{:S(2)}, u32[]{:S(2)}) collective-permute-start(f32[64,128]{1,0:T(8,128)S(1)} %slice_exponential_fusion), channel_id=1, source_target_pairs={{0,1},{1,2},{2,3},{3,4},{4,5},{5,6},{6,7},{7,8},{8,9},{9,10},{10,1... | collective-permute-start | bytes 98312 | tf_op jit(solution)/shard_map/ppermute | solution.py:338
  89.5 0.0 copy-start.1
  89.5 1.4 %copy-done.1 = f32[1,2,3,8,64,128]{5,4,3,2,1,0:T(8,128)S(1)} copy-done((f32[1,2,3,8,64,128]{5,4,3,2,1,0:T(8,128)S(1)}, f32[1,2,3,8,64,128]{5,4,3,2,1,0:T(8,128)}, u32[]{:S(2)}) %copy-start.1) | copy-done | bytes 1572888
  90.9 1.4 %shard_map.81.rest_ref = f32[2,3,8,64,128]{4,3,2,1,0:T(8,128)S(1)} custom-call(f32[1]{0:T(128)} %bitcast.20.rim_ref, f32[2,3,8,64,128]{4,3,2,1,0:T(8,128)S(1)} %bitcast.39, f32[2,3,1,64,128]{4,3,2,1,0:T(8,128)S(1)} %collective-permute-done.22.before_ref, f32[2,3,1,64,128]{4,3,2,1,0:T(8,128)S(1)} %collective-permute-done.23.after_ref, ...), custom_call_target="tpu_custom_call" | custom-call | bytes 12582912 | tf_op jit(solution)/shard_map/pallas_call | solution.py:443
  92.3 2.0 %collective-permute-done.21 = f32[64,128]{1,0:T(8,128)S(1)} collective-permute-done((f32[64,128]{1,0:T(8,128)S(1)}, f32[64,128]{1,0:T(8,128)S(1)}, u32[]{:S(2)}, u32[]{:S(2)}) %collective-permute-start.21) | collective-permute-done | bytes 32800 | tf_op jit(solution)/shard_map/ppermute | solution.py:338
  94.3 1.4 %shard_map.82 = f32[2,3,8,64,128]{4,3,2,1,0:T(8,128)} custom-call(f32[1]{0:T(128)S(6)} %copy.16.omega_ref, f32[8,64,128]{2,1,0:T(8,128)S(1)} %bitcast.42, f32[64,128]{1,0:T(8,128)S(1)} %fusion.7.prior_ref, f32[2,3,8,64,128]{4,3,2,1,0:T(8,128)S(1)} %shard_map.81.rest_ref, f32[2,3,8,64,128]{4,3,2,1,0:T(8,128)S(1)} %bitcast.40), custom_call_target="tpu_custom_call" | custom-call | tf_op jit(solution)/shard_map/pallas_call | solution.py:476
  (35 shorter events, 0.1 us)
Async XLA Ops:
  0.0 2.0 %collective-permute-start = (f32[512,128]{1,0:T(8,128)}, f32[512,128]{1,0:T(8,128)S(1)}, u32[]{:S(2)}, u32[]{:S(2)}) collective-permute-start(f32[512,128]{1,0:T(8,128)} %bitcast.49), channel_id=1, source_target_pairs={{0,1},{1,0},{2,3},{3,2},{4,5},{5,4},{6,7},{7,6},{8,9},{9,8},{10,11... | collective-permute-start | bytes 786440 | tf_op jit(solution)/shard_map/ppermute | solution.py:265
  0.0 9.6 %collective-permute-start.1 = (f32[512,128]{1,0:T(8,128)}, f32[512,128]{1,0:T(8,128)S(1)}, u32[]{:S(2)}, u32[]{:S(2)}) collective-permute-start(f32[512,128]{1,0:T(8,128)} %bitcast.50), channel_id=1, source_target_pairs={{0,8},{8,16},{16,24},{24,32},{32,40},{40,48},{48,56},{56,0},{1,57}... | collective-permute-start | bytes 786440 | tf_op jit(solution)/shard_map/ppermute | solution.py:314
  2.0 10.8 %collective-permute-start.3 = (f32[512,128]{1,0:T(8,128)S(1)}, f32[512,128]{1,0:T(8,128)S(1)}, u32[]{:S(2)}, u32[]{:S(2)}) collective-permute-start(f32[512,128]{1,0:T(8,128)S(1)} %collective-permute-done.after_ref.refs_1_), channel_id=1, source_target_pairs={{0,8},{8,16},{16,24},{24,32},{32,40},{40,48},{48,56},{56,0},{1,57}... | collective-permute-start | bytes 786440 | tf_op jit(solution)/shard_map/ppermute | solution.py:314
  3.9 0.7 copy-start.3
  4.6 0.7 copy-start.4
  5.4 0.7 copy-start.5
  9.6 28.1 %copy-start.2 = (f32[512,1,128]{2,1,0:T(1,128)S(1)}, f32[512,1,128]{2,1,0:T(1,128)}, u32[]{:S(2)}) copy-start(f32[512,1,128]{2,1,0:T(1,128)} %param.7) | copy-start | bytes 786436
  9.6 7.1 %collective-permute-start.5 = (f32[512,128]{1,0:T(8,128)S(1)}, f32[512,128]{1,0:T(8,128)S(1)}, u32[]{:S(2)}, u32[]{:S(2)}) collective-permute-start(f32[512,128]{1,0:T(8,128)S(1)} %shard_map.74.refs_2_), channel_id=1, source_target_pairs={{0,8},{8,16},{16,24},{24,32},{32,40},{40,48},{48,56},{56,0},{1,57}... | collective-permute-start | bytes 786440 | tf_op jit(solution)/shard_map/ppermute | solution.py:314
  12.8 14.1 %collective-permute-start.7 = (f32[512,128]{1,0:T(8,128)S(1)}, f32[512,128]{1,0:T(8,128)S(1)}, u32[]{:S(2)}, u32[]{:S(2)}) collective-permute-start(f32[512,128]{1,0:T(8,128)S(1)} %collective-permute-done.3.refs_1_.refs_4_), channel_id=1, source_target_pairs={{0,8},{8,16},{16,24},{24,32},{32,40},{40,48},{48,56},{56,0},{1,57}... | collective-permute-start | bytes 786440 | tf_op jit(solution)/shard_map/ppermute | solution.py:314
  16.7 11.8 %collective-permute-start.9 = (f32[512,128]{1,0:T(8,128)S(1)}, f32[512,128]{1,0:T(8,128)S(1)}, u32[]{:S(2)}, u32[]{:S(2)}) collective-permute-start(f32[512,128]{1,0:T(8,128)S(1)} %shard_map.75.refs_6_), channel_id=1, source_target_pairs={{0,8},{8,16},{16,24},{24,32},{32,40},{40,48},{48,56},{56,0},{1,57}... | collective-permute-start | bytes 786440 | tf_op jit(solution)/shard_map/ppermute | solution.py:314
  19.2 16.9 %all-to-all-start = ((f32[16,56,128]{2,1,0:T(8,128)}), f32[16,56,128]{2,1,0:T(8,128)S(1)}, u32[]{:S(2)}, u32[]{:S(2)}) async-start(f32[16,56,128]{2,1,0:T(8,128)} %shard_map.73.refs_1_), calls=%async_computation | async-start | bytes 917504 | tf_op jit(solution)/shard_map/all_to_all | solution.py:359
  26.3 4.5 %collective-permute-start.2 = (f32[512,128]{1,0:T(8,128)S(1)}, f32[512,128]{1,0:T(8,128)S(1)}, u32[]{:S(2)}, u32[]{:S(2)}) collective-permute-start(f32[512,128]{1,0:T(8,128)S(1)} %shard_map.74.refs_2_), channel_id=1, source_target_pairs={{0,1},{1,0},{2,3},{3,2},{4,5},{5,4},{6,7},{7,6},{8,9},{9,8},{10,11... | collective-permute-start | bytes 786440 | tf_op jit(solution)/shard_map/ppermute | solution.py:265
  26.4 5.0 %collective-permute-start.4 = (f32[512,128]{1,0:T(8,128)S(1)}, f32[512,128]{1,0:T(8,128)S(1)}, u32[]{:S(2)}, u32[]{:S(2)}) collective-permute-start(f32[512,128]{1,0:T(8,128)S(1)} %collective-permute-done.3.refs_1_.refs_4_), channel_id=1, source_target_pairs={{0,1},{1,0},{2,3},{3,2},{4,5},{5,4},{6,7},{7,6},{8,9},{9,8},{10,11... | collective-permute-start | bytes 786440 | tf_op jit(solution)/shard_map/ppermute | solution.py:265
  26.9 6.4 %collective-permute-start.11 = (f32[512,128]{1,0:T(8,128)S(1)}, f32[512,128]{1,0:T(8,128)S(1)}, u32[]{:S(2)}, u32[]{:S(2)}) collective-permute-start(f32[512,128]{1,0:T(8,128)S(1)} %collective-permute-done.7.refs_1_.refs_8_), channel_id=1, source_target_pairs={{0,8},{8,16},{16,24},{24,32},{32,40},{40,48},{48,56},{56,0},{1,57}... | collective-permute-start | bytes 786440 | tf_op jit(solution)/shard_map/ppermute | solution.py:314
  28.5 7.5 %collective-permute-start.13 = (f32[512,128]{1,0:T(8,128)S(1)}, f32[512,128]{1,0:T(8,128)S(1)}, u32[]{:S(2)}, u32[]{:S(2)}) collective-permute-start(f32[512,128]{1,0:T(8,128)S(1)} %shard_map.76.refs_10_), channel_id=1, source_target_pairs={{0,8},{8,16},{16,24},{24,32},{32,40},{40,48},{48,56},{56,0},{1,57}... | collective-permute-start | bytes 786440 | tf_op jit(solution)/shard_map/ppermute | solution.py:314
  30.8 5.4 %collective-permute-start.6 = (f32[512,128]{1,0:T(8,128)S(1)}, f32[512,128]{1,0:T(8,128)}, u32[]{:S(2)}, u32[]{:S(2)}) collective-permute-start(f32[512,128]{1,0:T(8,128)S(1)} %shard_map.75.refs_6_), channel_id=1, source_target_pairs={{0,1},{1,0},{2,3},{3,2},{4,5},{5,4},{6,7},{7,6},{8,9},{9,8},{10,11... | collective-permute-start | bytes 786440 | tf_op jit(solution)/shard_map/ppermute | solution.py:265
  30.9 5.4 %collective-permute-start.10 = (f32[512,128]{1,0:T(8,128)S(1)}, f32[512,128]{1,0:T(8,128)}, u32[]{:S(2)}, u32[]{:S(2)}) collective-permute-start(f32[512,128]{1,0:T(8,128)S(1)} %shard_map.76.refs_10_), channel_id=1, source_target_pairs={{0,1},{1,0},{2,3},{3,2},{4,5},{5,4},{6,7},{7,6},{8,9},{9,8},{10,11... | collective-permute-start | bytes 786440 | tf_op jit(solution)/shard_map/ppermute | solution.py:265
  31.4 4.9 %collective-permute-start.8 = (f32[512,128]{1,0:T(8,128)S(1)}, f32[512,128]{1,0:T(8,128)}, u32[]{:S(2)}, u32[]{:S(2)}) collective-permute-start(f32[512,128]{1,0:T(8,128)S(1)} %collective-permute-done.7.refs_1_.refs_8_), channel_id=1, source_target_pairs={{0,1},{1,0},{2,3},{3,2},{4,5},{5,4},{6,7},{7,6},{8,9},{9,8},{10,11... | collective-permute-start | bytes 786440 | tf_op jit(solution)/shard_map/ppermute | solution.py:265
  33.2 3.1 %collective-permute-start.12 = (f32[512,128]{1,0:T(8,128)S(1)}, f32[512,128]{1,0:T(8,128)}, u32[]{:S(2)}, u32[]{:S(2)}) collective-permute-start(f32[512,128]{1,0:T(8,128)S(1)} %collective-permute-done.11.refs_12_), channel_id=1, source_target_pairs={{0,1},{1,0},{2,3},{3,2},{4,5},{5,4},{6,7},{7,6},{8,9},{9,8},{10,11... | collective-permute-start | bytes 786440 | tf_op jit(solution)/shard_map/ppermute | solution.py:265
  36.0 1.7 %collective-permute-start.14 = (f32[512,128]{1,0:T(8,128)S(1)}, f32[512,128]{1,0:T(8,128)}, u32[]{:S(2)}, u32[]{:S(2)}) collective-permute-start(f32[512,128]{1,0:T(8,128)S(1)} %collective-permute-done.13.refs_14_), channel_id=1, source_target_pairs={{0,1},{1,0},{2,3},{3,2},{4,5},{5,4},{6,7},{7,6},{8,9},{9,8},{10,11... | collective-permute-start | bytes 786440 | tf_op jit(solution)/shard_map/ppermute | solution.py:265
  43.7 16.5 %collective-permute-start.15 = (f32[4,512,128]{2,1,0:T(8,128)S(1)}, f32[4,512,128]{2,1,0:T(8,128)S(1)}, u32[]{:S(2)}, u32[]{:S(2)}) collective-permute-start(f32[4,512,128]{2,1,0:T(8,128)S(1)} %shard_map.78.rest_0_), channel_id=1, source_target_pairs={{0,128},{1,5},{2,130},{3,7},{4,132},{5,1},{6,134},{7,3},{64,192},{... | collective-permute-start | bytes 3145736 | tf_op jit(solution)/shard_map/ppermute | solution.py:377
  51.7 19.5 %collective-permute-start.17 = (f32[4,512,128]{2,1,0:T(8,128)S(1)}, f32[4,512,128]{2,1,0:T(8,128)S(1)}, u32[]{:S(2)}, u32[]{:S(2)}) collective-permute-start(f32[4,512,128]{2,1,0:T(8,128)S(1)} %get-tuple-element.8), channel_id=1, source_target_pairs={{0,192},{1,7},{2,194},{3,1},{4,196},{5,3},{6,198},{7,5},{64,0},{65... | collective-permute-start | bytes 3145736 | tf_op jit(solution)/shard_map/ppermute | solution.py:377
  51.8 19.5 %collective-permute-start.16 = (f32[4,512,128]{2,1,0:T(8,128)S(1)}, f32[4,512,128]{2,1,0:T(8,128)S(1)}, u32[]{:S(2)}, u32[]{:S(2)}) collective-permute-start(f32[4,512,128]{2,1,0:T(8,128)S(1)} %get-tuple-element.7), channel_id=1, source_target_pairs={{0,64},{1,3},{2,66},{3,5},{4,68},{5,7},{6,70},{7,1},{64,128},{65,6... | collective-permute-start | bytes 3145736 | tf_op jit(solution)/shard_map/ppermute | solution.py:377
  64.3 11.9 %copy-start = (f32[1,2,3,8,64,128]{5,4,3,2,1,0:T(8,128)S(1)}, f32[1,2,3,8,64,128]{5,4,3,2,1,0:T(8,128)}, u32[]{:S(2)}) copy-start(f32[1,2,3,8,64,128]{5,4,3,2,1,0:T(8,128)} %param.11) | copy-start | bytes 4718596
  71.5 13.0 %collective-permute-start.20 = (f32[512,128]{1,0:T(8,128)S(1)}, f32[512,128]{1,0:T(8,128)S(1)}, u32[]{:S(2)}, u32[]{:S(2)}) collective-permute-start(f32[512,128]{1,0:T(8,128)S(1)} %get-tuple-element.10), channel_id=1, source_target_pairs={{0,6},{1,193},{2,0},{3,195},{4,2},{5,197},{6,4},{7,199},{64,70},{6... | collective-permute-start | bytes 786440 | tf_op jit(solution)/shard_map/ppermute | solution.py:377
  74.3 12.5 %collective-permute-start.19 = (f32[512,128]{1,0:T(8,128)S(1)}, f32[512,128]{1,0:T(8,128)S(1)}, u32[]{:S(2)}, u32[]{:S(2)}) collective-permute-start(f32[512,128]{1,0:T(8,128)S(1)} %get-tuple-element.11), channel_id=1, source_target_pairs={{0,2},{1,65},{2,4},{3,67},{4,6},{5,69},{6,0},{7,71},{64,66},{65,12... | collective-permute-start | bytes 786440 | tf_op jit(solution)/shard_map/ppermute | solution.py:377
  74.3 12.5 %collective-permute-start.18 = (f32[512,128]{1,0:T(8,128)S(1)}, f32[512,128]{1,0:T(8,128)S(1)}, u32[]{:S(2)}, u32[]{:S(2)}) collective-permute-start(f32[512,128]{1,0:T(8,128)S(1)} %get-tuple-element.9), channel_id=1, source_target_pairs={{0,4},{1,129},{2,6},{3,131},{4,0},{5,133},{6,2},{7,135},{64,68},{6... | collective-permute-start | bytes 786440 | tf_op jit(solution)/shard_map/ppermute | solution.py:377
  76.9 12.6 %collective-permute-start.22 = (f32[2,3,1,64,128]{4,3,2,1,0:T(8,128)}, f32[2,3,1,64,128]{4,3,2,1,0:T(8,128)S(1)}, u32[]{:S(2)}, u32[]{:S(2)}) collective-permute-start(f32[2,3,1,64,128]{4,3,2,1,0:T(8,128)} %get-tuple-element.13), channel_id=1, source_target_pairs={{0,1},{1,2},{2,3},{3,4},{4,5},{5,6},{6,7},{7,8},{8,9},{9,10},{10,1... | collective-permute-start | bytes 589832 | tf_op jit(solution)/shard_map/ppermute | solution.py:338
  78.8 10.7 %collective-permute-start.23 = (f32[2,3,1,64,128]{4,3,2,1,0:T(8,128)S(1)}, f32[2,3,1,64,128]{4,3,2,1,0:T(8,128)S(1)}, u32[]{:S(2)}, u32[]{:S(2)}) collective-permute-start(f32[2,3,1,64,128]{4,3,2,1,0:T(8,128)S(1)} %get-tuple-element.12), channel_id=1, source_target_pairs={{1,0},{2,1},{3,2},{4,3},{5,4},{6,5},{7,6},{8,7},{9,8},{10,9},{11,1... | collective-permute-start | bytes 589832 | tf_op jit(solution)/shard_map/ppermute | solution.py:338
  86.9 7.3 %collective-permute-start.21 = (f32[64,128]{1,0:T(8,128)S(1)}, f32[64,128]{1,0:T(8,128)S(1)}, u32[]{:S(2)}, u32[]{:S(2)}) collective-permute-start(f32[64,128]{1,0:T(8,128)S(1)} %slice_exponential_fusion), channel_id=1, source_target_pairs={{0,1},{1,2},{2,3},{3,4},{4,5},{5,6},{6,7},{7,8},{8,9},{9,10},{10,1... | collective-permute-start | bytes 98312 | tf_op jit(solution)/shard_map/ppermute | solution.py:338
  89.5 1.4 %copy-start.1 = (f32[1,2,3,8,64,128]{5,4,3,2,1,0:T(8,128)S(1)}, f32[1,2,3,8,64,128]{5,4,3,2,1,0:T(8,128)}, u32[]{:S(2)}) copy-start(f32[1,2,3,8,64,128]{5,4,3,2,1,0:T(8,128)} %param.12) | copy-start | bytes 4718596

commit v6 on v5

--- a/solution.py
+++ b/solution.py
@@ -9,7 +9,7 @@
 
 CHUNK = 256
 FIELDS = 3
-STEP = 16
+STEP = 32
 NEAR = 512
 
 
@@ -161,7 +161,7 @@
     lane_rows = cap // 128
     iota = lax.broadcasted_iota(jnp.int32, (columns, 128), 0)
     lanes = lax.broadcasted_iota(jnp.int32, (1, 128), 1)
-    picked[...] = jnp.zeros_like(picked)
+    depth = lax.broadcasted_iota(jnp.int32, (CHUNK, 128), 0)
 
     def gather(slot, at, begin, count, j):
         first = begin + j * CHUNK
@@ -199,7 +199,7 @@
     def combine(slot, half, at, begin, count, j):
         first = begin + j * CHUNK
         left = count - j * CHUNK
-        rows = picked[slot]
+        rows = jnp.where(depth < left, picked[slot], 0.0)
         high = rows.astype(jnp.bfloat16)
         low = (rows - high.astype(jnp.float32)).astype(jnp.bfloat16)
         hot = []
@@ -315,7 +315,7 @@
         if step == 1:
             pair[0] = ordered(pair[0], lists)
         elif step < nz // 2:
-            pair[0] = ordered(pair[0], mates)
+            pair[0] = ordered(pair[0], mates, arrays[3 if step == 2 else 5])
         mates = pair[-1]
         for core, one in enumerate(pair):
             take(one, core * nz + step)

time: 96.9 us -> 96.6 us (level)
  starting transfers between devices: 42.3 us -> 41 us
  waiting for transfers between devices: 24.5 us -> 25.6 us
    ppermute x7, starting transfers between devices: 15.1 us -> 11.5 us  [gathered(): pair = [lax.ppermute(one, ('z', 'c'), onward) for one in pair]]
    ppermute x8, starting transfers between devices: 1.14 us -> 3.03 us  [moved(): lax.ppermute(value, axis, [(i, (i + by) % count) for i in range(count)])]
    ppermute x7, waiting for transfers between devices: 6.81 us -> 8.16 us  [gathered(): pair = [lax.ppermute(one, ('z', 'c'), onward) for one in pair]]
where the time goes in v6:
time: 96.6 us; the launch traced here: 95.4 us
  starting transfers between devices  41 us (42%)
  waiting for transfers between devices  25.6 us (27%)
  Pallas kernels  22.6 us (23%)
  local copies, waits for them, and re-layouts  4.46 us (5%)
  between operations  1.08 us (1%)
    pallas_call x3, Pallas kernels, partial_sums(): pl.pallas_call(functools.partial(partials_kernel, [job[:2] for job in job...  14.9 us
    ppermute x6, waiting for transfers between devices, sent(): return lax.ppermute(value, ('y', 'x', 'c'), pairs)  14.1 us
    ppermute x7, starting transfers between devices, gathered(): pair = [lax.ppermute(one, ('z', 'c'), onward) for one in pair]  11.5 us
    ppermute x6, starting transfers between devices, sent(): return lax.ppermute(value, ('y', 'x', 'c'), pairs)  9.72 us
    ppermute x3, starting transfers between devices, shifted(): return lax.ppermute(shard, axis, pairs)  9.58 us
    ppermute x7, waiting for transfers between devices, gathered(): pair = [lax.ppermute(one, ('z', 'c'), onward) for one in pair]  8.16 us
    all_to_all x1, starting transfers between devices, log_conductivity(): lax.all_to_all(lists, ('y', 'x'), split_axis=0, concat_axis=0, tiled=True)  7.17 us
    unnamed x12, local copies, waits for them, and re-layouts  3.57 us
  transfers between devices with their start and end apart: 25, of which 8 were waited for; matrix products, arithmetic and copies ran while one was open for 1% of the time, Pallas kernels for 16%

profile of v6, /device:TPU:56, one launch (start us, length us, event | category | flops | bytes accessed | tf_op | source)
XLA Modules:
  0.0 95.4 jit_solution(3529295323826375646)
XLA Ops:
  0.0 1.9 %collective-permute-start.1 = (f32[512,128]{1,0:T(8,128)}, f32[512,128]{1,0:T(8,128)S(1)}, u32[]{:S(2)}, u32[]{:S(2)}) collective-permute-start(f32[512,128]{1,0:T(8,128)} %bitcast.50), channel_id=1, source_target_pairs={{0,8},{8,16},{16,24},{24,32},{32,40},{40,48},{48,56},{56,0},{1,57}... | collective-permute-start | bytes 786440 | tf_op jit(solution)/shard_map/ppermute | solution.py:314
  1.9 0.1 pad_add_fusion.1.here_ref
  2.0 1.9 %collective-permute-start.3 = (f32[512,128]{1,0:T(8,128)S(1)}, f32[512,128]{1,0:T(8,128)S(1)}, u32[]{:S(2)}, u32[]{:S(2)}) collective-permute-start(f32[512,128]{1,0:T(8,128)S(1)} %collective-permute-done.after_ref.refs_1_), channel_id=1, source_target_pairs={{0,8},{8,16},{16,24},{24,32},{32,40},{40,48},{48,56},{56,0},{1,57}... | collective-permute-start | bytes 786440 | tf_op jit(solution)/shard_map/ppermute | solution.py:314
  3.9 0.7 copy-done.3
  4.7 0.7 copy-done.4
  5.4 0.7 copy-done.5
  6.1 3.5 %shard_map.73.refs_1_ = f32[16,56,128]{2,1,0:T(8,128)} custom-call(s32[2]{0:T(128)S(1)} %pad_add_fusion.1.here_ref, s32[8,512]{1,0:T(8,128)S(1)} %bitcast.52, s32[8,512]{1,0:T(8,128)S(1)} %bitcast.53, f32[8,512]{1,0:T(8,128)S(1)} %bitcast.54, f32[512,128]{1,0:T(8,128)S(1)} %collective-permute-done.after_ref.refs_1_), custom_call_target="tpu_custom_call" | custom-call | bytes 12582912 | tf_op jit(solution)/shard_map/pallas_call | solution.py:138
  9.6 0.0 copy-start.2
  9.6 2.2 %collective-permute-start.2 = (f32[512,128]{1,0:T(8,128)S(1)}, f32[512,128]{1,0:T(8,128)S(1)}, u32[]{:S(2)}, u32[]{:S(2)}) collective-permute-start(f32[512,128]{1,0:T(8,128)S(1)} %shard_map.74.refs_2_), channel_id=1, source_target_pairs={{0,1},{1,0},{2,3},{3,2},{4,5},{5,4},{6,7},{7,6},{8,9},{9,8},{10,11... | collective-permute-start | bytes 786440 | tf_op jit(solution)/shard_map/ppermute | solution.py:265
  11.8 1.1 %collective-permute-start.5 = (f32[512,128]{1,0:T(8,128)S(1)}, f32[512,128]{1,0:T(8,128)S(1)}, u32[]{:S(2)}, u32[]{:S(2)}) collective-permute-start(f32[512,128]{1,0:T(8,128)S(1)} %shard_map.74.refs_2_), channel_id=1, source_target_pairs={{0,8},{8,16},{16,24},{24,32},{32,40},{40,48},{48,56},{56,0},{1,57}... | collective-permute-start | bytes 786440 | tf_op jit(solution)/shard_map/ppermute | solution.py:314
  12.9 0.2 collective-permute-start.4
  13.1 1.4 %collective-permute-start.7 = (f32[512,128]{1,0:T(8,128)S(1)}, f32[512,128]{1,0:T(8,128)S(1)}, u32[]{:S(2)}, u32[]{:S(2)}) collective-permute-start(f32[512,128]{1,0:T(8,128)S(1)} %collective-permute-done.3.refs_1_.refs_4_), channel_id=1, source_target_pairs={{0,8},{8,16},{16,24},{24,32},{32,40},{40,48},{48,56},{56,0},{1,57}... | collective-permute-start | bytes 786440 | tf_op jit(solution)/shard_map/ppermute | solution.py:314
  14.6 3.6 %collective-permute-done.5.refs_0_ = f32[512,128]{1,0:T(8,128)S(1)} collective-permute-done((f32[512,128]{1,0:T(8,128)S(1)}, f32[512,128]{1,0:T(8,128)S(1)}, u32[]{:S(2)}, u32[]{:S(2)}) %collective-permute-start.5) | collective-permute-done | bytes 262176 | tf_op jit(solution)/shard_map/ppermute | solution.py:314
  18.1 1.1 %collective-permute-start.9 = (f32[512,128]{1,0:T(8,128)S(1)}, f32[512,128]{1,0:T(8,128)S(1)}, u32[]{:S(2)}, u32[]{:S(2)}) collective-permute-start(f32[512,128]{1,0:T(8,128)S(1)} %shard_map.75.refs_6_), channel_id=1, source_target_pairs={{0,8},{8,16},{16,24},{24,32},{32,40},{40,48},{48,56},{56,0},{1,57}... | collective-permute-start | bytes 786440 | tf_op jit(solution)/shard_map/ppermute | solution.py:314
  19.3 7.2 %all-to-all-start = ((f32[16,56,128]{2,1,0:T(8,128)}), f32[16,56,128]{2,1,0:T(8,128)S(1)}, u32[]{:S(2)}, u32[]{:S(2)}) async-start(f32[16,56,128]{2,1,0:T(8,128)} %shard_map.73.refs_1_), calls=%async_computation | async-start | bytes 917504 | tf_op jit(solution)/shard_map/all_to_all | solution.py:359
  26.5 1.7 %collective-permute-start.11 = (f32[512,128]{1,0:T(8,128)S(1)}, f32[512,128]{1,0:T(8,128)S(1)}, u32[]{:S(2)}, u32[]{:S(2)}) collective-permute-start(f32[512,128]{1,0:T(8,128)S(1)} %collective-permute-done.7.refs_1_.refs_8_), channel_id=1, source_target_pairs={{0,8},{8,16},{16,24},{24,32},{32,40},{40,48},{48,56},{56,0},{1,57}... | collective-permute-start | bytes 786440 | tf_op jit(solution)/shard_map/ppermute | solution.py:314
  28.2 2.2 %collective-permute-start.13 = (f32[512,128]{1,0:T(8,128)S(1)}, f32[512,128]{1,0:T(8,128)S(1)}, u32[]{:S(2)}, u32[]{:S(2)}) collective-permute-start(f32[512,128]{1,0:T(8,128)S(1)} %shard_map.76.refs_10_), channel_id=1, source_target_pairs={{0,8},{8,16},{16,24},{24,32},{32,40},{40,48},{48,56},{56,0},{1,57}... | collective-permute-start | bytes 786440 | tf_op jit(solution)/shard_map/ppermute | solution.py:314
  30.4 0.1 pad_add_fusion.place_ref
  30.5 0.0 collective-permute-start.6
  30.5 0.5 collective-permute-start.10
  31.0 0.1 collective-permute-start.8
  31.1 1.8 %collective-permute-done.11.refs_12_ = f32[512,128]{1,0:T(8,128)S(1)} collective-permute-done((f32[512,128]{1,0:T(8,128)S(1)}, f32[512,128]{1,0:T(8,128)S(1)}, u32[]{:S(2)}, u32[]{:S(2)}) %collective-permute-start.11) | collective-permute-done | bytes 262176 | tf_op jit(solution)/shard_map/ppermute | solution.py:314
  32.9 2.8 %collective-permute-done.13.refs_14_ = f32[512,128]{1,0:T(8,128)S(1)} collective-permute-done((f32[512,128]{1,0:T(8,128)S(1)}, f32[512,128]{1,0:T(8,128)S(1)}, u32[]{:S(2)}, u32[]{:S(2)}) %collective-permute-start.13) | collective-permute-done | bytes 262176 | tf_op jit(solution)/shard_map/ppermute | solution.py:314
  35.7 0.1 copy.12
  35.8 0.1 convert_element_type.17.count_ref
  36.0 1.4 %collective-permute-done.14.refs_15_ = f32[512,128]{1,0:T(8,128)} collective-permute-done((f32[512,128]{1,0:T(8,128)S(1)}, f32[512,128]{1,0:T(8,128)}, u32[]{:S(2)}, u32[]{:S(2)}) %collective-permute-start.14) | collective-permute-done | bytes 262176 | tf_op jit(solution)/shard_map/ppermute | solution.py:265
  37.4 1.6 %shard_map.77.table_ref = f32[8192,128]{1,0:T(8,128)S(1)} custom-call(f32[512,128]{1,0:T(8,128)S(1)} %bitcast.51, f32[512,128]{1,0:T(8,128)S(1)} %collective-permute-done.after_ref.refs_1_, f32[512,128]{1,0:T(8,128)S(1)} %shard_map.74.refs_2_, f32[512,128]{1,0:T(8,128)S(1)} %collective-permute-done.2.refs_2_.refs_3_, ...), custom_call_target="tpu_custom_call" | custom-call | tf_op jit(solution)/shard_map/pallas_call | solution.py:324
  38.9 4.4 %shard_map.78.rest_0_ = f32[4,512,128]{2,1,0:T(8,128)S(1)} custom-call(s32[3]{0:T(128)S(1)} %pad_add_fusion.place_ref, s32[32]{0:T(128)S(1)} %convert_element_type.17.count_ref, s32[8192]{0:T(1024)S(1)} %bitcast.46, f32[8192]{0:T(1024)S(1)} %bitcast.43, f32[16,56,128]{2,1,0:T(8,128)S(1)} %all-to-all-done.list_ref, f32[8192,128]{1,0:T(8,128)S(1)} %shard_map.77.table_ref), custom_call_target="tpu_custom_call" | custom-call | bytes 10485760 | tf_op jit(solution)/shard_map/pallas_call | solution.py:246
  43.3 1.5 %collective-permute-start.15 = (f32[4,512,128]{2,1,0:T(8,128)S(1)}, f32[4,512,128]{2,1,0:T(8,128)S(1)}, u32[]{:S(2)}, u32[]{:S(2)}) collective-permute-start(f32[4,512,128]{2,1,0:T(8,128)S(1)} %shard_map.78.rest_0_), channel_id=1, source_target_pairs={{0,128},{1,5},{2,130},{3,7},{4,132},{5,1},{6,134},{7,3},{64,192},{... | collective-permute-start | bytes 3145736 | tf_op jit(solution)/shard_map/ppermute | solution.py:377
  44.8 6.5 %shard_map.80 = (f32[4,512,128]{2,1,0:T(8,128)S(1)}, f32[4,512,128]{2,1,0:T(8,128)S(1)}) custom-call(s32[3]{0:T(128)S(1)} %pad_add_fusion.place_ref, s32[32]{0:T(128)S(1)} %convert_element_type.17.count_ref, s32[8192]{0:T(1024)S(1)} %bitcast.47, f32[8192]{0:T(1024)S(1)} %bitcast.44, f32[16,56,128]{2,1,0:T(8,128)S(1)} %all-to-all-done.list_ref, ...), custom_call_target="tpu_custom_call" | custom-call | bytes 41943040 | tf_op jit(solution)/shard_map/pallas_call | solution.py:246
  51.3 0.1 collective-permute-start.17
  51.4 3.2 %collective-permute-start.16 = (f32[4,512,128]{2,1,0:T(8,128)S(1)}, f32[4,512,128]{2,1,0:T(8,128)S(1)}, u32[]{:S(2)}, u32[]{:S(2)}) collective-permute-start(f32[4,512,128]{2,1,0:T(8,128)S(1)} %get-tuple-element.7), channel_id=1, source_target_pairs={{0,64},{1,3},{2,66},{3,5},{4,68},{5,7},{6,70},{7,1},{64,128},{65,6... | collective-permute-start | bytes 3145736 | tf_op jit(solution)/shard_map/ppermute | solution.py:377
  54.6 5.2 %collective-permute-done.15.rest_0_ = f32[4,512,128]{2,1,0:T(8,128)S(1)} collective-permute-done((f32[4,512,128]{2,1,0:T(8,128)S(1)}, f32[4,512,128]{2,1,0:T(8,128)S(1)}, u32[]{:S(2)}, u32[]{:S(2)}) %collective-permute-start.15) | collective-permute-done | bytes 1048608 | tf_op jit(solution)/shard_map/ppermute | solution.py:377
  59.8 4.0 %shard_map.79.earlier_ref = f32[4,512,128]{2,1,0:T(8,128)S(1)} custom-call(s32[3]{0:T(128)S(1)} %pad_add_fusion.place_ref, s32[32]{0:T(128)S(1)} %convert_element_type.17.count_ref, s32[8192]{0:T(1024)S(1)} %bitcast.48, f32[8192]{0:T(1024)S(1)} %bitcast.45, f32[16,56,128]{2,1,0:T(8,128)S(1)} %all-to-all-done.list_ref, f32[8192,128]{1,0:T(8,128)S(1)} %shard_map.77.table_ref, ...), custom_call_target="tpu_custom_call" | custom-call | bytes 41943040 | tf_op jit(solution)/shard_map/pallas_call | solution.py:246
  63.8 7.1 %collective-permute-done.17 = f32[4,512,128]{2,1,0:T(8,128)S(1)} collective-permute-done((f32[4,512,128]{2,1,0:T(8,128)S(1)}, f32[4,512,128]{2,1,0:T(8,128)S(1)}, u32[]{:S(2)}, u32[]{:S(2)}) %collective-permute-start.17) | collective-permute-done | bytes 1048608 | tf_op jit(solution)/shard_map/ppermute | solution.py:377
  70.9 0.2 fusion.2
  71.2 2.6 %collective-permute-start.20 = (f32[512,128]{1,0:T(8,128)S(1)}, f32[512,128]{1,0:T(8,128)S(1)}, u32[]{:S(2)}, u32[]{:S(2)}) collective-permute-start(f32[512,128]{1,0:T(8,128)S(1)} %get-tuple-element.10), channel_id=1, source_target_pairs={{0,6},{1,193},{2,0},{3,195},{4,2},{5,197},{6,4},{7,199},{64,70},{6... | collective-permute-start | bytes 786440 | tf_op jit(solution)/shard_map/ppermute | solution.py:377
  73.8 2.3 %collective-permute-start.18 = (f32[512,128]{1,0:T(8,128)S(1)}, f32[512,128]{1,0:T(8,128)S(1)}, u32[]{:S(2)}, u32[]{:S(2)}) collective-permute-start(f32[512,128]{1,0:T(8,128)S(1)} %get-tuple-element.9), channel_id=1, source_target_pairs={{0,4},{1,129},{2,6},{3,131},{4,0},{5,133},{6,2},{7,135},{64,68},{6... | collective-permute-start | bytes 786440 | tf_op jit(solution)/shard_map/ppermute | solution.py:377
  76.1 0.7 fusion.8
  76.8 1.9 %collective-permute-start.22 = (f32[2,3,1,64,128]{4,3,2,1,0:T(8,128)}, f32[2,3,1,64,128]{4,3,2,1,0:T(8,128)S(1)}, u32[]{:S(2)}, u32[]{:S(2)}) collective-permute-start(f32[2,3,1,64,128]{4,3,2,1,0:T(8,128)} %get-tuple-element.13), channel_id=1, source_target_pairs={{0,1},{1,2},{2,3},{3,4},{4,5},{5,6},{6,7},{7,8},{8,9},{9,10},{10,1... | collective-permute-start | bytes 589832 | tf_op jit(solution)/shard_map/ppermute | solution.py:338
  78.7 5.8 %collective-permute-start.23 = (f32[2,3,1,64,128]{4,3,2,1,0:T(8,128)S(1)}, f32[2,3,1,64,128]{4,3,2,1,0:T(8,128)S(1)}, u32[]{:S(2)}, u32[]{:S(2)}) collective-permute-start(f32[2,3,1,64,128]{4,3,2,1,0:T(8,128)S(1)} %get-tuple-element.12), channel_id=1, source_target_pairs={{1,0},{2,1},{3,2},{4,3},{5,4},{6,5},{7,6},{8,7},{9,8},{10,9},{11,1... | collective-permute-start | bytes 589832 | tf_op jit(solution)/shard_map/ppermute | solution.py:338
  84.5 1.8 %collective-permute-done.19 = f32[512,128]{1,0:T(8,128)S(1)} collective-permute-done((f32[512,128]{1,0:T(8,128)S(1)}, f32[512,128]{1,0:T(8,128)S(1)}, u32[]{:S(2)}, u32[]{:S(2)}) %collective-permute-start.19) | collective-permute-done | bytes 262176 | tf_op jit(solution)/shard_map/ppermute | solution.py:377
  86.3 0.1 fusion.6
  86.5 1.9 %collective-permute-start.21 = (f32[64,128]{1,0:T(8,128)S(1)}, f32[64,128]{1,0:T(8,128)S(1)}, u32[]{:S(2)}, u32[]{:S(2)}) collective-permute-start(f32[64,128]{1,0:T(8,128)S(1)} %slice_exponential_fusion), channel_id=1, source_target_pairs={{0,1},{1,2},{2,3},{3,4},{4,5},{5,6},{6,7},{7,8},{8,9},{9,10},{10,1... | collective-permute-start | bytes 98312 | tf_op jit(solution)/shard_map/ppermute | solution.py:338
  89.1 1.4 %copy-done.1 = f32[1,2,3,8,64,128]{5,4,3,2,1,0:T(8,128)S(1)} copy-done((f32[1,2,3,8,64,128]{5,4,3,2,1,0:T(8,128)S(1)}, f32[1,2,3,8,64,128]{5,4,3,2,1,0:T(8,128)}, u32[]{:S(2)}) %copy-start.1) | copy-done | bytes 1572888
  90.5 1.4 %shard_map.81.rest_ref = f32[2,3,8,64,128]{4,3,2,1,0:T(8,128)S(1)} custom-call(f32[1]{0:T(128)} %bitcast.20.rim_ref, f32[2,3,8,64,128]{4,3,2,1,0:T(8,128)S(1)} %bitcast.39, f32[2,3,1,64,128]{4,3,2,1,0:T(8,128)S(1)} %collective-permute-done.22.before_ref, f32[2,3,1,64,128]{4,3,2,1,0:T(8,128)S(1)} %collective-permute-done.23.after_ref, ...), custom_call_target="tpu_custom_call" | custom-call | bytes 12582912 | tf_op jit(solution)/shard_map/pallas_call | solution.py:443
  91.8 2.0 %collective-permute-done.21 = f32[64,128]{1,0:T(8,128)S(1)} collective-permute-done((f32[64,128]{1,0:T(8,128)S(1)}, f32[64,128]{1,0:T(8,128)S(1)}, u32[]{:S(2)}, u32[]{:S(2)}) %collective-permute-start.21) | collective-permute-done | bytes 32800 | tf_op jit(solution)/shard_map/ppermute | solution.py:338
  93.8 1.4 %shard_map.82 = f32[2,3,8,64,128]{4,3,2,1,0:T(8,128)} custom-call(f32[1]{0:T(128)S(6)} %copy.16.omega_ref, f32[8,64,128]{2,1,0:T(8,128)S(1)} %bitcast.42, f32[64,128]{1,0:T(8,128)S(1)} %fusion.7.prior_ref, f32[2,3,8,64,128]{4,3,2,1,0:T(8,128)S(1)} %shard_map.81.rest_ref, f32[2,3,8,64,128]{4,3,2,1,0:T(8,128)S(1)} %bitcast.40), custom_call_target="tpu_custom_call" | custom-call | tf_op jit(solution)/shard_map/pallas_call | solution.py:476
  (35 shorter events, 0.1 us)
Async XLA Ops:
  0.0 2.0 %collective-permute-start = (f32[512,128]{1,0:T(8,128)}, f32[512,128]{1,0:T(8,128)S(1)}, u32[]{:S(2)}, u32[]{:S(2)}) collective-permute-start(f32[512,128]{1,0:T(8,128)} %bitcast.49), channel_id=1, source_target_pairs={{0,1},{1,0},{2,3},{3,2},{4,5},{5,4},{6,7},{7,6},{8,9},{9,8},{10,11... | collective-permute-start | bytes 786440 | tf_op jit(solution)/shard_map/ppermute | solution.py:265
  0.0 9.6 %collective-permute-start.1 = (f32[512,128]{1,0:T(8,128)}, f32[512,128]{1,0:T(8,128)S(1)}, u32[]{:S(2)}, u32[]{:S(2)}) collective-permute-start(f32[512,128]{1,0:T(8,128)} %bitcast.50), channel_id=1, source_target_pairs={{0,8},{8,16},{16,24},{24,32},{32,40},{40,48},{48,56},{56,0},{1,57}... | collective-permute-start | bytes 786440 | tf_op jit(solution)/shard_map/ppermute | solution.py:314
  2.0 10.9 %collective-permute-start.3 = (f32[512,128]{1,0:T(8,128)S(1)}, f32[512,128]{1,0:T(8,128)S(1)}, u32[]{:S(2)}, u32[]{:S(2)}) collective-permute-start(f32[512,128]{1,0:T(8,128)S(1)} %collective-permute-done.after_ref.refs_1_), channel_id=1, source_target_pairs={{0,8},{8,16},{16,24},{24,32},{32,40},{40,48},{48,56},{56,0},{1,57}... | collective-permute-start | bytes 786440 | tf_op jit(solution)/shard_map/ppermute | solution.py:314
  3.9 0.7 copy-start.3
  4.6 0.7 copy-start.4
  5.4 0.7 copy-start.5
  9.6 27.8 %copy-start.2 = (f32[512,1,128]{2,1,0:T(1,128)S(1)}, f32[512,1,128]{2,1,0:T(1,128)}, u32[]{:S(2)}) copy-start(f32[512,1,128]{2,1,0:T(1,128)} %param.7) | copy-start | bytes 786436
  9.6 5.0 %collective-permute-start.2 = (f32[512,128]{1,0:T(8,128)S(1)}, f32[512,128]{1,0:T(8,128)S(1)}, u32[]{:S(2)}, u32[]{:S(2)}) collective-permute-start(f32[512,128]{1,0:T(8,128)S(1)} %shard_map.74.refs_2_), channel_id=1, source_target_pairs={{0,1},{1,0},{2,3},{3,2},{4,5},{5,4},{6,7},{7,6},{8,9},{9,8},{10,11... | collective-permute-start | bytes 786440 | tf_op jit(solution)/shard_map/ppermute | solution.py:265
  11.8 6.4 %collective-permute-start.5 = (f32[512,128]{1,0:T(8,128)S(1)}, f32[512,128]{1,0:T(8,128)S(1)}, u32[]{:S(2)}, u32[]{:S(2)}) collective-permute-start(f32[512,128]{1,0:T(8,128)S(1)} %shard_map.74.refs_2_), channel_id=1, source_target_pairs={{0,8},{8,16},{16,24},{24,32},{32,40},{40,48},{48,56},{56,0},{1,57}... | collective-permute-start | bytes 786440 | tf_op jit(solution)/shard_map/ppermute | solution.py:314
  12.9 15.3 %collective-permute-start.4 = (f32[512,128]{1,0:T(8,128)S(1)}, f32[512,128]{1,0:T(8,128)S(1)}, u32[]{:S(2)}, u32[]{:S(2)}) collective-permute-start(f32[512,128]{1,0:T(8,128)S(1)} %collective-permute-done.3.refs_1_.refs_4_), channel_id=1, source_target_pairs={{0,1},{1,0},{2,3},{3,2},{4,5},{5,4},{6,7},{7,6},{8,9},{9,8},{10,11... | collective-permute-start | bytes 786440 | tf_op jit(solution)/shard_map/ppermute | solution.py:265
  13.1 13.3 %collective-permute-start.7 = (f32[512,128]{1,0:T(8,128)S(1)}, f32[512,128]{1,0:T(8,128)S(1)}, u32[]{:S(2)}, u32[]{:S(2)}) collective-permute-start(f32[512,128]{1,0:T(8,128)S(1)} %collective-permute-done.3.refs_1_.refs_4_), channel_id=1, source_target_pairs={{0,8},{8,16},{16,24},{24,32},{32,40},{40,48},{48,56},{56,0},{1,57}... | collective-permute-start | bytes 786440 | tf_op jit(solution)/shard_map/ppermute | solution.py:314
  18.1 10.1 %collective-permute-start.9 = (f32[512,128]{1,0:T(8,128)S(1)}, f32[512,128]{1,0:T(8,128)S(1)}, u32[]{:S(2)}, u32[]{:S(2)}) collective-permute-start(f32[512,128]{1,0:T(8,128)S(1)} %shard_map.75.refs_6_), channel_id=1, source_target_pairs={{0,8},{8,16},{16,24},{24,32},{32,40},{40,48},{48,56},{56,0},{1,57}... | collective-permute-start | bytes 786440 | tf_op jit(solution)/shard_map/ppermute | solution.py:314
  19.3 16.4 %all-to-all-start = ((f32[16,56,128]{2,1,0:T(8,128)}), f32[16,56,128]{2,1,0:T(8,128)S(1)}, u32[]{:S(2)}, u32[]{:S(2)}) async-start(f32[16,56,128]{2,1,0:T(8,128)} %shard_map.73.refs_1_), calls=%async_computation | async-start | bytes 917504 | tf_op jit(solution)/shard_map/all_to_all | solution.py:359
  26.5 6.4 %collective-permute-start.11 = (f32[512,128]{1,0:T(8,128)S(1)}, f32[512,128]{1,0:T(8,128)S(1)}, u32[]{:S(2)}, u32[]{:S(2)}) collective-permute-start(f32[512,128]{1,0:T(8,128)S(1)} %collective-permute-done.7.refs_1_.refs_8_), channel_id=1, source_target_pairs={{0,8},{8,16},{16,24},{24,32},{32,40},{40,48},{48,56},{56,0},{1,57}... | collective-permute-start | bytes 786440 | tf_op jit(solution)/shard_map/ppermute | solution.py:314
  28.2 7.5 %collective-permute-start.13 = (f32[512,128]{1,0:T(8,128)S(1)}, f32[512,128]{1,0:T(8,128)S(1)}, u32[]{:S(2)}, u32[]{:S(2)}) collective-permute-start(f32[512,128]{1,0:T(8,128)S(1)} %shard_map.76.refs_10_), channel_id=1, source_target_pairs={{0,8},{8,16},{16,24},{24,32},{32,40},{40,48},{48,56},{56,0},{1,57}... | collective-permute-start | bytes 786440 | tf_op jit(solution)/shard_map/ppermute | solution.py:314
  30.5 5.4 %collective-permute-start.6 = (f32[512,128]{1,0:T(8,128)S(1)}, f32[512,128]{1,0:T(8,128)}, u32[]{:S(2)}, u32[]{:S(2)}) collective-permute-start(f32[512,128]{1,0:T(8,128)S(1)} %shard_map.75.refs_6_), channel_id=1, source_target_pairs={{0,1},{1,0},{2,3},{3,2},{4,5},{5,4},{6,7},{7,6},{8,9},{9,8},{10,11... | collective-permute-start | bytes 786440 | tf_op jit(solution)/shard_map/ppermute | solution.py:265
  30.5 5.4 %collective-permute-start.10 = (f32[512,128]{1,0:T(8,128)S(1)}, f32[512,128]{1,0:T(8,128)}, u32[]{:S(2)}, u32[]{:S(2)}) collective-permute-start(f32[512,128]{1,0:T(8,128)S(1)} %shard_map.76.refs_10_), channel_id=1, source_target_pairs={{0,1},{1,0},{2,3},{3,2},{4,5},{5,4},{6,7},{7,6},{8,9},{9,8},{10,11... | collective-permute-start | bytes 786440 | tf_op jit(solution)/shard_map/ppermute | solution.py:265
  31.0 4.9 %collective-permute-start.8 = (f32[512,128]{1,0:T(8,128)S(1)}, f32[512,128]{1,0:T(8,128)}, u32[]{:S(2)}, u32[]{:S(2)}) collective-permute-start(f32[512,128]{1,0:T(8,128)S(1)} %collective-permute-done.7.refs_1_.refs_8_), channel_id=1, source_target_pairs={{0,1},{1,0},{2,3},{3,2},{4,5},{5,4},{6,7},{7,6},{8,9},{9,8},{10,11... | collective-permute-start | bytes 786440 | tf_op jit(solution)/shard_map/ppermute | solution.py:265
  32.9 3.1 %collective-permute-start.12 = (f32[512,128]{1,0:T(8,128)S(1)}, f32[512,128]{1,0:T(8,128)}, u32[]{:S(2)}, u32[]{:S(2)}) collective-permute-start(f32[512,128]{1,0:T(8,128)S(1)} %collective-permute-done.11.refs_12_), channel_id=1, source_target_pairs={{0,1},{1,0},{2,3},{3,2},{4,5},{5,4},{6,7},{7,6},{8,9},{9,8},{10,11... | collective-permute-start | bytes 786440 | tf_op jit(solution)/shard_map/ppermute | solution.py:265
  35.7 1.7 %collective-permute-start.14 = (f32[512,128]{1,0:T(8,128)S(1)}, f32[512,128]{1,0:T(8,128)}, u32[]{:S(2)}, u32[]{:S(2)}) collective-permute-start(f32[512,128]{1,0:T(8,128)S(1)} %collective-permute-done.13.refs_14_), channel_id=1, source_target_pairs={{0,1},{1,0},{2,3},{3,2},{4,5},{5,4},{6,7},{7,6},{8,9},{9,8},{10,11... | collective-permute-start | bytes 786440 | tf_op jit(solution)/shard_map/ppermute | solution.py:265
  43.3 16.5 %collective-permute-start.15 = (f32[4,512,128]{2,1,0:T(8,128)S(1)}, f32[4,512,128]{2,1,0:T(8,128)S(1)}, u32[]{:S(2)}, u32[]{:S(2)}) collective-permute-start(f32[4,512,128]{2,1,0:T(8,128)S(1)} %shard_map.78.rest_0_), channel_id=1, source_target_pairs={{0,128},{1,5},{2,130},{3,7},{4,132},{5,1},{6,134},{7,3},{64,192},{... | collective-permute-start | bytes 3145736 | tf_op jit(solution)/shard_map/ppermute | solution.py:377
  51.3 19.6 %collective-permute-start.17 = (f32[4,512,128]{2,1,0:T(8,128)S(1)}, f32[4,512,128]{2,1,0:T(8,128)S(1)}, u32[]{:S(2)}, u32[]{:S(2)}) collective-permute-start(f32[4,512,128]{2,1,0:T(8,128)S(1)} %get-tuple-element.8), channel_id=1, source_target_pairs={{0,192},{1,7},{2,194},{3,1},{4,196},{5,3},{6,198},{7,5},{64,0},{65... | collective-permute-start | bytes 3145736 | tf_op jit(solution)/shard_map/ppermute | solution.py:377
  51.4 19.5 %collective-permute-start.16 = (f32[4,512,128]{2,1,0:T(8,128)S(1)}, f32[4,512,128]{2,1,0:T(8,128)S(1)}, u32[]{:S(2)}, u32[]{:S(2)}) collective-permute-start(f32[4,512,128]{2,1,0:T(8,128)S(1)} %get-tuple-element.7), channel_id=1, source_target_pairs={{0,64},{1,3},{2,66},{3,5},{4,68},{5,7},{6,70},{7,1},{64,128},{65,6... | collective-permute-start | bytes 3145736 | tf_op jit(solution)/shard_map/ppermute | solution.py:377
  63.8 12.3 %copy-start = (f32[1,2,3,8,64,128]{5,4,3,2,1,0:T(8,128)S(1)}, f32[1,2,3,8,64,128]{5,4,3,2,1,0:T(8,128)}, u32[]{:S(2)}) copy-start(f32[1,2,3,8,64,128]{5,4,3,2,1,0:T(8,128)} %param.11) | copy-start | bytes 4718596
  71.2 13.3 %collective-permute-start.20 = (f32[512,128]{1,0:T(8,128)S(1)}, f32[512,128]{1,0:T(8,128)S(1)}, u32[]{:S(2)}, u32[]{:S(2)}) collective-permute-start(f32[512,128]{1,0:T(8,128)S(1)} %get-tuple-element.10), channel_id=1, source_target_pairs={{0,6},{1,193},{2,0},{3,195},{4,2},{5,197},{6,4},{7,199},{64,70},{6... | collective-permute-start | bytes 786440 | tf_op jit(solution)/shard_map/ppermute | solution.py:377
  73.8 12.5 %collective-permute-start.19 = (f32[512,128]{1,0:T(8,128)S(1)}, f32[512,128]{1,0:T(8,128)S(1)}, u32[]{:S(2)}, u32[]{:S(2)}) collective-permute-start(f32[512,128]{1,0:T(8,128)S(1)} %get-tuple-element.11), channel_id=1, source_target_pairs={{0,2},{1,65},{2,4},{3,67},{4,6},{5,69},{6,0},{7,71},{64,66},{65,12... | collective-permute-start | bytes 786440 | tf_op jit(solution)/shard_map/ppermute | solution.py:377
  73.8 12.5 %collective-permute-start.18 = (f32[512,128]{1,0:T(8,128)S(1)}, f32[512,128]{1,0:T(8,128)S(1)}, u32[]{:S(2)}, u32[]{:S(2)}) collective-permute-start(f32[512,128]{1,0:T(8,128)S(1)} %get-tuple-element.9), channel_id=1, source_target_pairs={{0,4},{1,129},{2,6},{3,131},{4,0},{5,133},{6,2},{7,135},{64,68},{6... | collective-permute-start | bytes 786440 | tf_op jit(solution)/shard_map/ppermute | solution.py:377
  76.8 12.3 %collective-permute-start.22 = (f32[2,3,1,64,128]{4,3,2,1,0:T(8,128)}, f32[2,3,1,64,128]{4,3,2,1,0:T(8,128)S(1)}, u32[]{:S(2)}, u32[]{:S(2)}) collective-permute-start(f32[2,3,1,64,128]{4,3,2,1,0:T(8,128)} %get-tuple-element.13), channel_id=1, source_target_pairs={{0,1},{1,2},{2,3},{3,4},{4,5},{5,6},{6,7},{7,8},{8,9},{9,10},{10,1... | collective-permute-start | bytes 589832 | tf_op jit(solution)/shard_map/ppermute | solution.py:338
  78.7 10.4 %collective-permute-start.23 = (f32[2,3,1,64,128]{4,3,2,1,0:T(8,128)S(1)}, f32[2,3,1,64,128]{4,3,2,1,0:T(8,128)S(1)}, u32[]{:S(2)}, u32[]{:S(2)}) collective-permute-start(f32[2,3,1,64,128]{4,3,2,1,0:T(8,128)S(1)} %get-tuple-element.12), channel_id=1, source_target_pairs={{1,0},{2,1},{3,2},{4,3},{5,4},{6,5},{7,6},{8,7},{9,8},{10,9},{11,1... | collective-permute-start | bytes 589832 | tf_op jit(solution)/shard_map/ppermute | solution.py:338
  86.5 7.3 %collective-permute-start.21 = (f32[64,128]{1,0:T(8,128)S(1)}, f32[64,128]{1,0:T(8,128)S(1)}, u32[]{:S(2)}, u32[]{:S(2)}) collective-permute-start(f32[64,128]{1,0:T(8,128)S(1)} %slice_exponential_fusion), channel_id=1, source_target_pairs={{0,1},{1,2},{2,3},{3,4},{4,5},{5,6},{6,7},{7,8},{8,9},{9,10},{10,1... | collective-permute-start | bytes 98312 | tf_op jit(solution)/shard_map/ppermute | solution.py:338
  89.1 1.4 %copy-start.1 = (f32[1,2,3,8,64,128]{5,4,3,2,1,0:T(8,128)S(1)}, f32[1,2,3,8,64,128]{5,4,3,2,1,0:T(8,128)}, u32[]{:S(2)}) copy-start(f32[1,2,3,8,64,128]{5,4,3,2,1,0:T(8,128)} %param.12) | copy-start | bytes 4718596
